TPU v7x, 256 devices: a whole 4x4x8 slice. The times are simulated.
256 devices in a mesh: cuts: 8 (over x_lo, y), dev: 32 (over x_hi, z, core).
Axes of the slice: x: 4 (x_hi: 2, x_lo: 2; x = x_hi * 2 + x_lo), y: 4, z: 8, core: 2. Of those that a mesh axis runs over, the one named last changes fastest.
Arguments:
- gate_pre: bfloat16 [32768, 1024], P(('cuts', 'dev')), may hold values from -24 to 24
- up_pre: bfloat16 [32768, 1024], P(('cuts', 'dev')), may hold values from -6 to 6
- out_grad: bfloat16 [32768, 3584], P(('cuts', 'dev')), may hold values from -0.25 to 0.25
- route_weight: float32 [32768], P(('cuts', 'dev')), may hold values from 0.1 to 1
- row_token: int32 [32768], P(('cuts', 'dev')), may hold values from 0 to 127
- master: float32 [1024, 3584], P(('cuts', 'dev')), may hold values from -0.0625 to 0.0625
- moment: float32 [1024, 3584], P(('cuts', 'dev')), may hold values from -6 to 6
- second: float32 [1024, 3584], P(('cuts', 'dev')), may hold values from 0.1 to 4
Outputs:
- new_weight: bfloat16 [1024, 3584], replicated
- new_master: float32 [1024, 3584], P(('cuts', 'dev'))
- new_moment: float32 [1024, 3584], P(('cuts', 'dev'))
- new_second: float32 [1024, 3584], P(('cuts', 'dev'))
Inputs may be any that keep to these rules, and one draw needn't show every extreme that they name: `row_token`: each entry names a row of out_grad in the same block of 128 rows as the entry itself.
All inputs are finite; a program needn't handle non-finite values.
Results may differ from a plain program's by a relative error of at most 0.01.
Values may be sent and summed in bfloat16 or wider, within the bound.
No kernel may reach another device: no remote copies, remote signals or barrier semaphores. Data moves between devices by JAX's collectives and lax.ppermute only.
A program may use at most 64 MiB of HBM per device.

v0:
```python
import jax
import jax.numpy as jnp
from jax import lax
from jax.sharding import PartitionSpec as P

STEP = 10


def shards(gate_pre, up_pre, out_grad, route_weight, row_token, master, moment, second):
    hidden = (jax.nn.silu(gate_pre.astype(jnp.float32)) * up_pre.astype(jnp.float32)).astype(
        jnp.bfloat16
    )
    picked = jnp.take(out_grad, row_token, axis=0)
    scaled = (picked.astype(jnp.float32) * route_weight[:, None]).astype(jnp.bfloat16)
    rows_here = hidden.shape[0]
    width_hidden = hidden.shape[1]
    count_cuts = lax.axis_size("cuts")
    count_dev = lax.axis_size("dev")
    share = width_hidden // (count_cuts * count_dev)
    slab = share * count_cuts
    arranged = hidden.reshape(rows_here, count_cuts, count_dev, share)
    taken = arranged
    taken = jnp.transpose(taken, (0, 2, 1, 3)).reshape(rows_here, lax.axis_size("dev") * slab)
    term = lax.dot_general(
        taken, scaled, (((0,), (0,)), ((), ())), preferred_element_type=jnp.float32
    )
    rounded = lax.optimization_barrier(term.astype(jnp.bfloat16))
    partial_sum = lax.psum_scatter(
        rounded.astype(jnp.float32).astype(jnp.bfloat16), "dev", scatter_dimension=0, tiled=True
    )
    grad = lax.psum_scatter(partial_sum, "cuts", scatter_dimension=0, tiled=True).astype(
        jnp.float32
    )
    new_moment = 0.9 * moment + 0.1 * grad
    new_second = 0.95 * second + 0.05 * grad * grad
    first_hat = new_moment / (1.0 - 0.9**STEP)
    second_hat = new_second / (1.0 - 0.95**STEP)
    new_master = master - 0.001 * (first_hat / (jnp.sqrt(second_hat) + 1e-08) + 0.1 * master)
    weight_piece = new_master.astype(jnp.bfloat16)
    new_weight = lax.all_gather(weight_piece, ("cuts", "dev"), axis=0, tiled=True)
    return (new_weight, new_master, new_moment, new_second)


def solution(mesh):
    in_specs = (
        P(("cuts", "dev"), None),
        P(("cuts", "dev"), None),
        P(("cuts", "dev"), None),
        P(("cuts", "dev")),
        P(("cuts", "dev")),
        P(("cuts", "dev"), None),
        P(("cuts", "dev"), None),
        P(("cuts", "dev"), None),
    )
    out_specs = (P(), P(("cuts", "dev"), None), P(("cuts", "dev"), None), P(("cuts", "dev"), None))
    return jax.shard_map(shards, mesh=mesh, in_specs=in_specs, out_specs=out_specs, check_vma=False)
```

profile of v0, /device:TPU:1, one launch (start us, length us, event | category | flops | bytes accessed | tf_op | source)
XLA Modules:
  0.0 680.9 jit_solution(3250617202675591963)
XLA Ops:
  7.2 0.0 copy-start
  7.2 0.0 copy-start.4
  7.2 0.0 reduce-scatter.2.cloned.1.call-start
  7.2 0.7 compare_and_fusion
  8.0 0.7 compare_select_fusion
  8.6 1.1 copy.15
  9.8 1.1 copy.16
  10.9 0.2 fusion.7
  11.1 0.1 copy.17
  11.2 0.0 copy-done
  11.2 1.1 gather_fusion
  12.3 0.0 copy-done.4
  12.3 0.0 copy-start.5
  12.3 0.0 copy-start.1
  12.3 0.0 copy-start.2
  12.4 0.0 copy-start.3
  12.4 5.2 convolution_convert_fusion
  17.6 0.0 reduce-scatter.2.cloned.1.call-update
  17.6 0.0 all-reduce.3.cloned.1.call-start
  17.7 141.1 %reduce-scatter.2.cloned.1.call-done = bf16[32,3584]{1,0:T(8,128)(2,1)} async-done(((bf16[1024,3584]{1,0:T(8,128)(2,1)}), bf16[32,3584]{1,0:T(8,128)(2,1)}) %reduce-scatter.2.cloned.1.call-update) | async-done | bytes 229392 | tf_op jit(solution)/shard_map/reduce_scatter | solution.py:28
  158.7 0.0 all-reduce.3.cloned.1.call-update
  158.8 0.0 all-gather.3.cloned.1.call-start
  158.8 0.0 copy-done.5
  158.8 0.6 dynamic-slice
  160.1 75.6 %all-reduce.3.cloned.1.call-done = bf16[32,3584]{1,0:T(8,128)(2,1)} async-done(((bf16[32,3584]{1,0:T(8,128)(2,1)}), bf16[32,3584]{1,0:T(8,128)(2,1)}) %all-reduce.3.cloned.1.call-update) | async-done | bytes 229392
  235.7 0.0 copy-done.1
  235.7 0.0 copy-done.2
  235.7 0.0 copy-done.3
  235.7 1.6 convert_bitcast_fusion
  237.3 0.0 all-gather.3.cloned.1.call-update
  237.3 425.0 %all-gather.3.cloned.1.call-done = bf16[256,4,3584]{2,1,0:T(4,128)(2,1)} async-done(((bf16[1,4,3584]{2,1,0:T(4,128)(2,1)}), bf16[256,4,3584]{2,1,0:T(4,128)(2,1)}) %all-gather.3.cloned.1.call-update) | async-done | bytes 7340048 | tf_op jit(solution)/shard_map/all_gather | solution.py:40
  662.3 12.1 %reshape.32 = bf16[1024,3584]{1,0:T(8,128)(2,1)} reshape(bf16[256,4,3584]{2,1,0:T(4,128)(2,1)} %all-gather.3.cloned.1.call-done) | data formatting | bytes 14680064
  (1 shorter events, 0.0 us)
Async XLA Ops:
  7.2 4.0 copy-start
  7.2 5.1 copy-start.4
  7.2 151.6 %reduce-scatter.2.cloned.1.call-start = ((), (), s32[]{:S(2)}) async-start(), calls=%async_computation.1 | async-start | bytes 7569408 | tf_op jit(solution)/shard_map/reduce_scatter | solution.py:28
  12.3 146.5 %copy-start.5 = (u32[256]{0:T(256)S(1)}, u32[256]{0:T(256)}, u32[]{:S(2)}) copy-start(u32[256]{0:T(256)} %constant.47) | copy-start | bytes 3076
  12.3 223.4 %copy-start.1 = (f32[4,3584]{1,0:T(4,128)S(1)}, f32[4,3584]{1,0:T(4,128)}, u32[]{:S(2)}) copy-start(f32[4,3584]{1,0:T(4,128)} %param.13) | copy-start | bytes 172036
  12.3 223.3 %copy-start.2 = (f32[4,3584]{1,0:T(4,128)S(1)}, f32[4,3584]{1,0:T(4,128)}, u32[]{:S(2)}) copy-start(f32[4,3584]{1,0:T(4,128)} %param.14) | copy-start | bytes 172036
  12.4 223.3 %copy-start.3 = (f32[4,3584]{1,0:T(4,128)S(1)}, f32[4,3584]{1,0:T(4,128)}, u32[]{:S(2)}) copy-start(f32[4,3584]{1,0:T(4,128)} %param.15) | copy-start | bytes 172036
  17.6 218.1 %all-reduce.3.cloned.1.call-start = ((), (), s32[]{:S(2)}) async-start(), calls=%async_computation.3 | async-start | bytes 458752
  158.8 503.5 %all-gather.3.cloned.1.call-start = ((), (), s32[]{:S(2)}) async-start(), calls=%async_computation.2 | async-start | bytes 7368704 | tf_op jit(solution)/shard_map/all_gather | solution.py:40
Sparse Core Ops, SparseCore 0:
  17.7 140.9 reduce-scatter.1
  161.6 74.0 all-reduce.2
  238.2 424.0 all-gather.2
where the time goes:
time: 682 us; the launch traced here: 681 us
  waiting for transfers between devices  642 us (94%)
  local copies, waits for them, and re-layouts  16.2 us (2%)
  between operations  14.5 us (2%)
    all_gather x1, waiting for transfers between devices, shards(): lax.all_gather(weight_piece, ('cuts', 'dev'), axis=0, tiled=True)  425 us
    reduce_scatter x1, waiting for transfers between devices, shards(): lax.psum_scatter(rounded.astype(jnp.float32).astype(jnp.bfloat16), 'dev',...  141 us
    unnamed x4, waiting for transfers between devices  75.7 us
    unnamed x16, local copies, waits for them, and re-layouts  15 us
  transfers between devices with their start and end apart: 3, of which 3 were waited for; matrix products, arithmetic and copies ran while one was open for 0% of the time, Pallas kernels for 0%

commit v1 on v0

v1 whole, which is shorter than its diff:
```python
import jax
import jax.numpy as jnp
from jax import lax
from jax.sharding import Mesh, PartitionSpec as P

STEP = 10

SIZES = (2, 4, 2, 8, 2)
NAMES = ("xlo", "y", "xhi", "z", "core")
PLANE = ("xlo", "y", "xhi")
N_PLANE = 16
N_Z = 8
SWAP = [(0, 1), (1, 0)]


def gather_tokens(out_grad, row_token):
    return jnp.take(out_grad, row_token, axis=0, mode="clip")


def shards(gate_pre, up_pre, out_grad, route_weight, row_token, master, moment, second):
    first_core = lax.axis_index("core") == 0
    width = out_grad.shape[1]
    half = width // 2

    def mine_and_theirs(whole):
        left, right = whole[..., :half], whole[..., half:]
        return jnp.where(first_core, left, right), jnp.where(first_core, right, left)

    def in_core_order(own, peer, axis):
        return jnp.where(
            first_core,
            jnp.concatenate([own, peer], axis),
            jnp.concatenate([peer, own], axis),
        )

    state = jnp.stack([master, moment, second])
    state_mine, state_theirs = mine_and_theirs(state)
    state_peer = lax.ppermute(state_theirs, "core", SWAP)
    state_chip = in_core_order(state_mine, state_peer, 1)

    hidden = (jax.nn.silu(gate_pre.astype(jnp.float32)) * up_pre.astype(jnp.float32)).astype(
        jnp.bfloat16
    )
    hidden_peer = lax.ppermute(hidden, "core", SWAP)
    picked = gather_tokens(out_grad, row_token)
    scaled = (picked.astype(jnp.float32) * route_weight[:, None]).astype(jnp.bfloat16)
    scaled_mine, scaled_theirs = mine_and_theirs(scaled)
    scaled_peer = lax.ppermute(scaled_theirs, "core", SWAP)

    term = lax.dot_general(
        jnp.concatenate([hidden, hidden_peer], 0),
        jnp.concatenate([scaled_mine, scaled_peer], 0),
        (((0,), (0,)), ((), ())),
        preferred_element_type=jnp.float32,
    ).astype(jnp.bfloat16)
    rows = term.shape[0]
    blocks = lax.all_to_all(term.reshape(N_PLANE, rows // N_PLANE, half), PLANE, 0, 0)
    plane_sum = jnp.sum(blocks.astype(jnp.float32), 0).astype(jnp.bfloat16)
    rows = plane_sum.shape[0]
    blocks = lax.all_to_all(plane_sum.reshape(N_Z, rows // N_Z, half), "z", 0, 0)
    grad = jnp.sum(blocks.astype(jnp.float32), 0)

    new_moment = 0.9 * state_chip[1] + 0.1 * grad
    new_second = 0.95 * state_chip[2] + 0.05 * grad * grad
    first_hat = new_moment / (1.0 - 0.9**STEP)
    second_hat = new_second / (1.0 - 0.95**STEP)
    new_master = state_chip[0] - 0.001 * (
        first_hat / (jnp.sqrt(second_hat) + 1e-08) + 0.1 * state_chip[0]
    )
    piece = new_master.astype(jnp.bfloat16)

    new_state = jnp.stack([new_master, new_moment, new_second])
    top, bottom = new_state[:, : master.shape[0]], new_state[:, master.shape[0] :]
    state_own = jnp.where(first_core, top, bottom)
    state_back = lax.ppermute(jnp.where(first_core, bottom, top), "core", SWAP)
    state_out = in_core_order(state_own, state_back, 2)

    along_z = lax.all_to_all(jnp.broadcast_to(piece, (N_Z,) + piece.shape), "z", 0, 0)
    along_z = along_z.reshape(-1, half)
    plane = lax.all_to_all(jnp.broadcast_to(along_z, (N_PLANE,) + along_z.shape), PLANE, 0, 0)
    plane = plane.reshape(-1, half)
    plane_peer = lax.ppermute(plane, "core", SWAP)
    new_weight = in_core_order(plane, plane_peer, 1)
    return (new_weight, state_out[0], state_out[1], state_out[2])


def solution(mesh):
    grid = Mesh(mesh.devices.reshape(SIZES), NAMES)
    rows = P(NAMES, None)
    in_specs = (rows, rows, rows, P(NAMES), P(NAMES), rows, rows, rows)
    out_specs = (P(), rows, rows, rows)
    return jax.shard_map(shards, mesh=grid, in_specs=in_specs, out_specs=out_specs, check_vma=False)
```

time: 682 us -> 172 us (0.25)
  waiting for transfers between devices: 642 us -> 72.9 us
  blocking collectives: 0 us -> 59.4 us
  starting transfers between devices: 0.12 us -> 24.5 us
  between operations: 14.5 us -> 0.83 us
  local copies, waits for them, and re-layouts: 16.2 us -> 2.58 us
    all_gather x1 -> x0, waiting for transfers between devices: 425 us -> none  [shards(): lax.all_gather(weight_piece, ('cuts', 'dev'), axis=0, tiled=True)]
    reduce_scatter x1 -> x0, waiting for transfers between devices: 141 us -> none  [shards(): lax.psum_scatter(rounded.astype(jnp.float32).astype(jnp.bfloat16), 'dev',...]
    unnamed x4 -> x0, waiting for transfers between devices: 75.7 us -> none
    all_to_all x0 -> x2, waiting for transfers between devices: none -> 64.5 us  [the longest x1 58.6 us: shards(): lax.all_to_all(term.reshape(N_PLANE, rows // N_PLANE, half), PLANE, 0, 0)]
    all_to_all x0 -> x2, blocking collectives: none -> 59.4 us  [the longest x1 47.8 us: shards(): lax.all_to_all(jnp.broadcast_to(along_z, (N_PLANE,) + along_z.shape), PLA...]
    unnamed x16 -> x14, local copies, waits for them, and re-layouts: 15 us -> 0.43 us
    all_to_all x0 -> x2, starting transfers between devices: none -> 13.2 us  [the longest x1 8.19 us: shards(): lax.all_to_all(plane_sum.reshape(N_Z, rows // N_Z, half), 'z', 0, 0)]
    ppermute x0 -> x5, starting transfers between devices: none -> 11.3 us  [the longest x1 5.85 us: shards(): plane_peer = lax.ppermute(plane, 'core', SWAP)]
  transfers between devices with their start and end apart: 3 -> 7, of which waited for: 3 -> 5; matrix products, arithmetic and copies ran while one was open for 0% -> 1% of each run, Pallas kernels for 0% -> 0%
where the time goes in v1:
time: 172 us
  waiting for transfers between devices  72.9 us (42%)
  blocking collectives  59.4 us (35%)
  starting transfers between devices  24.5 us (14%)
  other arithmetic  8.79 us (5%)
  matrix products  3.01 us (2%)
  local copies, waits for them, and re-layouts  2.58 us (2%)
    all_to_all x1, waiting for transfers between devices, shards(): lax.all_to_all(term.reshape(N_PLANE, rows // N_PLANE, half), PLANE, 0, 0)  58.6 us
    all_to_all x1, blocking collectives, shards(): lax.all_to_all(jnp.broadcast_to(along_z, (N_PLANE,) + along_z.shape), PLA...  47.8 us
    all_to_all x1, blocking collectives, shards(): lax.all_to_all(jnp.broadcast_to(piece, (N_Z,) + piece.shape), 'z', 0, 0)  11.5 us
    all_to_all x1, starting transfers between devices, shards(): lax.all_to_all(plane_sum.reshape(N_Z, rows // N_Z, half), 'z', 0, 0)  8.19 us
    all_to_all x1, waiting for transfers between devices, shards(): lax.all_to_all(plane_sum.reshape(N_Z, rows // N_Z, half), 'z', 0, 0)  5.98 us
    ppermute x1, waiting for transfers between devices, shards(): state_back = lax.ppermute(jnp.where(first_core, bottom, top), 'core', SWAP)  5.94 us
    ppermute x1, starting transfers between devices, shards(): plane_peer = lax.ppermute(plane, 'core', SWAP)  5.85 us
    all_to_all x1, starting transfers between devices, shards(): lax.all_to_all(term.reshape(N_PLANE, rows // N_PLANE, half), PLANE, 0, 0)  5.06 us
  transfers between devices with their start and end apart: 7, of which 5 were waited for; matrix products, arithmetic and copies ran while one was open for 1% of the time, Pallas kernels for 0%

profile of v1, /device:TPU:1, one launch (start us, length us, event | category | flops | bytes accessed | tf_op | source)
XLA Modules:
  0.0 172.0 jit_solution(4252175101309787169)
XLA Ops:
  0.6 0.0 copy-start
  0.7 0.8 pad_clamp_fusion
  1.4 0.4 copy-done
  1.8 1.1 gather_fusion
  3.0 0.2 multiply_convert_fusion
  3.2 0.1 broadcast_select_fusion.1
  3.3 3.3 %collective-permute-start.2 = (bf16[128,1792]{1,0:T(8,128)(2,1)S(1)}, bf16[128,1792]{1,0:T(8,128)(2,1)S(1)}, u32[]{:S(2)}, u32[]{:S(2)}) collective-permute-start(bf16[128,1792]{1,0:T(8,128)(2,1)S(1)} %get-tuple-element.8), channel_id=1, source_target_pairs={{0,1},{1,0},{2,3},{3,2},{4,5},{5,4},{6,7},{7,6},{8,9},{9,8},{10,11... | collective-permute-start | bytes 1376264 | tf_op jit(solution)/shard_map/ppermute | solution.py:48
  6.6 0.2 fusion.10
  6.8 0.0 copy-start.3
  6.8 0.0 copy-start.4
  6.8 0.0 copy-start.5
  6.8 0.1 collective-permute-start.1
  6.9 1.5 collective-permute-done.1
  8.4 3.0 %convolution_convert_fusion = bf16[1024,1792]{1,0:T(8,128)(2,1)} fusion(bf16[128,1792]{1,0:T(8,128)(2,1)S(1)} %collective-permute-done.2, bf16[128,1792]{1,0:T(8,128)(2,1)S(1)} %get-tuple-element.7, bf16[128,1024]{1,0:T(8,128)(2,1)S(1)} %collective-permute-done.1, bf16[128,1024]{1,0:T(8,128)(2,1)S(1)} %fusion.10), kind=kOutput, calls=%fused_computation.2 | convolution fusion | flops 944242688 | bytes 5111808 | tf_op jit(solution)/shard_map/dot_general | solution.py:50
  11.4 5.1 %all-to-all-start = ((bf16[16,64,1792]{2,1,0:T(8,128)(2,1)}), bf16[16,64,1792]{2,1,0:T(8,128)(2,1)}, u32[]{:S(2)}, u32[]{:S(2)}) async-start(bf16[16,64,1792]{2,1,0:T(8,128)(2,1)} %bitcast.41), calls=%async_computation | async-start | bytes 7340032 | tf_op jit(solution)/shard_map/all_to_all | solution.py:57
  16.6 58.6 %all-to-all-done = bf16[16,64,1792]{2,1,0:T(8,128)(2,1)} async-done(((bf16[16,64,1792]{2,1,0:T(8,128)(2,1)}), bf16[16,64,1792]{2,1,0:T(8,128)(2,1)}, u32[]{:S(2)}, u32[]{:S(2)}) %all-to-all-start) | async-done | bytes 3670048 | tf_op jit(solution)/shard_map/all_to_all | solution.py:57
  75.2 3.3 %reduce_sum.23 = bf16[64,1792]{1,0:T(8,128)(2,1)} reduce(bf16[16,64,1792]{2,1,0:T(8,128)(2,1)} %all-to-all-done, bf16[]{:T(256)} %constant.9.clone.1), dimensions={0}, to_apply=%region_0.1 | reduce | flops 1720320 | bytes 3899394 | tf_op jit(solution)/shard_map/reduce_sum | solution.py:58
  78.5 8.2 %all-to-all-start.1 = ((bf16[8,8,1792]{2,1,0:T(8,128)(2,1)}), bf16[8,8,1792]{2,1,0:T(8,128)(2,1)S(1)}, u32[]{:S(2)}, u32[]{:S(2)}) async-start(bf16[8,8,1792]{2,1,0:T(8,128)(2,1)} %bitcast.6), calls=%async_computation.1 | async-start | bytes 458752 | tf_op jit(solution)/shard_map/all_to_all | solution.py:60
  86.7 1.9 %collective-permute-start = (f32[3,4,1792]{2,1,0:T(4,128)S(1)}, f32[3,4,1792]{2,1,0:T(4,128)S(1)}, u32[]{:S(2)}, u32[]{:S(2)}) collective-permute-start(f32[3,4,1792]{2,1,0:T(4,128)S(1)} %get-tuple-element.15), channel_id=1, source_target_pairs={{0,1},{1,0},{2,3},{3,2},{4,5},{5,4},{6,7},{7,6},{8,9},{9,8},{10,11... | collective-permute-start | bytes 258056 | tf_op jit(solution)/shard_map/ppermute | solution.py:38
  88.5 0.9 collective-permute-done
  89.5 0.1 maximum_select_fusion.1
  89.5 6.0 %all-to-all-done.1 = bf16[8,8,1792]{2,1,0:T(8,128)(2,1)S(1)} async-done(((bf16[8,8,1792]{2,1,0:T(8,128)(2,1)}), bf16[8,8,1792]{2,1,0:T(8,128)(2,1)S(1)}, u32[]{:S(2)}, u32[]{:S(2)}) %all-to-all-start.1) | async-done | bytes 229408 | tf_op jit(solution)/shard_map/all_to_all | solution.py:60
  95.6 0.1 fusion.20
  95.7 11.5 %all_to_all.20 = bf16[8,8,1792]{2,1,0:T(8,128)(2,1)S(1)} all-to-all(bf16[8,8,1792]{2,1,0:T(8,128)(2,1)S(1)} %broadcast_in_dim.12), channel_id=1, replica_groups=mesh['xlo'=2,'y'=4,'xhi'=2,'z'=8,'core'=2] {'z'}, dimensions={0} | all-to-all | bytes 458752 | tf_op jit(solution)/shard_map/all_to_all | solution.py:78
  107.2 0.4 broadcast_in_dim.13
  107.6 47.8 %all_to_all.21 = bf16[16,64,1792]{2,1,0:T(8,128)(2,1)S(1)} all-to-all(bf16[16,64,1792]{2,1,0:T(8,128)(2,1)S(1)} %broadcast_in_dim.13), channel_id=1, replica_groups=mesh['xlo'=2,'y'=4,'xhi'=2,'z'=8,'core'=2] {'xlo','y','xhi'}, dimensions={0} | all-to-all | bytes 7340032 | tf_op jit(solution)/shard_map/all_to_all | solution.py:80
  155.4 5.9 %collective-permute-start.3 = (bf16[1024,1792]{1,0:T(8,128)(2,1)S(1)}, bf16[1024,1792]{1,0:T(8,128)(2,1)S(1)}, u32[]{:S(2)}, u32[]{:S(2)}) collective-permute-start(bf16[1024,1792]{1,0:T(8,128)(2,1)S(1)} %bitcast.42), channel_id=1, source_target_pairs={{0,1},{1,0},{2,3},{3,2},{4,5},{5,4},{6,7},{7,6},{8,9},{9,8},{10,11... | collective-permute-start | bytes 11010056 | tf_op jit(solution)/shard_map/ppermute | solution.py:82
  161.2 0.1 multiply_subtract_fusion
  161.3 0.1 collective-permute-start.4
  161.4 5.9 %collective-permute-done.4 = f32[3,4,1792]{2,1,0:T(4,128)S(1)} collective-permute-done((f32[3,4,1792]{2,1,0:T(4,128)S(1)}, f32[3,4,1792]{2,1,0:T(4,128)S(1)}, u32[]{:S(2)}, u32[]{:S(2)}) %collective-permute-start.4) | collective-permute-done | bytes 86048 | tf_op jit(solution)/shard_map/ppermute | solution.py:75
  167.4 0.7 slice_bitcast_fusion
  168.1 3.9 %maximum_select_fusion = bf16[1024,3584]{1,0:T(8,128)(2,1)} fusion(bf16[1024,1792]{1,0:T(8,128)(2,1)S(1)} %collective-permute-done.3, bf16[1024,1792]{1,0:T(8,128)(2,1)S(1)} %bitcast.43, pred[]{:T(512)S(6)} %eq.3), kind=kLoop, calls=%fused_computation.1 | loop fusion | flops 33030144 | bytes 14680065 | tf_op jit(solution)/shard_map/jit(_where)/select_n | solution.py:30
  (18 shorter events, 0.2 us)
Async XLA Ops:
  0.6 1.2 copy-start
  0.6 2.3 %copy-start.6 = (f32[128]{0:T(128)S(1)}, f32[128]{0:T(128)}, u32[]{:S(2)}) copy-start(f32[128]{0:T(128)} %param.11) | copy-start | bytes 1540
  0.7 5.9 %copy-start.1 = (bf16[128,1024]{1,0:T(8,128)(2,1)S(1)}, bf16[128,1024]{1,0:T(8,128)(2,1)}, u32[]{:S(2)}) copy-start(bf16[128,1024]{1,0:T(8,128)(2,1)} %param.9) | copy-start | bytes 786436
  0.7 5.9 %copy-start.2 = (bf16[128,1024]{1,0:T(8,128)(2,1)S(1)}, bf16[128,1024]{1,0:T(8,128)(2,1)}, u32[]{:S(2)}) copy-start(bf16[128,1024]{1,0:T(8,128)(2,1)} %param.8) | copy-start | bytes 786436
  3.3 5.2 %collective-permute-start.2 = (bf16[128,1792]{1,0:T(8,128)(2,1)S(1)}, bf16[128,1792]{1,0:T(8,128)(2,1)S(1)}, u32[]{:S(2)}, u32[]{:S(2)}) collective-permute-start(bf16[128,1792]{1,0:T(8,128)(2,1)S(1)} %get-tuple-element.8), channel_id=1, source_target_pairs={{0,1},{1,0},{2,3},{3,2},{4,5},{5,4},{6,7},{7,6},{8,9},{9,8},{10,11... | collective-permute-start | bytes 1376264 | tf_op jit(solution)/shard_map/ppermute | solution.py:48
  6.8 9.7 %copy-start.3 = (f32[4,3584]{1,0:T(4,128)S(1)}, f32[4,3584]{1,0:T(4,128)}, u32[]{:S(2)}) copy-start(f32[4,3584]{1,0:T(4,128)} %param.15) | copy-start | bytes 172036
  6.8 9.7 %copy-start.4 = (f32[4,3584]{1,0:T(4,128)S(1)}, f32[4,3584]{1,0:T(4,128)}, u32[]{:S(2)}) copy-start(f32[4,3584]{1,0:T(4,128)} %param.14) | copy-start | bytes 172036
  6.8 9.7 %copy-start.5 = (f32[4,3584]{1,0:T(4,128)S(1)}, f32[4,3584]{1,0:T(4,128)}, u32[]{:S(2)}) copy-start(f32[4,3584]{1,0:T(4,128)} %param.13) | copy-start | bytes 172036
  6.8 1.6 collective-permute-start.1
  11.4 63.7 %all-to-all-start = ((bf16[16,64,1792]{2,1,0:T(8,128)(2,1)}), bf16[16,64,1792]{2,1,0:T(8,128)(2,1)}, u32[]{:S(2)}, u32[]{:S(2)}) async-start(bf16[16,64,1792]{2,1,0:T(8,128)(2,1)} %bitcast.41), calls=%async_computation | async-start | bytes 7340032 | tf_op jit(solution)/shard_map/all_to_all | solution.py:57
  78.5 17.1 %all-to-all-start.1 = ((bf16[8,8,1792]{2,1,0:T(8,128)(2,1)}), bf16[8,8,1792]{2,1,0:T(8,128)(2,1)S(1)}, u32[]{:S(2)}, u32[]{:S(2)}) async-start(bf16[8,8,1792]{2,1,0:T(8,128)(2,1)} %bitcast.6), calls=%async_computation.1 | async-start | bytes 458752 | tf_op jit(solution)/shard_map/all_to_all | solution.py:60
  86.7 2.8 %collective-permute-start = (f32[3,4,1792]{2,1,0:T(4,128)S(1)}, f32[3,4,1792]{2,1,0:T(4,128)S(1)}, u32[]{:S(2)}, u32[]{:S(2)}) collective-permute-start(f32[3,4,1792]{2,1,0:T(4,128)S(1)} %get-tuple-element.15), channel_id=1, source_target_pairs={{0,1},{1,0},{2,3},{3,2},{4,5},{5,4},{6,7},{7,6},{8,9},{9,8},{10,11... | collective-permute-start | bytes 258056 | tf_op jit(solution)/shard_map/ppermute | solution.py:38
  155.4 12.7 %collective-permute-start.3 = (bf16[1024,1792]{1,0:T(8,128)(2,1)S(1)}, bf16[1024,1792]{1,0:T(8,128)(2,1)S(1)}, u32[]{:S(2)}, u32[]{:S(2)}) collective-permute-start(bf16[1024,1792]{1,0:T(8,128)(2,1)S(1)} %bitcast.42), channel_id=1, source_target_pairs={{0,1},{1,0},{2,3},{3,2},{4,5},{5,4},{6,7},{7,6},{8,9},{9,8},{10,11... | collective-permute-start | bytes 11010056 | tf_op jit(solution)/shard_map/ppermute | solution.py:82
  161.3 6.0 %collective-permute-start.4 = (f32[3,4,1792]{2,1,0:T(4,128)S(1)}, f32[3,4,1792]{2,1,0:T(4,128)S(1)}, u32[]{:S(2)}, u32[]{:S(2)}) collective-permute-start(f32[3,4,1792]{2,1,0:T(4,128)S(1)} %get-tuple-element.13), channel_id=1, source_target_pairs={{0,1},{1,0},{2,3},{3,2},{4,5},{5,4},{6,7},{7,6},{8,9},{9,8},{10,11... | collective-permute-start | bytes 258056 | tf_op jit(solution)/shard_map/ppermute | solution.py:75

commit v2 on v1

v2 whole, which is shorter than its diff:
```python
import functools

import jax
import jax.numpy as jnp
from jax import lax
from jax.experimental import pallas as pl
from jax.experimental.pallas import tpu as pltpu
from jax.sharding import Mesh, PartitionSpec as P

STEP = 10

SIZES = (2, 4, 2, 8, 2)
NAMES = ("xlo", "y", "xhi", "z", "core")
N_X = N_Y = 4
N_Z = 8
BLOCK = 64
SWAP = [(0, 1), (1, 0)]
VMEM = 40 * 1024 * 1024


def along_x(value, shift):
    place = [(x % 2) * 2 + x // 2 for x in range(N_X)]
    pairs = [(place[x], place[(x + shift) % N_X]) for x in range(N_X)]
    return lax.ppermute(value, ("xlo", "xhi"), pairs)


def along_y(value, shift):
    return lax.ppermute(value, "y", [(y, (y + shift) % N_Y) for y in range(N_Y)])


def block_of(x, y):
    return (x % 2) * 8 + y * 2 + x // 2


def position():
    return 2 * lax.axis_index("xhi") + lax.axis_index("xlo"), lax.axis_index("y")


def terms_kernel(here, hidden, hidden_peer, scaled, scaled_peer, *refs):
    outs, turned = refs[:-1], refs[-1]
    tokens = hidden.shape[0]
    turned[:, :tokens] = hidden[...].T
    turned[:, tokens:] = hidden_peer[...].T
    both = jnp.concatenate([scaled[...], scaled_peer[...]], 0)
    width = both.shape[1] // 2
    x, y = here[0], here[1]

    def rows(dx, dy):
        start = block_of((x + dx) % N_X, (y + dy) % N_Y) * BLOCK
        return turned[pl.ds(pl.multiple_of(start, BLOCK), BLOCK), :]

    for side in range(2):
        columns = both[:, side * width : (side + 1) * width]
        for far in range(4):
            for near in range(4):
                lhs = rows(near, far) if side == 0 else rows(far, near)
                outs[4 * side + far][near * BLOCK : (near + 1) * BLOCK, :] = jnp.dot(
                    lhs, columns, preferred_element_type=jnp.float32
                ).astype(jnp.bfloat16)


def terms(here, hidden, hidden_peer, scaled, scaled_peer):
    width = scaled.shape[1] // 2
    tokens = hidden.shape[0]
    whole = pl.BlockSpec(memory_space=pltpu.VMEM)
    return pl.pallas_call(
        terms_kernel,
        out_shape=[jax.ShapeDtypeStruct((4 * BLOCK, width), jnp.bfloat16)] * 8,
        in_specs=[pl.BlockSpec(memory_space=pltpu.SMEM)] + [whole] * 4,
        out_specs=[whole] * 8,
        scratch_shapes=[pltpu.VMEM((hidden.shape[1], 2 * tokens), jnp.bfloat16)],
        compiler_params=pltpu.CompilerParams(vmem_limit_bytes=VMEM),
        cost_estimate=pl.CostEstimate(
            flops=2 * 2 * tokens * hidden.shape[1] * 2 * width,
            bytes_accessed=5_000_000,
            transcendentals=0,
        ),
    )(here, hidden, hidden_peer, scaled, scaled_peer)


def join_kernel(here, *refs):
    pieces, out, sems = refs[:16], refs[16], refs[17]
    width = pieces[0].shape[1]
    x, y, core = here[0], here[1], here[2]
    copies = []
    for owner in range(2):
        column = (core if owner == 0 else 1 - core) * (2 * width)
        for side in range(2):
            for far in range(4):
                piece = pieces[8 * owner + 4 * side + far]
                for near in range(4):
                    dx, dy = (near, far) if side == 0 else (far, near)
                    row = block_of((x + N_X - dx) % N_X, (y + N_Y - dy) % N_Y) * BLOCK
                    copy = pltpu.make_async_copy(
                        piece.at[pl.ds(near * BLOCK, BLOCK), :],
                        out.at[
                            pl.ds(pl.multiple_of(row, BLOCK), BLOCK),
                            pl.ds(pl.multiple_of(column + side * width, 128), width),
                        ],
                        sems.at[len(copies)],
                    )
                    copy.start()
                    copies.append(copy)
    for copy in copies:
        copy.wait()


def join(here, pieces):
    rows, width = pieces[0].shape
    size = rows * width * 16
    return pl.pallas_call(
        join_kernel,
        out_shape=jax.ShapeDtypeStruct((4 * rows, 4 * width), jnp.bfloat16),
        in_specs=[pl.BlockSpec(memory_space=pltpu.SMEM)] + [pl.BlockSpec(memory_space=pl.ANY)] * 16,
        out_specs=pl.BlockSpec(memory_space=pl.ANY),
        scratch_shapes=[pltpu.SemaphoreType.DMA((64,))],
        compiler_params=pltpu.CompilerParams(vmem_limit_bytes=VMEM),
        cost_estimate=pl.CostEstimate(flops=0, bytes_accessed=4 * size, transcendentals=0),
    )(here, *pieces)


def total(parts):
    return functools.reduce(lambda a, b: a + b, [part.astype(jnp.float32) for part in parts])


def shards(gate_pre, up_pre, out_grad, route_weight, row_token, master, moment, second):
    first_core = lax.axis_index("core") == 0
    here = jnp.stack([*position(), lax.axis_index("core")]).astype(jnp.int32)
    half = out_grad.shape[1] // 2
    quarter = half // 2

    def mine_and_theirs(whole):
        left, right = whole[..., :half], whole[..., half:]
        return jnp.where(first_core, left, right), jnp.where(first_core, right, left)

    def in_core_order(own, peer, axis):
        return jnp.where(
            first_core,
            jnp.concatenate([own, peer], axis),
            jnp.concatenate([peer, own], axis),
        )

    state = jnp.stack([master, moment, second])
    state_mine, state_theirs = mine_and_theirs(state)
    state_peer = lax.ppermute(state_theirs, "core", SWAP)
    state_chip = in_core_order(state_mine, state_peer, 1)

    hidden = (jax.nn.silu(gate_pre.astype(jnp.float32)) * up_pre.astype(jnp.float32)).astype(
        jnp.bfloat16
    )
    hidden_peer = lax.ppermute(hidden, "core", SWAP)
    picked = jnp.take(out_grad, row_token, axis=0, mode="clip")
    scaled = (picked.astype(jnp.float32) * route_weight[:, None]).astype(jnp.bfloat16)
    scaled_mine, scaled_theirs = mine_and_theirs(scaled)
    scaled_peer = lax.ppermute(scaled_theirs, "core", SWAP)

    blocks = terms(here, hidden, hidden_peer, scaled_mine, scaled_peer)
    first = [along_y(blocks[s], s) for s in (1, 2, 3)]
    other = [along_x(blocks[4 + s], s) for s in (1, 2, 3)]
    first, other = [blocks[0]] + first, [blocks[4]] + other

    def near(parts, s):
        return total([part[s * BLOCK : (s + 1) * BLOCK] for part in parts])

    first = [near(first, 0)] + [along_x(near(first, s).astype(jnp.bfloat16), s) for s in (1, 2, 3)]
    other = [near(other, 0)] + [along_y(near(other, s).astype(jnp.bfloat16), s) for s in (1, 2, 3)]
    plane_sum = jnp.concatenate([total(first), total(other)], 1).astype(jnp.bfloat16)
    parts = lax.all_to_all(plane_sum.reshape(N_Z, BLOCK // N_Z, half), "z", 0, 0)
    grad = jnp.sum(parts.astype(jnp.float32), 0)

    new_moment = 0.9 * state_chip[1] + 0.1 * grad
    new_second = 0.95 * state_chip[2] + 0.05 * grad * grad
    first_hat = new_moment / (1.0 - 0.9**STEP)
    second_hat = new_second / (1.0 - 0.95**STEP)
    new_master = state_chip[0] - 0.001 * (
        first_hat / (jnp.sqrt(second_hat) + 1e-08) + 0.1 * state_chip[0]
    )
    piece = new_master.astype(jnp.bfloat16)

    new_state = jnp.stack([new_master, new_moment, new_second])
    top, bottom = new_state[:, : master.shape[0]], new_state[:, master.shape[0] :]
    state_own = jnp.where(first_core, top, bottom)
    state_back = lax.ppermute(jnp.where(first_core, bottom, top), "core", SWAP)
    state_out = in_core_order(state_own, state_back, 2)

    column = lax.all_to_all(jnp.broadcast_to(piece, (N_Z,) + piece.shape), "z", 0, 0)
    column = column.reshape(BLOCK, half)
    first, other = column[:, :quarter], column[:, quarter:]
    first = jnp.concatenate([first] + [along_x(first, s) for s in (1, 2, 3)], 0)
    other = jnp.concatenate([other] + [along_y(other, s) for s in (1, 2, 3)], 0)
    pieces = [first] + [along_y(first, s) for s in (1, 2, 3)]
    pieces += [other] + [along_x(other, s) for s in (1, 2, 3)]
    pieces += [lax.ppermute(piece, "core", SWAP) for piece in pieces]
    return (join(here, pieces), state_out[0], state_out[1], state_out[2])


def solution(mesh):
    grid = Mesh(mesh.devices.reshape(SIZES), NAMES)
    rows = P(NAMES, None)
    in_specs = (rows, rows, rows, P(NAMES), P(NAMES), rows, rows, rows)
    out_specs = (P(), rows, rows, rows)
    return jax.shard_map(shards, mesh=grid, in_specs=in_specs, out_specs=out_specs, check_vma=False)
```

time: 172 us -> 150 us (0.87)
  the two profiles are of different devices: /device:TPU:1 before, /device:TPU:25 now
where the time goes in v2:
time: 150 us; the launch traced here: 149 us
  waiting for transfers between devices  72.1 us (48%)
  starting transfers between devices  63.2 us (42%)
  Pallas kernels  7.05 us (5%)
  other arithmetic  3 us (2%)
  local copies, waits for them, and re-layouts  2.98 us (2%)
    ppermute x12, waiting for transfers between devices, along_y(): lax.ppermute(value, 'y', [(y, (y + shift) % N_Y) for y in range(N_Y)])  35.1 us
    ppermute x12, waiting for transfers between devices, along_x(): return lax.ppermute(value, ('xlo', 'xhi'), pairs)  22.5 us
    ppermute x12, starting transfers between devices, along_x(): return lax.ppermute(value, ('xlo', 'xhi'), pairs)  15.4 us
    ppermute x8, starting transfers between devices, shards(): pieces += [lax.ppermute(piece, 'core', SWAP) for piece in pieces]  13.9 us
    ppermute x12, starting transfers between devices, along_y(): lax.ppermute(value, 'y', [(y, (y + shift) % N_Y) for y in range(N_Y)])  12.1 us
    all_to_all x1, waiting for transfers between devices, shards(): lax.all_to_all(jnp.broadcast_to(piece, (N_Z,) + piece.shape), 'z', 0, 0)  8.92 us
    all_to_all x1, starting transfers between devices, shards(): lax.all_to_all(plane_sum.reshape(N_Z, BLOCK // N_Z, half), 'z', 0, 0)  7.14 us
    ppermute x1, starting transfers between devices, shards(): state_peer = lax.ppermute(state_theirs, 'core', SWAP)  6.68 us
  transfers between devices with their start and end apart: 38, of which 20 were waited for; matrix products, arithmetic and copies ran while one was open for 1% of the time, Pallas kernels for 0%

profile of v2, /device:TPU:25, one launch (start us, length us, event | category | flops | bytes accessed | tf_op | source)
XLA Modules:
  0.0 149.3 jit_solution(9111845831657372937)
XLA Ops:
  1.8 1.1 gather_fusion
  5.0 1.1 collective-permute-done.1.hidden_peer
  6.1 3.0 %shard_map.111 = (bf16[256,896]{1,0:T(8,128)(2,1)S(1)}, bf16[256,896]{1,0:T(8,128)(2,1)S(1)}, bf16[256,896]{1,0:T(8,128)(2,1)S(1)}, bf16[256,896]{1,0:T(8,128)(2...) custom-call(s32[3]{0:T(128)S(1)} %pad_add_fusion.here, ...), custom_call_target="tpu_custom_call" | custom-call | flops 939524096 | bytes 5000000 | tf_op jit(solution)/shard_map/pallas_call | solution.py:66
  9.1 1.8 %collective-permute-start.3 = (bf16[256,896]{1,0:T(8,128)(2,1)S(1)}, bf16[256,896]{1,0:T(8,128)(2,1)S(1)}, u32[]{:S(2)}, u32[]{:S(2)}) collective-permute-start(bf16[256,896]{1,0:T(8,128)(2,1)S(1)} %get-tuple-element.13), channel_id=1, source_target_pairs={{0,32},{32,64},{64,96},{96,0},{1,33},{33,65},{65,97},{97,1},{2,34}... | collective-permute-start | bytes 1376264 | tf_op jit(solution)/shard_map/ppermute | solution.py:28
  11.6 1.1 collective-permute-start.9
  12.7 2.5 %collective-permute-start.10 = (bf16[256,896]{1,0:T(8,128)(2,1)S(1)}, bf16[256,896]{1,0:T(8,128)(2,1)S(1)}, u32[]{:S(2)}, u32[]{:S(2)}) collective-permute-start(bf16[256,896]{1,0:T(8,128)(2,1)S(1)} %get-tuple-element.18), channel_id=1, source_target_pairs={{0,16},{128,144},{16,0},{144,128},{1,17},{129,145},{17,1},{145,129... | collective-permute-start | bytes 1376264 | tf_op jit(solution)/shard_map/ppermute | solution.py:24
  15.1 5.8 %collective-permute-done.3 = bf16[256,896]{1,0:T(8,128)(2,1)S(1)} collective-permute-done((bf16[256,896]{1,0:T(8,128)(2,1)S(1)}, bf16[256,896]{1,0:T(8,128)(2,1)S(1)}, u32[]{:S(2)}, u32[]{:S(2)}) %collective-permute-start.3) | collective-permute-done | bytes 458784 | tf_op jit(solution)/shard_map/ppermute | solution.py:28
  21.0 2.5 %collective-permute-start.11 = (bf16[256,896]{1,0:T(8,128)(2,1)S(1)}, bf16[256,896]{1,0:T(8,128)(2,1)S(1)}, u32[]{:S(2)}, u32[]{:S(2)}) collective-permute-start(bf16[256,896]{1,0:T(8,128)(2,1)S(1)} %get-tuple-element.19), channel_id=1, source_target_pairs={{0,144},{128,0},{16,128},{144,16},{1,145},{129,1},{17,129},{145,17... | collective-permute-start | bytes 1376264 | tf_op jit(solution)/shard_map/ppermute | solution.py:24
  23.8 10.8 %collective-permute-done.5 = bf16[256,896]{1,0:T(8,128)(2,1)S(1)} collective-permute-done((bf16[256,896]{1,0:T(8,128)(2,1)S(1)}, bf16[256,896]{1,0:T(8,128)(2,1)S(1)}, u32[]{:S(2)}, u32[]{:S(2)}) %collective-permute-start.5) | collective-permute-done | bytes 458784 | tf_op jit(solution)/shard_map/ppermute | solution.py:28
  34.9 2.7 %collective-permute-start.8 = (bf16[64,896]{1,0:T(8,128)(2,1)S(1)}, bf16[64,896]{1,0:T(8,128)(2,1)S(1)}, u32[]{:S(2)}, u32[]{:S(2)}) collective-permute-start(bf16[64,896]{1,0:T(8,128)(2,1)S(1)} %get-tuple-element.24), channel_id=1, source_target_pairs={{0,144},{128,0},{16,128},{144,16},{1,145},{129,1},{17,129},{145,17... | collective-permute-start | bytes 344072 | tf_op jit(solution)/shard_map/ppermute | solution.py:24
  37.9 1.4 collective-permute-start.14
  39.3 1.0 collective-permute-done.6
  40.9 1.8 %collective-permute-done.7 = bf16[64,896]{1,0:T(8,128)(2,1)S(1)} collective-permute-done((bf16[64,896]{1,0:T(8,128)(2,1)S(1)}, bf16[64,896]{1,0:T(8,128)(2,1)S(1)}, u32[]{:S(2)}, u32[]{:S(2)}) %collective-permute-start.7) | collective-permute-done | bytes 114720 | tf_op jit(solution)/shard_map/ppermute | solution.py:24
  43.0 2.5 %collective-permute-done.13 = bf16[64,896]{1,0:T(8,128)(2,1)S(1)} collective-permute-done((bf16[64,896]{1,0:T(8,128)(2,1)S(1)}, bf16[64,896]{1,0:T(8,128)(2,1)S(1)}, u32[]{:S(2)}, u32[]{:S(2)}) %collective-permute-start.13) | collective-permute-done | bytes 114720 | tf_op jit(solution)/shard_map/ppermute | solution.py:28
  46.3 7.1 %all-to-all-start = ((bf16[8,8,1792]{2,1,0:T(8,128)(2,1)}), bf16[8,8,1792]{2,1,0:T(8,128)(2,1)S(1)}, u32[]{:S(2)}, u32[]{:S(2)}) async-start(bf16[8,8,1792]{2,1,0:T(8,128)(2,1)} %pad_maximum_fusion.2), calls=%async_computation | async-start | bytes 458752 | tf_op jit(solution)/shard_map/all_to_all | solution.py:168
  53.5 6.7 %collective-permute-start = (f32[3,4,1792]{2,1,0:T(4,128)S(1)}, f32[3,4,1792]{2,1,0:T(4,128)S(1)}, u32[]{:S(2)}, u32[]{:S(2)}) collective-permute-start(f32[3,4,1792]{2,1,0:T(4,128)S(1)} %get-tuple-element.39), channel_id=1, source_target_pairs={{0,1},{1,0},{2,3},{3,2},{4,5},{5,4},{6,7},{7,6},{8,9},{9,8},{10,11... | collective-permute-start | bytes 258056 | tf_op jit(solution)/shard_map/ppermute | solution.py:145
  61.2 1.3 all-to-all-done
  63.2 5.7 %all-to-all-start.1 = ((bf16[8,8,1792]{2,1,0:T(8,128)(2,1)}), bf16[8,8,1792]{2,1,0:T(8,128)(2,1)S(1)}, u32[]{:S(2)}, u32[]{:S(2)}) async-start(bf16[8,8,1792]{2,1,0:T(8,128)(2,1)} %broadcast_in_dim.9), calls=%async_computation.1 | async-start | bytes 458752 | tf_op jit(solution)/shard_map/all_to_all | solution.py:186
  69.0 8.9 %all-to-all-done.1 = bf16[8,8,1792]{2,1,0:T(8,128)(2,1)S(1)} async-done(((bf16[8,8,1792]{2,1,0:T(8,128)(2,1)}), bf16[8,8,1792]{2,1,0:T(8,128)(2,1)S(1)}, u32[]{:S(2)}, u32[]{:S(2)}) %all-to-all-start.1) | async-done | bytes 229408 | tf_op jit(solution)/shard_map/all_to_all | solution.py:186
  77.9 3.5 %collective-permute-start.17 = (bf16[64,896]{1,0:T(8,128)(2,1)S(1)}, bf16[64,896]{1,0:T(8,128)(2,1)S(1)}, u32[]{:S(2)}, u32[]{:S(2)}) collective-permute-start(bf16[64,896]{1,0:T(8,128)(2,1)S(1)} %get-tuple-element.32), channel_id=1, source_target_pairs={{0,144},{128,0},{16,128},{144,16},{1,145},{129,1},{17,129},{145,17... | collective-permute-start | bytes 344072 | tf_op jit(solution)/shard_map/ppermute | solution.py:24
  82.1 1.6 %collective-permute-start.23 = (bf16[64,896]{1,0:T(8,128)(2,1)S(1)}, bf16[64,896]{1,0:T(8,128)(2,1)S(1)}, u32[]{:S(2)}, u32[]{:S(2)}) collective-permute-start(bf16[64,896]{1,0:T(8,128)(2,1)S(1)} %get-tuple-element.31), channel_id=1, source_target_pairs={{0,96},{32,0},{64,32},{96,64},{1,97},{33,1},{65,33},{97,65},{2,98}... | collective-permute-start | bytes 344072 | tf_op jit(solution)/shard_map/ppermute | solution.py:28
  84.4 1.8 %collective-permute-start.21 = (bf16[64,896]{1,0:T(8,128)(2,1)S(1)}, bf16[64,896]{1,0:T(8,128)(2,1)S(1)}, u32[]{:S(2)}, u32[]{:S(2)}) collective-permute-start(bf16[64,896]{1,0:T(8,128)(2,1)S(1)} %get-tuple-element.31), channel_id=1, source_target_pairs={{0,32},{32,64},{64,96},{96,0},{1,33},{33,65},{65,97},{97,1},{2,34}... | collective-permute-start | bytes 344072 | tf_op jit(solution)/shard_map/ppermute | solution.py:28
  87.6 8.1 %collective-permute-start.27 = (bf16[256,896]{1,0:T(8,128)(2,1)S(1)}, bf16[256,896]{1,0:T(8,128)(2,1)S(1)}, u32[]{:S(2)}, u32[]{:S(2)}) collective-permute-start(bf16[256,896]{1,0:T(8,128)(2,1)S(1)} %pad_maximum_fusion.refs_0_), channel_id=1, source_target_pairs={{0,1},{1,0},{2,3},{3,2},{4,5},{5,4},{6,7},{7,6},{8,9},{9,8},{10,11... | collective-permute-start | bytes 1376264 | tf_op jit(solution)/shard_map/ppermute | solution.py:193
  95.6 1.5 collective-permute-start.20
  97.4 2.1 %collective-permute-start.18 = (bf16[256,896]{1,0:T(8,128)(2,1)S(1)}, bf16[256,896]{1,0:T(8,128)(2,1)S(1)}, u32[]{:S(2)}, u32[]{:S(2)}) collective-permute-start(bf16[256,896]{1,0:T(8,128)(2,1)S(1)} %pad_maximum_fusion.refs_0_), channel_id=1, source_target_pairs={{0,32},{32,64},{64,96},{96,0},{1,33},{33,65},{65,97},{97,1},{2,34}... | collective-permute-start | bytes 1376264 | tf_op jit(solution)/shard_map/ppermute | solution.py:28
  101.7 1.6 %collective-permute-start.26 = (bf16[256,896]{1,0:T(8,128)(2,1)S(1)}, bf16[256,896]{1,0:T(8,128)(2,1)S(1)}, u32[]{:S(2)}, u32[]{:S(2)}) collective-permute-start(bf16[256,896]{1,0:T(8,128)(2,1)S(1)} %pad_maximum_fusion.1.refs_4_), channel_id=1, source_target_pairs={{0,144},{128,0},{16,128},{144,16},{1,145},{129,1},{17,129},{145,17... | collective-permute-start | bytes 1376264 | tf_op jit(solution)/shard_map/ppermute | solution.py:24
  103.3 15.4 %collective-permute-done.20.refs_3_ = bf16[256,896]{1,0:T(8,128)(2,1)S(1)} collective-permute-done((bf16[256,896]{1,0:T(8,128)(2,1)S(1)}, bf16[256,896]{1,0:T(8,128)(2,1)S(1)}, u32[]{:S(2)}, u32[]{:S(2)}) %collective-permute-start.20) | collective-permute-done | bytes 458784 | tf_op jit(solution)/shard_map/ppermute | solution.py:28
  119.5 1.2 collective-permute-start.30
  121.4 10.0 %collective-permute-done.25.refs_6_ = bf16[256,896]{1,0:T(8,128)(2,1)S(1)} collective-permute-done((bf16[256,896]{1,0:T(8,128)(2,1)S(1)}, bf16[256,896]{1,0:T(8,128)(2,1)S(1)}, u32[]{:S(2)}, u32[]{:S(2)}) %collective-permute-start.25) | collective-permute-done | bytes 458784 | tf_op jit(solution)/shard_map/ppermute | solution.py:24
  131.4 3.1 %collective-permute-start.34 = (bf16[256,896]{1,0:T(8,128)(2,1)S(1)}, bf16[256,896]{1,0:T(8,128)(2,1)S(1)}, u32[]{:S(2)}, u32[]{:S(2)}) collective-permute-start(bf16[256,896]{1,0:T(8,128)(2,1)S(1)} %collective-permute-done.26.refs_7_), channel_id=1, source_target_pairs={{0,1},{1,0},{2,3},{3,2},{4,5},{5,4},{6,7},{7,6},{8,9},{9,8},{10,11... | collective-permute-start | bytes 1376264 | tf_op jit(solution)/shard_map/ppermute | solution.py:193
  134.6 7.9 %collective-permute-done.24.refs_5_ = bf16[256,896]{1,0:T(8,128)(2,1)S(1)} collective-permute-done((bf16[256,896]{1,0:T(8,128)(2,1)S(1)}, bf16[256,896]{1,0:T(8,128)(2,1)S(1)}, u32[]{:S(2)}, u32[]{:S(2)}) %collective-permute-start.24) | collective-permute-done | bytes 458784 | tf_op jit(solution)/shard_map/ppermute | solution.py:24
  145.1 4.1 %shard_map.112 = bf16[1024,3584]{1,0:T(8,128)(2,1)} custom-call(s32[3]{0:T(128)S(1)} %pad_add_fusion.here, bf16[256,896]{1,0:T(8,128)(2,1)S(1)} %pad_maximum_fusion.refs_0_, bf16[256,896]{1,0:T(8,128)(2,1)S(1)} %collective-permute-done.18.refs_1_, bf16[256,896]{1,0:T(8,128)(2,1)S(1)} %collective-permute-done.19.refs_2_, ...), custom_call_target="tpu_custom_call" | custom-call | bytes 14680064 | tf_op jit(solution)/shard_map/pallas_call | solution.py:111
  (85 shorter events, 17.7 us)
Async XLA Ops:
  9.1 11.8 %collective-permute-start.3 = (bf16[256,896]{1,0:T(8,128)(2,1)S(1)}, bf16[256,896]{1,0:T(8,128)(2,1)S(1)}, u32[]{:S(2)}, u32[]{:S(2)}) collective-permute-start(bf16[256,896]{1,0:T(8,128)(2,1)S(1)} %get-tuple-element.13), channel_id=1, source_target_pairs={{0,32},{32,64},{64,96},{96,0},{1,33},{33,65},{65,97},{97,1},{2,34}... | collective-permute-start | bytes 1376264 | tf_op jit(solution)/shard_map/ppermute | solution.py:28
  10.9 13.0 %collective-permute-start.4 = (bf16[256,896]{1,0:T(8,128)(2,1)S(1)}, bf16[256,896]{1,0:T(8,128)(2,1)S(1)}, u32[]{:S(2)}, u32[]{:S(2)}) collective-permute-start(bf16[256,896]{1,0:T(8,128)(2,1)S(1)} %get-tuple-element.14), channel_id=1, source_target_pairs={{0,64},{32,96},{64,0},{96,32},{1,65},{33,97},{65,1},{97,33},{2,66}... | collective-permute-start | bytes 1376264 | tf_op jit(solution)/shard_map/ppermute | solution.py:28
  11.5 23.2 %collective-permute-start.5 = (bf16[256,896]{1,0:T(8,128)(2,1)S(1)}, bf16[256,896]{1,0:T(8,128)(2,1)S(1)}, u32[]{:S(2)}, u32[]{:S(2)}) collective-permute-start(bf16[256,896]{1,0:T(8,128)(2,1)S(1)} %get-tuple-element.15), channel_id=1, source_target_pairs={{0,96},{32,0},{64,32},{96,64},{1,97},{33,1},{65,33},{97,65},{2,98}... | collective-permute-start | bytes 1376264 | tf_op jit(solution)/shard_map/ppermute | solution.py:28
  11.6 26.0 %collective-permute-start.9 = (bf16[256,896]{1,0:T(8,128)(2,1)S(1)}, bf16[256,896]{1,0:T(8,128)(2,1)S(1)}, u32[]{:S(2)}, u32[]{:S(2)}) collective-permute-start(bf16[256,896]{1,0:T(8,128)(2,1)S(1)} %get-tuple-element.17), channel_id=1, source_target_pairs={{0,128},{128,16},{16,144},{144,0},{1,129},{129,17},{17,145},{145,1... | collective-permute-start | bytes 1376264 | tf_op jit(solution)/shard_map/ppermute | solution.py:24
  12.7 24.9 %collective-permute-start.10 = (bf16[256,896]{1,0:T(8,128)(2,1)S(1)}, bf16[256,896]{1,0:T(8,128)(2,1)S(1)}, u32[]{:S(2)}, u32[]{:S(2)}) collective-permute-start(bf16[256,896]{1,0:T(8,128)(2,1)S(1)} %get-tuple-element.18), channel_id=1, source_target_pairs={{0,16},{128,144},{16,0},{144,128},{1,17},{129,145},{17,1},{145,129... | collective-permute-start | bytes 1376264 | tf_op jit(solution)/shard_map/ppermute | solution.py:24
  21.0 16.7 %collective-permute-start.11 = (bf16[256,896]{1,0:T(8,128)(2,1)S(1)}, bf16[256,896]{1,0:T(8,128)(2,1)S(1)}, u32[]{:S(2)}, u32[]{:S(2)}) collective-permute-start(bf16[256,896]{1,0:T(8,128)(2,1)S(1)} %get-tuple-element.19), channel_id=1, source_target_pairs={{0,144},{128,0},{16,128},{144,16},{1,145},{129,1},{17,129},{145,17... | collective-permute-start | bytes 1376264 | tf_op jit(solution)/shard_map/ppermute | solution.py:24
  34.8 5.5 %collective-permute-start.6 = (bf16[64,896]{1,0:T(8,128)(2,1)S(1)}, bf16[64,896]{1,0:T(8,128)(2,1)S(1)}, u32[]{:S(2)}, u32[]{:S(2)}) collective-permute-start(bf16[64,896]{1,0:T(8,128)(2,1)S(1)} %get-tuple-element.23), channel_id=1, source_target_pairs={{0,128},{128,16},{16,144},{144,0},{1,129},{129,17},{17,145},{145,1... | collective-permute-start | bytes 344072 | tf_op jit(solution)/shard_map/ppermute | solution.py:24
  34.9 6.0 %collective-permute-start.8 = (bf16[64,896]{1,0:T(8,128)(2,1)S(1)}, bf16[64,896]{1,0:T(8,128)(2,1)S(1)}, u32[]{:S(2)}, u32[]{:S(2)}) collective-permute-start(bf16[64,896]{1,0:T(8,128)(2,1)S(1)} %get-tuple-element.24), channel_id=1, source_target_pairs={{0,144},{128,0},{16,128},{144,16},{1,145},{129,1},{17,129},{145,17... | collective-permute-start | bytes 344072 | tf_op jit(solution)/shard_map/ppermute | solution.py:24
  37.6 5.1 %collective-permute-start.7 = (bf16[64,896]{1,0:T(8,128)(2,1)S(1)}, bf16[64,896]{1,0:T(8,128)(2,1)S(1)}, u32[]{:S(2)}, u32[]{:S(2)}) collective-permute-start(bf16[64,896]{1,0:T(8,128)(2,1)S(1)} %get-tuple-element.25), channel_id=1, source_target_pairs={{0,16},{128,144},{16,0},{144,128},{1,17},{129,145},{17,1},{145,129... | collective-permute-start | bytes 344072 | tf_op jit(solution)/shard_map/ppermute | solution.py:24
  37.9 5.1 %collective-permute-start.14 = (bf16[64,896]{1,0:T(8,128)(2,1)S(1)}, bf16[64,896]{1,0:T(8,128)(2,1)S(1)}, u32[]{:S(2)}, u32[]{:S(2)}) collective-permute-start(bf16[64,896]{1,0:T(8,128)(2,1)S(1)} %get-tuple-element.27), channel_id=1, source_target_pairs={{0,96},{32,0},{64,32},{96,64},{1,97},{33,1},{65,33},{97,65},{2,98}... | collective-permute-start | bytes 344072 | tf_op jit(solution)/shard_map/ppermute | solution.py:28
  40.4 5.1 %collective-permute-start.13 = (bf16[64,896]{1,0:T(8,128)(2,1)S(1)}, bf16[64,896]{1,0:T(8,128)(2,1)S(1)}, u32[]{:S(2)}, u32[]{:S(2)}) collective-permute-start(bf16[64,896]{1,0:T(8,128)(2,1)S(1)} %get-tuple-element.28), channel_id=1, source_target_pairs={{0,64},{32,96},{64,0},{96,32},{1,65},{33,97},{65,1},{97,33},{2,66}... | collective-permute-start | bytes 344072 | tf_op jit(solution)/shard_map/ppermute | solution.py:28
  46.3 16.1 %all-to-all-start = ((bf16[8,8,1792]{2,1,0:T(8,128)(2,1)}), bf16[8,8,1792]{2,1,0:T(8,128)(2,1)S(1)}, u32[]{:S(2)}, u32[]{:S(2)}) async-start(bf16[8,8,1792]{2,1,0:T(8,128)(2,1)} %pad_maximum_fusion.2), calls=%async_computation | async-start | bytes 458752 | tf_op jit(solution)/shard_map/all_to_all | solution.py:168
  53.5 7.6 %collective-permute-start = (f32[3,4,1792]{2,1,0:T(4,128)S(1)}, f32[3,4,1792]{2,1,0:T(4,128)S(1)}, u32[]{:S(2)}, u32[]{:S(2)}) collective-permute-start(f32[3,4,1792]{2,1,0:T(4,128)S(1)} %get-tuple-element.39), channel_id=1, source_target_pairs={{0,1},{1,0},{2,3},{3,2},{4,5},{5,4},{6,7},{7,6},{8,9},{9,8},{10,11... | collective-permute-start | bytes 258056 | tf_op jit(solution)/shard_map/ppermute | solution.py:145
  63.2 14.7 %all-to-all-start.1 = ((bf16[8,8,1792]{2,1,0:T(8,128)(2,1)}), bf16[8,8,1792]{2,1,0:T(8,128)(2,1)S(1)}, u32[]{:S(2)}, u32[]{:S(2)}) async-start(bf16[8,8,1792]{2,1,0:T(8,128)(2,1)} %broadcast_in_dim.9), calls=%async_computation.1 | async-start | bytes 458752 | tf_op jit(solution)/shard_map/all_to_all | solution.py:186
  77.9 6.5 %collective-permute-start.17 = (bf16[64,896]{1,0:T(8,128)(2,1)S(1)}, bf16[64,896]{1,0:T(8,128)(2,1)S(1)}, u32[]{:S(2)}, u32[]{:S(2)}) collective-permute-start(bf16[64,896]{1,0:T(8,128)(2,1)S(1)} %get-tuple-element.32), channel_id=1, source_target_pairs={{0,144},{128,0},{16,128},{144,16},{1,145},{129,1},{17,129},{145,17... | collective-permute-start | bytes 344072 | tf_op jit(solution)/shard_map/ppermute | solution.py:24
  81.4 5.3 %collective-permute-start.16 = (bf16[64,896]{1,0:T(8,128)(2,1)S(1)}, bf16[64,896]{1,0:T(8,128)(2,1)S(1)}, u32[]{:S(2)}, u32[]{:S(2)}) collective-permute-start(bf16[64,896]{1,0:T(8,128)(2,1)S(1)} %get-tuple-element.32), channel_id=1, source_target_pairs={{0,16},{128,144},{16,0},{144,128},{1,17},{129,145},{17,1},{145,129... | collective-permute-start | bytes 344072 | tf_op jit(solution)/shard_map/ppermute | solution.py:24
  81.4 6.1 %collective-permute-start.15 = (bf16[64,896]{1,0:T(8,128)(2,1)S(1)}, bf16[64,896]{1,0:T(8,128)(2,1)S(1)}, u32[]{:S(2)}, u32[]{:S(2)}) collective-permute-start(bf16[64,896]{1,0:T(8,128)(2,1)S(1)} %get-tuple-element.32), channel_id=1, source_target_pairs={{0,128},{128,16},{16,144},{144,0},{1,129},{129,17},{17,145},{145,1... | collective-permute-start | bytes 344072 | tf_op jit(solution)/shard_map/ppermute | solution.py:24
  82.1 15.0 %collective-permute-start.23 = (bf16[64,896]{1,0:T(8,128)(2,1)S(1)}, bf16[64,896]{1,0:T(8,128)(2,1)S(1)}, u32[]{:S(2)}, u32[]{:S(2)}) collective-permute-start(bf16[64,896]{1,0:T(8,128)(2,1)S(1)} %get-tuple-element.31), channel_id=1, source_target_pairs={{0,96},{32,0},{64,32},{96,64},{1,97},{33,1},{65,33},{97,65},{2,98}... | collective-permute-start | bytes 344072 | tf_op jit(solution)/shard_map/ppermute | solution.py:28
  83.7 13.8 %collective-permute-start.22 = (bf16[64,896]{1,0:T(8,128)(2,1)S(1)}, bf16[64,896]{1,0:T(8,128)(2,1)S(1)}, u32[]{:S(2)}, u32[]{:S(2)}) collective-permute-start(bf16[64,896]{1,0:T(8,128)(2,1)S(1)} %get-tuple-element.31), channel_id=1, source_target_pairs={{0,64},{32,96},{64,0},{96,32},{1,65},{33,97},{65,1},{97,33},{2,66}... | collective-permute-start | bytes 344072 | tf_op jit(solution)/shard_map/ppermute | solution.py:28
  84.4 15.1 %collective-permute-start.21 = (bf16[64,896]{1,0:T(8,128)(2,1)S(1)}, bf16[64,896]{1,0:T(8,128)(2,1)S(1)}, u32[]{:S(2)}, u32[]{:S(2)}) collective-permute-start(bf16[64,896]{1,0:T(8,128)(2,1)S(1)} %get-tuple-element.31), channel_id=1, source_target_pairs={{0,32},{32,64},{64,96},{96,0},{1,33},{33,65},{65,97},{97,1},{2,34}... | collective-permute-start | bytes 344072 | tf_op jit(solution)/shard_map/ppermute | solution.py:28
  87.6 14.1 %collective-permute-start.27 = (bf16[256,896]{1,0:T(8,128)(2,1)S(1)}, bf16[256,896]{1,0:T(8,128)(2,1)S(1)}, u32[]{:S(2)}, u32[]{:S(2)}) collective-permute-start(bf16[256,896]{1,0:T(8,128)(2,1)S(1)} %pad_maximum_fusion.refs_0_), channel_id=1, source_target_pairs={{0,1},{1,0},{2,3},{3,2},{4,5},{5,4},{6,7},{7,6},{8,9},{9,8},{10,11... | collective-permute-start | bytes 1376264 | tf_op jit(solution)/shard_map/ppermute | solution.py:193
  95.6 23.1 %collective-permute-start.20 = (bf16[256,896]{1,0:T(8,128)(2,1)S(1)}, bf16[256,896]{1,0:T(8,128)(2,1)S(1)}, u32[]{:S(2)}, u32[]{:S(2)}) collective-permute-start(bf16[256,896]{1,0:T(8,128)(2,1)S(1)} %pad_maximum_fusion.refs_0_), channel_id=1, source_target_pairs={{0,96},{32,0},{64,32},{96,64},{1,97},{33,1},{65,33},{97,65},{2,98}... | collective-permute-start | bytes 1376264 | tf_op jit(solution)/shard_map/ppermute | solution.py:28
  97.1 22.4 %collective-permute-start.19 = (bf16[256,896]{1,0:T(8,128)(2,1)S(1)}, bf16[256,896]{1,0:T(8,128)(2,1)S(1)}, u32[]{:S(2)}, u32[]{:S(2)}) collective-permute-start(bf16[256,896]{1,0:T(8,128)(2,1)S(1)} %pad_maximum_fusion.refs_0_), channel_id=1, source_target_pairs={{0,64},{32,96},{64,0},{96,32},{1,65},{33,97},{65,1},{97,33},{2,66}... | collective-permute-start | bytes 1376264 | tf_op jit(solution)/shard_map/ppermute | solution.py:28
  97.4 22.1 %collective-permute-start.18 = (bf16[256,896]{1,0:T(8,128)(2,1)S(1)}, bf16[256,896]{1,0:T(8,128)(2,1)S(1)}, u32[]{:S(2)}, u32[]{:S(2)}) collective-permute-start(bf16[256,896]{1,0:T(8,128)(2,1)S(1)} %pad_maximum_fusion.refs_0_), channel_id=1, source_target_pairs={{0,32},{32,64},{64,96},{96,0},{1,33},{33,65},{65,97},{97,1},{2,34}... | collective-permute-start | bytes 1376264 | tf_op jit(solution)/shard_map/ppermute | solution.py:28
  101.3 19.5 %collective-permute-start.31 = (bf16[256,896]{1,0:T(8,128)(2,1)S(1)}, bf16[256,896]{1,0:T(8,128)(2,1)S(1)}, u32[]{:S(2)}, u32[]{:S(2)}) collective-permute-start(bf16[256,896]{1,0:T(8,128)(2,1)S(1)} %pad_maximum_fusion.1.refs_4_), channel_id=1, source_target_pairs={{0,1},{1,0},{2,3},{3,2},{4,5},{5,4},{6,7},{7,6},{8,9},{9,8},{10,11... | collective-permute-start | bytes 1376264 | tf_op jit(solution)/shard_map/ppermute | solution.py:193
  101.7 19.3 %collective-permute-start.26 = (bf16[256,896]{1,0:T(8,128)(2,1)S(1)}, bf16[256,896]{1,0:T(8,128)(2,1)S(1)}, u32[]{:S(2)}, u32[]{:S(2)}) collective-permute-start(bf16[256,896]{1,0:T(8,128)(2,1)S(1)} %pad_maximum_fusion.1.refs_4_), channel_id=1, source_target_pairs={{0,144},{128,0},{16,128},{144,16},{1,145},{129,1},{17,129},{145,17... | collective-permute-start | bytes 1376264 | tf_op jit(solution)/shard_map/ppermute | solution.py:24
  118.7 12.7 %collective-permute-start.25 = (bf16[256,896]{1,0:T(8,128)(2,1)S(1)}, bf16[256,896]{1,0:T(8,128)(2,1)S(1)}, u32[]{:S(2)}, u32[]{:S(2)}) collective-permute-start(bf16[256,896]{1,0:T(8,128)(2,1)S(1)} %pad_maximum_fusion.1.refs_4_), channel_id=1, source_target_pairs={{0,16},{128,144},{16,0},{144,128},{1,17},{129,145},{17,1},{145,129... | collective-permute-start | bytes 1376264 | tf_op jit(solution)/shard_map/ppermute | solution.py:24
  119.5 23.0 %collective-permute-start.24 = (bf16[256,896]{1,0:T(8,128)(2,1)S(1)}, bf16[256,896]{1,0:T(8,128)(2,1)S(1)}, u32[]{:S(2)}, u32[]{:S(2)}) collective-permute-start(bf16[256,896]{1,0:T(8,128)(2,1)S(1)} %pad_maximum_fusion.1.refs_4_), channel_id=1, source_target_pairs={{0,128},{128,16},{16,144},{144,0},{1,129},{129,17},{17,145},{145,1... | collective-permute-start | bytes 1376264 | tf_op jit(solution)/shard_map/ppermute | solution.py:24
  119.5 23.5 %collective-permute-start.30 = (bf16[256,896]{1,0:T(8,128)(2,1)S(1)}, bf16[256,896]{1,0:T(8,128)(2,1)S(1)}, u32[]{:S(2)}, u32[]{:S(2)}) collective-permute-start(bf16[256,896]{1,0:T(8,128)(2,1)S(1)} %collective-permute-done.20.refs_3_), channel_id=1, source_target_pairs={{0,1},{1,0},{2,3},{3,2},{4,5},{5,4},{6,7},{7,6},{8,9},{9,8},{10,11... | collective-permute-start | bytes 1376264 | tf_op jit(solution)/shard_map/ppermute | solution.py:193
  120.8 22.8 %collective-permute-start.29 = (bf16[256,896]{1,0:T(8,128)(2,1)S(1)}, bf16[256,896]{1,0:T(8,128)(2,1)S(1)}, u32[]{:S(2)}, u32[]{:S(2)}) collective-permute-start(bf16[256,896]{1,0:T(8,128)(2,1)S(1)} %collective-permute-done.19.refs_2_), channel_id=1, source_target_pairs={{0,1},{1,0},{2,3},{3,2},{4,5},{5,4},{6,7},{7,6},{8,9},{9,8},{10,11... | collective-permute-start | bytes 1376264 | tf_op jit(solution)/shard_map/ppermute | solution.py:193
  121.0 22.7 %collective-permute-start.28 = (bf16[256,896]{1,0:T(8,128)(2,1)S(1)}, bf16[256,896]{1,0:T(8,128)(2,1)S(1)}, u32[]{:S(2)}, u32[]{:S(2)}) collective-permute-start(bf16[256,896]{1,0:T(8,128)(2,1)S(1)} %collective-permute-done.18.refs_1_), channel_id=1, source_target_pairs={{0,1},{1,0},{2,3},{3,2},{4,5},{5,4},{6,7},{7,6},{8,9},{9,8},{10,11... | collective-permute-start | bytes 1376264 | tf_op jit(solution)/shard_map/ppermute | solution.py:193
  131.4 12.2 %collective-permute-start.34 = (bf16[256,896]{1,0:T(8,128)(2,1)S(1)}, bf16[256,896]{1,0:T(8,128)(2,1)S(1)}, u32[]{:S(2)}, u32[]{:S(2)}) collective-permute-start(bf16[256,896]{1,0:T(8,128)(2,1)S(1)} %collective-permute-done.26.refs_7_), channel_id=1, source_target_pairs={{0,1},{1,0},{2,3},{3,2},{4,5},{5,4},{6,7},{7,6},{8,9},{9,8},{10,11... | collective-permute-start | bytes 1376264 | tf_op jit(solution)/shard_map/ppermute | solution.py:193
  (13 other events, 77.7 us)

commit v3 on v2

--- a/solution.py
+++ b/solution.py
@@ -79,44 +79,58 @@
 
 
 def join_kernel(here, *refs):
-    pieces, out, sems = refs[:16], refs[16], refs[17]
+    pieces, out, sems = refs[:8], refs[-2], refs[-1]
     width = pieces[0].shape[1]
-    x, y, core = here[0], here[1], here[2]
+    x, y, column = here[0], here[1], here[2]
     copies = []
-    for owner in range(2):
-        column = (core if owner == 0 else 1 - core) * (2 * width)
-        for side in range(2):
-            for far in range(4):
-                piece = pieces[8 * owner + 4 * side + far]
-                for near in range(4):
-                    dx, dy = (near, far) if side == 0 else (far, near)
-                    row = block_of((x + N_X - dx) % N_X, (y + N_Y - dy) % N_Y) * BLOCK
-                    copy = pltpu.make_async_copy(
-                        piece.at[pl.ds(near * BLOCK, BLOCK), :],
-                        out.at[
-                            pl.ds(pl.multiple_of(row, BLOCK), BLOCK),
-                            pl.ds(pl.multiple_of(column + side * width, 128), width),
-                        ],
-                        sems.at[len(copies)],
-                    )
-                    copy.start()
-                    copies.append(copy)
-    for copy in copies:
-        copy.wait()
-
-
-def join(here, pieces):
+
+    def copy(source, row, column):
+        started = pltpu.make_async_copy(
+            source,
+            out.at[
+                pl.ds(pl.multiple_of(row, BLOCK), BLOCK),
+                pl.ds(pl.multiple_of(column, 128), width),
+            ],
+            sems.at[len(copies)],
+        )
+        started.start()
+        copies.append(started)
+
+    for far in range(4):
+        for near in range(4):
+            place = pl.ds(near * BLOCK, BLOCK)
+            row = block_of((x + N_X - near) % N_X, (y + N_Y - far) % N_Y) * BLOCK
+            copy(pieces[far].at[place, :], row, column)
+            row = block_of((x + N_X - far) % N_X, (y + N_Y - near) % N_Y) * BLOCK
+            copy(pieces[4 + far].at[place, :], row, column + width)
+    for started in copies:
+        started.wait()
+
+
+def join(here, core, pieces, out=None):
     rows, width = pieces[0].shape
     size = rows * width * 16
+    place = jnp.stack([here[0], here[1], core * (2 * width)])
+    anywhere = pl.BlockSpec(memory_space=pl.ANY)
+    begun = [] if out is None else [out]
     return pl.pallas_call(
         join_kernel,
         out_shape=jax.ShapeDtypeStruct((4 * rows, 4 * width), jnp.bfloat16),
-        in_specs=[pl.BlockSpec(memory_space=pltpu.SMEM)] + [pl.BlockSpec(memory_space=pl.ANY)] * 16,
-        out_specs=pl.BlockSpec(memory_space=pl.ANY),
-        scratch_shapes=[pltpu.SemaphoreType.DMA((64,))],
+        in_specs=[pl.BlockSpec(memory_space=pltpu.SMEM)] + [anywhere] * (8 + len(begun)),
+        out_specs=anywhere,
+        scratch_shapes=[pltpu.SemaphoreType.DMA((32,))],
+        input_output_aliases={9: 0} if begun else {},
         compiler_params=pltpu.CompilerParams(vmem_limit_bytes=VMEM),
-        cost_estimate=pl.CostEstimate(flops=0, bytes_accessed=4 * size, transcendentals=0),
-    )(here, *pieces)
+        cost_estimate=pl.CostEstimate(flops=0, bytes_accessed=2 * size, transcendentals=0),
+    )(place, *pieces, *begun)
+
+
+def together(*values):
+    return lax.optimization_barrier(values)
+
+
+def after(value, earlier):
+    return lax.optimization_barrier((value, earlier))[0]
 
 
 def total(parts):
@@ -155,15 +169,28 @@
     scaled_peer = lax.ppermute(scaled_theirs, "core", SWAP)
 
     blocks = terms(here, hidden, hidden_peer, scaled_mine, scaled_peer)
-    first = [along_y(blocks[s], s) for s in (1, 2, 3)]
-    other = [along_x(blocks[4 + s], s) for s in (1, 2, 3)]
-    first, other = [blocks[0]] + first, [blocks[4]] + other
+    parts = together(
+        *[along_y(blocks[s], s) for s in (1, 3)],
+        *[along_x(blocks[4 + s], s) for s in (1, 3)],
+        along_x(blocks[6], 2),
+        along_y(blocks[2], 2),
+    )
+    first, other = [blocks[0], *parts[0:2], parts[5]], [blocks[4], *parts[2:4], parts[4]]
 
     def near(parts, s):
         return total([part[s * BLOCK : (s + 1) * BLOCK] for part in parts])
 
-    first = [near(first, 0)] + [along_x(near(first, s).astype(jnp.bfloat16), s) for s in (1, 2, 3)]
-    other = [near(other, 0)] + [along_y(near(other, s).astype(jnp.bfloat16), s) for s in (1, 2, 3)]
+    parts = together(
+        *[near(first, s).astype(jnp.bfloat16) for s in (1, 3, 2)],
+        *[near(other, s).astype(jnp.bfloat16) for s in (1, 3, 2)],
+        near(first, 0), near(other, 0),
+    )
+    parts = together(
+        *[along_x(parts[k], s) for k, s in enumerate((1, 3, 2))],
+        *[along_y(parts[3 + k], s) for k, s in enumerate((1, 3, 2))],
+        *parts[6:],
+    )
+    first, other = [parts[6], *parts[:3]], [parts[7], *parts[3:6]]
     plane_sum = jnp.concatenate([total(first), total(other)], 1).astype(jnp.bfloat16)
     parts = lax.all_to_all(plane_sum.reshape(N_Z, BLOCK // N_Z, half), "z", 0, 0)
     grad = jnp.sum(parts.astype(jnp.float32), 0)
@@ -185,13 +212,21 @@
 
     column = lax.all_to_all(jnp.broadcast_to(piece, (N_Z,) + piece.shape), "z", 0, 0)
     column = column.reshape(BLOCK, half)
-    first, other = column[:, :quarter], column[:, quarter:]
-    first = jnp.concatenate([first] + [along_x(first, s) for s in (1, 2, 3)], 0)
-    other = jnp.concatenate([other] + [along_y(other, s) for s in (1, 2, 3)], 0)
-    pieces = [first] + [along_y(first, s) for s in (1, 2, 3)]
-    pieces += [other] + [along_x(other, s) for s in (1, 2, 3)]
-    pieces += [lax.ppermute(piece, "core", SWAP) for piece in pieces]
-    return (join(here, pieces), state_out[0], state_out[1], state_out[2])
+    first, other = together(column[:, :quarter], column[:, quarter:])
+    parts = together(
+        *[along_x(first, s) for s in (1, 2, 3)], *[along_y(other, s) for s in (1, 2, 3)]
+    )
+    first = jnp.concatenate([first, *parts[:3]], 0)
+    other = jnp.concatenate([other, *parts[3:]], 0)
+    first, other = together(first, other)
+    pieces = list(together(
+        first, *[along_y(first, s) for s in (1, 2, 3)],
+        other, *[along_x(other, s) for s in (1, 2, 3)],
+    ))
+    swapped = [lax.ppermute(piece, "core", SWAP) for piece in pieces]
+    core = here[2]
+    new_weight = join(here, 1 - core, swapped, join(here, core, pieces))
+    return (new_weight, state_out[0], state_out[1], state_out[2])
 
 
 def solution(mesh):

time: 150 us -> 132 us (0.88)
  the two profiles are of different devices: /device:TPU:25 before, /device:TPU:1 now
where the time goes in v3:
time: 132 us
  starting transfers between devices  60.6 us (46%)
  waiting for transfers between devices  44.8 us (34%)
  blocking collectives  11.8 us (9%)
  Pallas kernels  8.28 us (6%)
  other arithmetic  3.14 us (2%)
  local copies, waits for them, and re-layouts  2.29 us (2%)
    ppermute x12, waiting for transfers between devices, along_y(): lax.ppermute(value, 'y', [(y, (y + shift) % N_Y) for y in range(N_Y)])  20.1 us
    ppermute x12, waiting for transfers between devices, along_x(): return lax.ppermute(value, ('xlo', 'xhi'), pairs)  18.1 us
    ppermute x1, starting transfers between devices, shards(): state_back = lax.ppermute(jnp.where(first_core, bottom, top), 'core', SWAP)  12.3 us
    ppermute x12, starting transfers between devices, along_x(): return lax.ppermute(value, ('xlo', 'xhi'), pairs)  12 us
    all_to_all x1, blocking collectives, shards(): lax.all_to_all(jnp.broadcast_to(piece, (N_Z,) + piece.shape), 'z', 0, 0)  11.8 us
    ppermute x8, starting transfers between devices, shards(): swapped = [lax.ppermute(piece, 'core', SWAP) for piece in pieces]  11.6 us
    ppermute x12, starting transfers between devices, along_y(): lax.ppermute(value, 'y', [(y, (y + shift) % N_Y) for y in range(N_Y)])  8.53 us
    all_to_all x1, starting transfers between devices, shards(): lax.all_to_all(plane_sum.reshape(N_Z, BLOCK // N_Z, half), 'z', 0, 0)  8.14 us
  transfers between devices with their start and end apart: 37, of which 19 were waited for; matrix products, arithmetic and copies ran while one was open for 1% of the time, Pallas kernels for 2%

profile of v3, /device:TPU:1, one launch (start us, length us, event | category | flops | bytes accessed | tf_op | source)
XLA Modules:
  0.0 132.0 jit_solution(2538381139181810614)
XLA Ops:
  1.8 1.1 gather_fusion
  3.3 3.3 %collective-permute-start.2 = (bf16[128,1792]{1,0:T(8,128)(2,1)S(1)}, bf16[128,1792]{1,0:T(8,128)(2,1)S(1)}, u32[]{:S(2)}, u32[]{:S(2)}) collective-permute-start(bf16[128,1792]{1,0:T(8,128)(2,1)S(1)} %get-tuple-element.111), channel_id=1, source_target_pairs={{0,1},{1,0},{2,3},{3,2},{4,5},{5,4},{6,7},{7,6},{8,9},{9,8},{10,11... | collective-permute-start | bytes 1376264 | tf_op jit(solution)/shard_map/ppermute | solution.py:169
  7.6 1.1 collective-permute-done.1.hidden_peer
  8.7 3.0 %shard_map.111 = (bf16[256,896]{1,0:T(8,128)(2,1)S(1)}, bf16[256,896]{1,0:T(8,128)(2,1)S(1)}, bf16[256,896]{1,0:T(8,128)(2,1)S(1)}, bf16[256,896]{1,0:T(8,128)(2...) custom-call(s32[3]{0:T(128)S(1)} %pad_add_fusion.2.here, ...), custom_call_target="tpu_custom_call" | custom-call | flops 939524096 | bytes 5000000 | tf_op jit(solution)/shard_map/pallas_call | solution.py:66
  11.7 2.7 %collective-permute-start.4 = (bf16[256,896]{1,0:T(8,128)(2,1)S(1)}, bf16[256,896]{1,0:T(8,128)(2,1)S(1)}, u32[]{:S(2)}, u32[]{:S(2)}) collective-permute-start(bf16[256,896]{1,0:T(8,128)(2,1)S(1)} %get-tuple-element.54), channel_id=1, source_target_pairs={{0,96},{32,0},{64,32},{96,64},{1,97},{33,1},{65,33},{97,65},{2,98}... | collective-permute-start | bytes 1376264 | tf_op jit(solution)/shard_map/ppermute | solution.py:28
  14.4 2.7 %collective-permute-start.6 = (bf16[256,896]{1,0:T(8,128)(2,1)S(1)}, bf16[256,896]{1,0:T(8,128)(2,1)S(1)}, u32[]{:S(2)}, u32[]{:S(2)}) collective-permute-start(bf16[256,896]{1,0:T(8,128)(2,1)S(1)} %get-tuple-element.56), channel_id=1, source_target_pairs={{0,144},{128,0},{16,128},{144,16},{1,145},{129,1},{17,129},{145,17... | collective-permute-start | bytes 1376264 | tf_op jit(solution)/shard_map/ppermute | solution.py:24
  17.1 7.6 %collective-permute-done.3 = bf16[256,896]{1,0:T(8,128)(2,1)S(1)} collective-permute-done((bf16[256,896]{1,0:T(8,128)(2,1)S(1)}, bf16[256,896]{1,0:T(8,128)(2,1)S(1)}, u32[]{:S(2)}, u32[]{:S(2)}) %collective-permute-start.3) | collective-permute-done | bytes 458784 | tf_op jit(solution)/shard_map/ppermute | solution.py:28
  24.7 2.5 %collective-permute-done.5 = bf16[256,896]{1,0:T(8,128)(2,1)S(1)} collective-permute-done((bf16[256,896]{1,0:T(8,128)(2,1)S(1)}, bf16[256,896]{1,0:T(8,128)(2,1)S(1)}, u32[]{:S(2)}, u32[]{:S(2)}) %collective-permute-start.5) | collective-permute-done | bytes 458784 | tf_op jit(solution)/shard_map/ppermute | solution.py:24
  27.1 9.0 %collective-permute-done.7 = bf16[256,896]{1,0:T(8,128)(2,1)S(1)} collective-permute-done((bf16[256,896]{1,0:T(8,128)(2,1)S(1)}, bf16[256,896]{1,0:T(8,128)(2,1)S(1)}, u32[]{:S(2)}, u32[]{:S(2)}) %collective-permute-start.7) | collective-permute-done | bytes 458784 | tf_op jit(solution)/shard_map/ppermute | solution.py:24
  37.7 2.5 %collective-permute-start.10 = (bf16[64,896]{1,0:T(8,128)(2,1)S(1)}, bf16[64,896]{1,0:T(8,128)(2,1)S(1)}, u32[]{:S(2)}, u32[]{:S(2)}) collective-permute-start(bf16[64,896]{1,0:T(8,128)(2,1)S(1)} %get-tuple-element.67), channel_id=1, source_target_pairs={{0,144},{128,0},{16,128},{144,16},{1,145},{129,1},{17,129},{145,17... | collective-permute-start | bytes 344072 | tf_op jit(solution)/shard_map/ppermute | solution.py:24
  40.2 2.7 %collective-permute-start.13 = (bf16[64,896]{1,0:T(8,128)(2,1)S(1)}, bf16[64,896]{1,0:T(8,128)(2,1)S(1)}, u32[]{:S(2)}, u32[]{:S(2)}) collective-permute-start(bf16[64,896]{1,0:T(8,128)(2,1)S(1)} %get-tuple-element.70), channel_id=1, source_target_pairs={{0,96},{32,0},{64,32},{96,64},{1,97},{33,1},{65,33},{97,65},{2,98}... | collective-permute-start | bytes 344072 | tf_op jit(solution)/shard_map/ppermute | solution.py:28
  43.2 3.2 %collective-permute-done.11 = bf16[64,896]{1,0:T(8,128)(2,1)S(1)} collective-permute-done((bf16[64,896]{1,0:T(8,128)(2,1)S(1)}, bf16[64,896]{1,0:T(8,128)(2,1)S(1)}, u32[]{:S(2)}, u32[]{:S(2)}) %collective-permute-start.11) | collective-permute-done | bytes 114720 | tf_op jit(solution)/shard_map/ppermute | solution.py:24
  46.5 2.5 %collective-permute-done.14 = bf16[64,896]{1,0:T(8,128)(2,1)S(1)} collective-permute-done((bf16[64,896]{1,0:T(8,128)(2,1)S(1)}, bf16[64,896]{1,0:T(8,128)(2,1)S(1)}, u32[]{:S(2)}, u32[]{:S(2)}) %collective-permute-start.14) | collective-permute-done | bytes 114720 | tf_op jit(solution)/shard_map/ppermute | solution.py:28
  49.8 8.1 %all-to-all-start = ((bf16[8,8,1792]{2,1,0:T(8,128)(2,1)}), bf16[8,8,1792]{2,1,0:T(8,128)(2,1)S(1)}, u32[]{:S(2)}, u32[]{:S(2)}) async-start(bf16[8,8,1792]{2,1,0:T(8,128)(2,1)} %pad_maximum_fusion.2), calls=%async_computation | async-start | bytes 458752 | tf_op jit(solution)/shard_map/all_to_all | solution.py:195
  58.0 4.0 %collective-permute-start = (f32[3,4,1792]{2,1,0:T(4,128)S(1)}, f32[3,4,1792]{2,1,0:T(4,128)S(1)}, u32[]{:S(2)}, u32[]{:S(2)}) collective-permute-start(f32[3,4,1792]{2,1,0:T(4,128)S(1)} %get-tuple-element.121), channel_id=1, source_target_pairs={{0,1},{1,0},{2,3},{3,2},{4,5},{5,4},{6,7},{7,6},{8,9},{9,8},{10,11... | collective-permute-start | bytes 258056 | tf_op jit(solution)/shard_map/ppermute | solution.py:159
  62.0 0.9 collective-permute-done
  63.0 3.9 %all-to-all-done = bf16[8,8,1792]{2,1,0:T(8,128)(2,1)S(1)} async-done(((bf16[8,8,1792]{2,1,0:T(8,128)(2,1)}), bf16[8,8,1792]{2,1,0:T(8,128)(2,1)S(1)}, u32[]{:S(2)}, u32[]{:S(2)}) %all-to-all-start) | async-done | bytes 229408 | tf_op jit(solution)/shard_map/all_to_all | solution.py:195
  67.1 11.8 %all_to_all.10 = bf16[8,8,1792]{2,1,0:T(8,128)(2,1)S(1)} all-to-all(bf16[8,8,1792]{2,1,0:T(8,128)(2,1)S(1)} %broadcast_in_dim.9), channel_id=1, replica_groups=mesh['xlo'=2,'y'=4,'xhi'=2,'z'=8,'core'=2] {'z'}, dimensions={0} | all-to-all | bytes 458752 | tf_op jit(solution)/shard_map/all_to_all | solution.py:213
  78.9 0.9 collective-permute-start.17
  79.8 1.5 %collective-permute-start.16 = (bf16[64,896]{1,0:T(8,128)(2,1)S(1)}, bf16[64,896]{1,0:T(8,128)(2,1)S(1)}, u32[]{:S(2)}, u32[]{:S(2)}) collective-permute-start(bf16[64,896]{1,0:T(8,128)(2,1)S(1)} %get-tuple-element.82), channel_id=1, source_target_pairs={{0,16},{128,144},{16,0},{144,128},{1,17},{129,145},{17,1},{145,129... | collective-permute-start | bytes 344072 | tf_op jit(solution)/shard_map/ppermute | solution.py:24
  83.5 1.4 %collective-permute-done.16 = bf16[64,896]{1,0:T(8,128)(2,1)S(1)} collective-permute-done((bf16[64,896]{1,0:T(8,128)(2,1)S(1)}, bf16[64,896]{1,0:T(8,128)(2,1)S(1)}, u32[]{:S(2)}, u32[]{:S(2)}) %collective-permute-start.16) | collective-permute-done | bytes 114720 | tf_op jit(solution)/shard_map/ppermute | solution.py:24
  85.0 1.2 collective-permute-done.15
  86.2 1.2 collective-permute-done.19
  87.4 1.2 collective-permute-done.18
  88.7 1.3 %collective-permute-start.23 = (bf16[256,896]{1,0:T(8,128)(2,1)S(1)}, bf16[256,896]{1,0:T(8,128)(2,1)S(1)}, u32[]{:S(2)}, u32[]{:S(2)}) collective-permute-start(bf16[256,896]{1,0:T(8,128)(2,1)S(1)} %pad_maximum_fusion.refs_0_), channel_id=1, source_target_pairs={{0,96},{32,0},{64,32},{96,64},{1,97},{33,1},{65,33},{97,65},{2,98}... | collective-permute-start | bytes 1376264 | tf_op jit(solution)/shard_map/ppermute | solution.py:28
  90.9 2.2 %collective-permute-start.26 = (bf16[256,896]{1,0:T(8,128)(2,1)S(1)}, bf16[256,896]{1,0:T(8,128)(2,1)S(1)}, u32[]{:S(2)}, u32[]{:S(2)}) collective-permute-start(bf16[256,896]{1,0:T(8,128)(2,1)S(1)} %pad_maximum_fusion.1.refs_4_), channel_id=1, source_target_pairs={{0,144},{128,0},{16,128},{144,16},{1,145},{129,1},{17,129},{145,17... | collective-permute-start | bytes 1376264 | tf_op jit(solution)/shard_map/ppermute | solution.py:24
  93.3 5.5 %collective-permute-done.23.refs_3_ = bf16[256,896]{1,0:T(8,128)(2,1)S(1)} collective-permute-done((bf16[256,896]{1,0:T(8,128)(2,1)S(1)}, bf16[256,896]{1,0:T(8,128)(2,1)S(1)}, u32[]{:S(2)}, u32[]{:S(2)}) %collective-permute-start.23) | collective-permute-done | bytes 458784 | tf_op jit(solution)/shard_map/ppermute | solution.py:28
  99.8 1.3 collective-permute-done.22.refs_2_
  101.0 12.3 %collective-permute-start.35 = (f32[3,4,1792]{2,1,0:T(4,128)S(1)}, f32[3,4,1792]{2,1,0:T(4,128)S(1)}, u32[]{:S(2)}, u32[]{:S(2)}) collective-permute-start(f32[3,4,1792]{2,1,0:T(4,128)S(1)} %get-tuple-element.119), channel_id=1, source_target_pairs={{0,1},{1,0},{2,3},{3,2},{4,5},{5,4},{6,7},{7,6},{8,9},{9,8},{10,11... | collective-permute-start | bytes 258056 | tf_op jit(solution)/shard_map/ppermute | solution.py:210
  113.3 9.4 %collective-permute-start.27 = (bf16[256,896]{1,0:T(8,128)(2,1)S(1)}, bf16[256,896]{1,0:T(8,128)(2,1)S(1)}, u32[]{:S(2)}, u32[]{:S(2)}) collective-permute-start(bf16[256,896]{1,0:T(8,128)(2,1)S(1)} %pad_maximum_fusion.refs_0_), channel_id=1, source_target_pairs={{0,1},{1,0},{2,3},{3,2},{4,5},{5,4},{6,7},{7,6},{8,9},{9,8},{10,11... | collective-permute-start | bytes 1376264 | tf_op jit(solution)/shard_map/ppermute | solution.py:226
  126.5 2.6 %shard_map.112.refs_8_ = bf16[1024,3584]{1,0:T(8,128)(2,1)} custom-call(s32[3]{0:T(128)S(1)} %pad_add_fusion.3.here, bf16[256,896]{1,0:T(8,128)(2,1)S(1)} %pad_maximum_fusion.refs_0_, bf16[256,896]{1,0:T(8,128)(2,1)S(1)} %collective-permute-done.21.refs_1_, bf16[256,896]{1,0:T(8,128)(2,1)S(1)} %collective-permute-done.22.refs_2_, ...), custom_call_target="tpu_custom_call" | custom-call | bytes 7340032 | tf_op jit(solution)/shard_map/pallas_call | solution.py:116
  129.2 2.7 %shard_map.113 = bf16[1024,3584]{1,0:T(8,128)(2,1)} custom-call(s32[3]{0:T(128)S(1)} %pad_add_fusion.here, bf16[256,896]{1,0:T(8,128)(2,1)S(1)} %collective-permute-done.27.refs_0_, bf16[256,896]{1,0:T(8,128)(2,1)S(1)} %collective-permute-done.28.refs_1_, bf16[256,896]{1,0:T(8,128)(2,1)S(1)} %collective-permute-done.29.refs_2_, ...), custom_call_target="tpu_custom_call", output_to_operand_aliasing={{}: (9, {})} | custom-call | bytes 7340032 | tf_op jit(solution)/shard_map/pallas_call | solution.py:116
  (86 shorter events, 13.6 us)
Async XLA Ops:
  3.3 5.4 %collective-permute-start.2 = (bf16[128,1792]{1,0:T(8,128)(2,1)S(1)}, bf16[128,1792]{1,0:T(8,128)(2,1)S(1)}, u32[]{:S(2)}, u32[]{:S(2)}) collective-permute-start(bf16[128,1792]{1,0:T(8,128)(2,1)S(1)} %get-tuple-element.111), channel_id=1, source_target_pairs={{0,1},{1,0},{2,3},{3,2},{4,5},{5,4},{6,7},{7,6},{8,9},{9,8},{10,11... | collective-permute-start | bytes 1376264 | tf_op jit(solution)/shard_map/ppermute | solution.py:169
  11.6 13.0 %collective-permute-start.3 = (bf16[256,896]{1,0:T(8,128)(2,1)S(1)}, bf16[256,896]{1,0:T(8,128)(2,1)S(1)}, u32[]{:S(2)}, u32[]{:S(2)}) collective-permute-start(bf16[256,896]{1,0:T(8,128)(2,1)S(1)} %get-tuple-element.53), channel_id=1, source_target_pairs={{0,32},{32,64},{64,96},{96,0},{1,33},{33,65},{65,97},{97,1},{2,34}... | collective-permute-start | bytes 1376264 | tf_op jit(solution)/shard_map/ppermute | solution.py:28
  11.7 12.9 %collective-permute-start.4 = (bf16[256,896]{1,0:T(8,128)(2,1)S(1)}, bf16[256,896]{1,0:T(8,128)(2,1)S(1)}, u32[]{:S(2)}, u32[]{:S(2)}) collective-permute-start(bf16[256,896]{1,0:T(8,128)(2,1)S(1)} %get-tuple-element.54), channel_id=1, source_target_pairs={{0,96},{32,0},{64,32},{96,64},{1,97},{33,1},{65,33},{97,65},{2,98}... | collective-permute-start | bytes 1376264 | tf_op jit(solution)/shard_map/ppermute | solution.py:28
  14.4 12.7 %collective-permute-start.5 = (bf16[256,896]{1,0:T(8,128)(2,1)S(1)}, bf16[256,896]{1,0:T(8,128)(2,1)S(1)}, u32[]{:S(2)}, u32[]{:S(2)}) collective-permute-start(bf16[256,896]{1,0:T(8,128)(2,1)S(1)} %get-tuple-element.55), channel_id=1, source_target_pairs={{0,128},{128,16},{16,144},{144,0},{1,129},{129,17},{17,145},{145,1... | collective-permute-start | bytes 1376264 | tf_op jit(solution)/shard_map/ppermute | solution.py:24
  14.4 12.7 %collective-permute-start.6 = (bf16[256,896]{1,0:T(8,128)(2,1)S(1)}, bf16[256,896]{1,0:T(8,128)(2,1)S(1)}, u32[]{:S(2)}, u32[]{:S(2)}) collective-permute-start(bf16[256,896]{1,0:T(8,128)(2,1)S(1)} %get-tuple-element.56), channel_id=1, source_target_pairs={{0,144},{128,0},{16,128},{144,16},{1,145},{129,1},{17,129},{145,17... | collective-permute-start | bytes 1376264 | tf_op jit(solution)/shard_map/ppermute | solution.py:24
  17.1 19.1 %collective-permute-start.7 = (bf16[256,896]{1,0:T(8,128)(2,1)S(1)}, bf16[256,896]{1,0:T(8,128)(2,1)S(1)}, u32[]{:S(2)}, u32[]{:S(2)}) collective-permute-start(bf16[256,896]{1,0:T(8,128)(2,1)S(1)} %get-tuple-element.57), channel_id=1, source_target_pairs={{0,16},{128,144},{16,0},{144,128},{1,17},{129,145},{17,1},{145,129... | collective-permute-start | bytes 1376264 | tf_op jit(solution)/shard_map/ppermute | solution.py:24
  24.7 12.3 %collective-permute-start.8 = (bf16[256,896]{1,0:T(8,128)(2,1)S(1)}, bf16[256,896]{1,0:T(8,128)(2,1)S(1)}, u32[]{:S(2)}, u32[]{:S(2)}) collective-permute-start(bf16[256,896]{1,0:T(8,128)(2,1)S(1)} %get-tuple-element.58), channel_id=1, source_target_pairs={{0,64},{32,96},{64,0},{96,32},{1,65},{33,97},{65,1},{97,33},{2,66}... | collective-permute-start | bytes 1376264 | tf_op jit(solution)/shard_map/ppermute | solution.py:28
  37.4 5.5 %collective-permute-start.9 = (bf16[64,896]{1,0:T(8,128)(2,1)S(1)}, bf16[64,896]{1,0:T(8,128)(2,1)S(1)}, u32[]{:S(2)}, u32[]{:S(2)}) collective-permute-start(bf16[64,896]{1,0:T(8,128)(2,1)S(1)} %get-tuple-element.66), channel_id=1, source_target_pairs={{0,128},{128,16},{16,144},{144,0},{1,129},{129,17},{17,145},{145,1... | collective-permute-start | bytes 344072 | tf_op jit(solution)/shard_map/ppermute | solution.py:24
  37.7 5.6 %collective-permute-start.10 = (bf16[64,896]{1,0:T(8,128)(2,1)S(1)}, bf16[64,896]{1,0:T(8,128)(2,1)S(1)}, u32[]{:S(2)}, u32[]{:S(2)}) collective-permute-start(bf16[64,896]{1,0:T(8,128)(2,1)S(1)} %get-tuple-element.67), channel_id=1, source_target_pairs={{0,144},{128,0},{16,128},{144,16},{1,145},{129,1},{17,129},{145,17... | collective-permute-start | bytes 344072 | tf_op jit(solution)/shard_map/ppermute | solution.py:24
  40.2 6.3 %collective-permute-start.11 = (bf16[64,896]{1,0:T(8,128)(2,1)S(1)}, bf16[64,896]{1,0:T(8,128)(2,1)S(1)}, u32[]{:S(2)}, u32[]{:S(2)}) collective-permute-start(bf16[64,896]{1,0:T(8,128)(2,1)S(1)} %get-tuple-element.68), channel_id=1, source_target_pairs={{0,16},{128,144},{16,0},{144,128},{1,17},{129,145},{17,1},{145,129... | collective-permute-start | bytes 344072 | tf_op jit(solution)/shard_map/ppermute | solution.py:24
  40.2 6.2 %collective-permute-start.12 = (bf16[64,896]{1,0:T(8,128)(2,1)S(1)}, bf16[64,896]{1,0:T(8,128)(2,1)S(1)}, u32[]{:S(2)}, u32[]{:S(2)}) collective-permute-start(bf16[64,896]{1,0:T(8,128)(2,1)S(1)} %get-tuple-element.69), channel_id=1, source_target_pairs={{0,32},{32,64},{64,96},{96,0},{1,33},{33,65},{65,97},{97,1},{2,34}... | collective-permute-start | bytes 344072 | tf_op jit(solution)/shard_map/ppermute | solution.py:28
  40.2 6.2 %collective-permute-start.13 = (bf16[64,896]{1,0:T(8,128)(2,1)S(1)}, bf16[64,896]{1,0:T(8,128)(2,1)S(1)}, u32[]{:S(2)}, u32[]{:S(2)}) collective-permute-start(bf16[64,896]{1,0:T(8,128)(2,1)S(1)} %get-tuple-element.70), channel_id=1, source_target_pairs={{0,96},{32,0},{64,32},{96,64},{1,97},{33,1},{65,33},{97,65},{2,98}... | collective-permute-start | bytes 344072 | tf_op jit(solution)/shard_map/ppermute | solution.py:28
  42.9 6.1 %collective-permute-start.14 = (bf16[64,896]{1,0:T(8,128)(2,1)S(1)}, bf16[64,896]{1,0:T(8,128)(2,1)S(1)}, u32[]{:S(2)}, u32[]{:S(2)}) collective-permute-start(bf16[64,896]{1,0:T(8,128)(2,1)S(1)} %get-tuple-element.71), channel_id=1, source_target_pairs={{0,64},{32,96},{64,0},{96,32},{1,65},{33,97},{65,1},{97,33},{2,66}... | collective-permute-start | bytes 344072 | tf_op jit(solution)/shard_map/ppermute | solution.py:28
  49.8 17.1 %all-to-all-start = ((bf16[8,8,1792]{2,1,0:T(8,128)(2,1)}), bf16[8,8,1792]{2,1,0:T(8,128)(2,1)S(1)}, u32[]{:S(2)}, u32[]{:S(2)}) async-start(bf16[8,8,1792]{2,1,0:T(8,128)(2,1)} %pad_maximum_fusion.2), calls=%async_computation | async-start | bytes 458752 | tf_op jit(solution)/shard_map/all_to_all | solution.py:195
  58.0 5.0 %collective-permute-start = (f32[3,4,1792]{2,1,0:T(4,128)S(1)}, f32[3,4,1792]{2,1,0:T(4,128)S(1)}, u32[]{:S(2)}, u32[]{:S(2)}) collective-permute-start(f32[3,4,1792]{2,1,0:T(4,128)S(1)} %get-tuple-element.121), channel_id=1, source_target_pairs={{0,1},{1,0},{2,3},{3,2},{4,5},{5,4},{6,7},{7,6},{8,9},{9,8},{10,11... | collective-permute-start | bytes 258056 | tf_op jit(solution)/shard_map/ppermute | solution.py:159
  79.8 5.1 %collective-permute-start.16 = (bf16[64,896]{1,0:T(8,128)(2,1)S(1)}, bf16[64,896]{1,0:T(8,128)(2,1)S(1)}, u32[]{:S(2)}, u32[]{:S(2)}) collective-permute-start(bf16[64,896]{1,0:T(8,128)(2,1)S(1)} %get-tuple-element.82), channel_id=1, source_target_pairs={{0,16},{128,144},{16,0},{144,128},{1,17},{129,145},{17,1},{145,129... | collective-permute-start | bytes 344072 | tf_op jit(solution)/shard_map/ppermute | solution.py:24
  81.3 4.9 %collective-permute-start.15 = (bf16[64,896]{1,0:T(8,128)(2,1)S(1)}, bf16[64,896]{1,0:T(8,128)(2,1)S(1)}, u32[]{:S(2)}, u32[]{:S(2)}) collective-permute-start(bf16[64,896]{1,0:T(8,128)(2,1)S(1)} %get-tuple-element.82), channel_id=1, source_target_pairs={{0,128},{128,16},{16,144},{144,0},{1,129},{129,17},{17,145},{145,1... | collective-permute-start | bytes 344072 | tf_op jit(solution)/shard_map/ppermute | solution.py:24
  82.1 4.2 %collective-permute-start.20 = (bf16[64,896]{1,0:T(8,128)(2,1)S(1)}, bf16[64,896]{1,0:T(8,128)(2,1)S(1)}, u32[]{:S(2)}, u32[]{:S(2)}) collective-permute-start(bf16[64,896]{1,0:T(8,128)(2,1)S(1)} %get-tuple-element.83), channel_id=1, source_target_pairs={{0,96},{32,0},{64,32},{96,64},{1,97},{33,1},{65,33},{97,65},{2,98}... | collective-permute-start | bytes 344072 | tf_op jit(solution)/shard_map/ppermute | solution.py:28
  82.2 5.2 %collective-permute-start.19 = (bf16[64,896]{1,0:T(8,128)(2,1)S(1)}, bf16[64,896]{1,0:T(8,128)(2,1)S(1)}, u32[]{:S(2)}, u32[]{:S(2)}) collective-permute-start(bf16[64,896]{1,0:T(8,128)(2,1)S(1)} %get-tuple-element.83), channel_id=1, source_target_pairs={{0,64},{32,96},{64,0},{96,32},{1,65},{33,97},{65,1},{97,33},{2,66}... | collective-permute-start | bytes 344072 | tf_op jit(solution)/shard_map/ppermute | solution.py:28
  82.9 5.7 %collective-permute-start.18 = (bf16[64,896]{1,0:T(8,128)(2,1)S(1)}, bf16[64,896]{1,0:T(8,128)(2,1)S(1)}, u32[]{:S(2)}, u32[]{:S(2)}) collective-permute-start(bf16[64,896]{1,0:T(8,128)(2,1)S(1)} %get-tuple-element.83), channel_id=1, source_target_pairs={{0,32},{32,64},{64,96},{96,0},{1,33},{33,65},{65,97},{97,1},{2,34}... | collective-permute-start | bytes 344072 | tf_op jit(solution)/shard_map/ppermute | solution.py:28
  88.7 10.1 %collective-permute-start.23 = (bf16[256,896]{1,0:T(8,128)(2,1)S(1)}, bf16[256,896]{1,0:T(8,128)(2,1)S(1)}, u32[]{:S(2)}, u32[]{:S(2)}) collective-permute-start(bf16[256,896]{1,0:T(8,128)(2,1)S(1)} %pad_maximum_fusion.refs_0_), channel_id=1, source_target_pairs={{0,96},{32,0},{64,32},{96,64},{1,97},{33,1},{65,33},{97,65},{2,98}... | collective-permute-start | bytes 1376264 | tf_op jit(solution)/shard_map/ppermute | solution.py:28
  90.2 10.8 %collective-permute-start.22 = (bf16[256,896]{1,0:T(8,128)(2,1)S(1)}, bf16[256,896]{1,0:T(8,128)(2,1)S(1)}, u32[]{:S(2)}, u32[]{:S(2)}) collective-permute-start(bf16[256,896]{1,0:T(8,128)(2,1)S(1)} %pad_maximum_fusion.refs_0_), channel_id=1, source_target_pairs={{0,64},{32,96},{64,0},{96,32},{1,65},{33,97},{65,1},{97,33},{2,66}... | collective-permute-start | bytes 1376264 | tf_op jit(solution)/shard_map/ppermute | solution.py:28
  90.9 22.4 %collective-permute-start.21 = (bf16[256,896]{1,0:T(8,128)(2,1)S(1)}, bf16[256,896]{1,0:T(8,128)(2,1)S(1)}, u32[]{:S(2)}, u32[]{:S(2)}) collective-permute-start(bf16[256,896]{1,0:T(8,128)(2,1)S(1)} %pad_maximum_fusion.refs_0_), channel_id=1, source_target_pairs={{0,32},{32,64},{64,96},{96,0},{1,33},{33,65},{65,97},{97,1},{2,34}... | collective-permute-start | bytes 1376264 | tf_op jit(solution)/shard_map/ppermute | solution.py:28
  90.9 22.4 %collective-permute-start.26 = (bf16[256,896]{1,0:T(8,128)(2,1)S(1)}, bf16[256,896]{1,0:T(8,128)(2,1)S(1)}, u32[]{:S(2)}, u32[]{:S(2)}) collective-permute-start(bf16[256,896]{1,0:T(8,128)(2,1)S(1)} %pad_maximum_fusion.1.refs_4_), channel_id=1, source_target_pairs={{0,144},{128,0},{16,128},{144,16},{1,145},{129,1},{17,129},{145,17... | collective-permute-start | bytes 1376264 | tf_op jit(solution)/shard_map/ppermute | solution.py:24
  93.1 20.2 %collective-permute-start.25 = (bf16[256,896]{1,0:T(8,128)(2,1)S(1)}, bf16[256,896]{1,0:T(8,128)(2,1)S(1)}, u32[]{:S(2)}, u32[]{:S(2)}) collective-permute-start(bf16[256,896]{1,0:T(8,128)(2,1)S(1)} %pad_maximum_fusion.1.refs_4_), channel_id=1, source_target_pairs={{0,16},{128,144},{16,0},{144,128},{1,17},{129,145},{17,1},{145,129... | collective-permute-start | bytes 1376264 | tf_op jit(solution)/shard_map/ppermute | solution.py:24
  98.8 14.5 %collective-permute-start.24 = (bf16[256,896]{1,0:T(8,128)(2,1)S(1)}, bf16[256,896]{1,0:T(8,128)(2,1)S(1)}, u32[]{:S(2)}, u32[]{:S(2)}) collective-permute-start(bf16[256,896]{1,0:T(8,128)(2,1)S(1)} %pad_maximum_fusion.1.refs_4_), channel_id=1, source_target_pairs={{0,128},{128,16},{16,144},{144,0},{1,129},{129,17},{17,145},{145,1... | collective-permute-start | bytes 1376264 | tf_op jit(solution)/shard_map/ppermute | solution.py:24
  101.0 22.2 %collective-permute-start.35 = (f32[3,4,1792]{2,1,0:T(4,128)S(1)}, f32[3,4,1792]{2,1,0:T(4,128)S(1)}, u32[]{:S(2)}, u32[]{:S(2)}) collective-permute-start(f32[3,4,1792]{2,1,0:T(4,128)S(1)} %get-tuple-element.119), channel_id=1, source_target_pairs={{0,1},{1,0},{2,3},{3,2},{4,5},{5,4},{6,7},{7,6},{8,9},{9,8},{10,11... | collective-permute-start | bytes 258056 | tf_op jit(solution)/shard_map/ppermute | solution.py:210
  113.3 10.8 %collective-permute-start.27 = (bf16[256,896]{1,0:T(8,128)(2,1)S(1)}, bf16[256,896]{1,0:T(8,128)(2,1)S(1)}, u32[]{:S(2)}, u32[]{:S(2)}) collective-permute-start(bf16[256,896]{1,0:T(8,128)(2,1)S(1)} %pad_maximum_fusion.refs_0_), channel_id=1, source_target_pairs={{0,1},{1,0},{2,3},{3,2},{4,5},{5,4},{6,7},{7,6},{8,9},{9,8},{10,11... | collective-permute-start | bytes 1376264 | tf_op jit(solution)/shard_map/ppermute | solution.py:226
  123.3 5.8 %collective-permute-start.30 = (bf16[256,896]{1,0:T(8,128)(2,1)S(1)}, bf16[256,896]{1,0:T(8,128)(2,1)S(1)}, u32[]{:S(2)}, u32[]{:S(2)}) collective-permute-start(bf16[256,896]{1,0:T(8,128)(2,1)S(1)} %collective-permute-done.23.refs_3_), channel_id=1, source_target_pairs={{0,1},{1,0},{2,3},{3,2},{4,5},{5,4},{6,7},{7,6},{8,9},{9,8},{10,11... | collective-permute-start | bytes 1376264 | tf_op jit(solution)/shard_map/ppermute | solution.py:226
  123.4 5.7 %collective-permute-start.31 = (bf16[256,896]{1,0:T(8,128)(2,1)S(1)}, bf16[256,896]{1,0:T(8,128)(2,1)S(1)}, u32[]{:S(2)}, u32[]{:S(2)}) collective-permute-start(bf16[256,896]{1,0:T(8,128)(2,1)S(1)} %pad_maximum_fusion.1.refs_4_), channel_id=1, source_target_pairs={{0,1},{1,0},{2,3},{3,2},{4,5},{5,4},{6,7},{7,6},{8,9},{9,8},{10,11... | collective-permute-start | bytes 1376264 | tf_op jit(solution)/shard_map/ppermute | solution.py:226
  124.1 5.0 %collective-permute-start.32 = (bf16[256,896]{1,0:T(8,128)(2,1)S(1)}, bf16[256,896]{1,0:T(8,128)(2,1)S(1)}, u32[]{:S(2)}, u32[]{:S(2)}) collective-permute-start(bf16[256,896]{1,0:T(8,128)(2,1)S(1)} %collective-permute-done.24.refs_5_), channel_id=1, source_target_pairs={{0,1},{1,0},{2,3},{3,2},{4,5},{5,4},{6,7},{7,6},{8,9},{9,8},{10,11... | collective-permute-start | bytes 1376264 | tf_op jit(solution)/shard_map/ppermute | solution.py:226
  124.8 4.4 %collective-permute-start.33 = (bf16[256,896]{1,0:T(8,128)(2,1)S(1)}, bf16[256,896]{1,0:T(8,128)(2,1)S(1)}, u32[]{:S(2)}, u32[]{:S(2)}) collective-permute-start(bf16[256,896]{1,0:T(8,128)(2,1)S(1)} %collective-permute-done.25.refs_6_), channel_id=1, source_target_pairs={{0,1},{1,0},{2,3},{3,2},{4,5},{5,4},{6,7},{7,6},{8,9},{9,8},{10,11... | collective-permute-start | bytes 1376264 | tf_op jit(solution)/shard_map/ppermute | solution.py:226
  (12 other events, 42.7 us)

commit v4 on v1

v4 whole, which is shorter than its diff:
```python
import functools

import jax
import jax.numpy as jnp
from jax import lax
from jax.experimental import pallas as pl
from jax.experimental.pallas import tpu as pltpu
from jax.sharding import Mesh, PartitionSpec as P

STEP = 10

SIZES = (2, 4, 2, 8, 2)
NAMES = ("xlo", "y", "xhi", "z", "core")
N = 4
N_Z = 8
BLOCK = 64
SWAP = [(0, 1), (1, 0)]
VMEM = 40 * 1024 * 1024


def in_plane(value, shift, first_axis):
    def index(x, y, core):
        return (((x % 2) * N + y) * 2 + x // 2) * 2 + core

    pairs = []
    for x in range(N):
        for y in range(N):
            for core in range(2):
                if (core == 0) == first_axis:
                    there = index(x, (y + shift) % N, core)
                else:
                    there = index((x + shift) % N, y, core)
                pairs.append((index(x, y, core), there))
    return lax.ppermute(value, ("xlo", "y", "xhi", "core"), pairs)


def far(value, shift):
    return in_plane(value, shift, True)


def near(value, shift):
    return in_plane(value, shift, False)


def swap(value):
    return lax.ppermute(value, "core", SWAP)


def block_row(here, core, far_step, near_step):
    dx = near_step + core * (far_step - near_step)
    dy = far_step + core * (near_step - far_step)
    x, y = (here[0] + dx) % N, (here[1] + dy) % N
    return pl.multiple_of(((x % 2) * 8 + y * 2 + x // 2) * BLOCK, BLOCK)


def terms_kernel(here, hidden, hidden_peer, scaled, scaled_peer, *refs):
    outs, turned = refs[:-1], refs[-1]
    tokens = hidden.shape[0]
    turned[:, :tokens] = hidden[...].T
    turned[:, tokens:] = hidden_peer[...].T
    columns = jnp.concatenate([scaled[...], scaled_peer[...]], 0)
    for f in range(N):
        rows = [turned[pl.ds(block_row(here, here[2], f, n), BLOCK), :] for n in range(N)]
        outs[f][...] = jnp.dot(
            jnp.concatenate(rows, 0), columns, preferred_element_type=jnp.float32
        ).astype(jnp.bfloat16)


def terms(here, hidden, hidden_peer, scaled, scaled_peer):
    tokens, width = scaled.shape
    whole = pl.BlockSpec(memory_space=pltpu.VMEM)
    return pl.pallas_call(
        terms_kernel,
        out_shape=[jax.ShapeDtypeStruct((N * BLOCK, width), jnp.bfloat16)] * N,
        in_specs=[pl.BlockSpec(memory_space=pltpu.SMEM)] + [whole] * 4,
        out_specs=[whole] * N,
        scratch_shapes=[pltpu.VMEM((hidden.shape[1], 2 * tokens), jnp.bfloat16)],
        compiler_params=pltpu.CompilerParams(vmem_limit_bytes=VMEM),
        cost_estimate=pl.CostEstimate(
            flops=2 * 2 * tokens * hidden.shape[1] * width,
            bytes_accessed=5_000_000,
            transcendentals=0,
        ),
    )(here, hidden, hidden_peer, scaled, scaled_peer)


def join_kernel(plan, here, *refs):
    pieces, out, sems = refs[: len(plan)], refs[-2], refs[-1]
    width = pieces[0].shape[1]
    copies = []
    for piece, (shift, begin, theirs) in zip(pieces, plan):
        core = 1 - here[2] if theirs else here[2]
        for n in range(piece.shape[0] // BLOCK):
            copy = pltpu.make_async_copy(
                piece.at[pl.ds(n * BLOCK, BLOCK), :],
                out.at[
                    pl.ds(block_row(here, core, N - shift, N - begin - n), BLOCK),
                    pl.ds(pl.multiple_of(core * width, 128), width),
                ],
                sems.at[len(copies)],
            )
            copy.start()
            copies.append(copy)
    for copy in copies:
        copy.wait()


def join(here, items, out=None):
    pieces = [item[0] for item in items]
    width = pieces[0].shape[1]
    blocks = sum(piece.shape[0] for piece in pieces) // BLOCK
    anywhere = pl.BlockSpec(memory_space=pl.ANY)
    begun = [] if out is None else [out]
    return pl.pallas_call(
        functools.partial(join_kernel, tuple(item[1:] for item in items)),
        out_shape=jax.ShapeDtypeStruct((N * N * BLOCK, 2 * width), jnp.bfloat16),
        in_specs=[pl.BlockSpec(memory_space=pltpu.SMEM)]
        + [pl.BlockSpec(memory_space=pltpu.VMEM)] * len(pieces)
        + [anywhere] * len(begun),
        out_specs=anywhere,
        scratch_shapes=[pltpu.SemaphoreType.DMA((blocks,))],
        input_output_aliases={len(pieces) + 1: 0} if begun else {},
        compiler_params=pltpu.CompilerParams(vmem_limit_bytes=VMEM),
        cost_estimate=pl.CostEstimate(
            flops=0, bytes_accessed=4 * blocks * BLOCK * width, transcendentals=0
        ),
    )(here, *pieces, *begun)


def together(*values):
    return lax.optimization_barrier(values)


def after(value, earlier):
    return lax.optimization_barrier((value, earlier))[0]


def total(parts):
    return functools.reduce(lambda a, b: a + b, [part.astype(jnp.float32) for part in parts])


def shards(gate_pre, up_pre, out_grad, route_weight, row_token, master, moment, second):
    core = lax.axis_index("core")
    first_core = core == 0
    here = jnp.stack([2 * lax.axis_index("xhi") + lax.axis_index("xlo"), lax.axis_index("y"), core])
    here = here.astype(jnp.int32)
    half = out_grad.shape[1] // 2

    def mine_and_theirs(whole):
        left, right = whole[..., :half], whole[..., half:]
        return jnp.where(first_core, left, right), jnp.where(first_core, right, left)

    def in_core_order(own, peer, axis):
        return jnp.where(
            first_core,
            jnp.concatenate([own, peer], axis),
            jnp.concatenate([peer, own], axis),
        )

    state = jnp.stack([master, moment, second])
    state_mine, state_theirs = mine_and_theirs(state)

    hidden = (jax.nn.silu(gate_pre.astype(jnp.float32)) * up_pre.astype(jnp.float32)).astype(
        jnp.bfloat16
    )
    named = row_token[:, None] == jnp.arange(out_grad.shape[0], dtype=jnp.int32)[None, :]
    picked = jnp.dot(named.astype(jnp.bfloat16), out_grad, preferred_element_type=jnp.float32)
    scaled = (picked * route_weight[:, None]).astype(jnp.bfloat16)
    scaled_mine, scaled_theirs = mine_and_theirs(scaled)

    blocks = terms(here, hidden, swap(hidden), scaled_mine, swap(scaled_theirs))
    *parts, state_peer = together(*[far(blocks[s], s) for s in (2, 1, 3)], swap(state_theirs))
    parts = [blocks[0], *parts]
    state_chip = in_core_order(state_mine, state_peer, 1)
    sums = [total([part[s * BLOCK : (s + 1) * BLOCK] for part in parts]) for s in range(N)]
    sums = together(sums[0], *[sums[s].astype(jnp.bfloat16) for s in (2, 1, 3)])
    parts = [sums[0], *together(*[near(value, s) for value, s in zip(sums[1:], (2, 1, 3))])]
    plane_sum = total(parts).astype(jnp.bfloat16)
    parts = lax.all_to_all(plane_sum.reshape(N_Z, BLOCK // N_Z, half), "z", 0, 0)
    grad = jnp.sum(parts.astype(jnp.float32), 0)

    new_moment = 0.9 * state_chip[1] + 0.1 * grad
    new_second = 0.95 * state_chip[2] + 0.05 * grad * grad
    first_hat = new_moment / (1.0 - 0.9**STEP)
    second_hat = new_second / (1.0 - 0.95**STEP)
    new_master = state_chip[0] - 0.001 * (
        first_hat / (jnp.sqrt(second_hat) + 1e-08) + 0.1 * state_chip[0]
    )
    piece = new_master.astype(jnp.bfloat16)

    new_state = jnp.stack([new_master, new_moment, new_second])
    top, bottom = new_state[:, : master.shape[0]], new_state[:, master.shape[0] :]
    state_own = jnp.where(first_core, top, bottom)
    state_out = in_core_order(state_own, swap(jnp.where(first_core, bottom, top)), 2)

    column = lax.all_to_all(jnp.broadcast_to(piece, (N_Z,) + piece.shape), "z", 0, 0)
    column = together(column.reshape(BLOCK, half))[0]
    parts = together(*[near(column, s) for s in (1, 2, 3)])
    (plane,) = together(jnp.concatenate([column, *parts], 0))
    one, three, peer, *state_out = together(
        far(plane, 1), far(plane, 3), swap(plane), *[state_out[k] for k in range(3)]
    )
    middle = plane.shape[0] // 2
    two_a, two_b, one_peer, three_peer, weight = together(
        far(one[:middle], 1),
        far(three[middle:], 3),
        swap(one),
        swap(three),
        join(here, [(plane, 0, 0, 0), (one, 1, 0, 0), (three, 3, 0, 0), (peer, 0, 0, 1)]),
    )
    items = [(two_a, 2, 0, 0), (two_b, 2, 2, 0), (one_peer, 1, 0, 1), (three_peer, 3, 0, 1)]
    items += [(swap(two_a), 2, 0, 1), (swap(two_b), 2, 2, 1)]
    weight = join(here, items, weight)
    return (weight, state_out[0], state_out[1], state_out[2])


def solution(mesh):
    grid = Mesh(mesh.devices.reshape(SIZES), NAMES)
    rows = P(NAMES, None)
    in_specs = (rows, rows, rows, P(NAMES), P(NAMES), rows, rows, rows)
    out_specs = (P(), rows, rows, rows)
    return jax.shard_map(shards, mesh=grid, in_specs=in_specs, out_specs=out_specs, check_vma=False)
```

time: 172 us -> 125 us (0.73)
  blocking collectives: 59.4 us -> 0 us
  starting transfers between devices: 24.5 us -> 46 us
  waiting for transfers between devices: 72.9 us -> 64.7 us
  Pallas kernels: 0 us -> 6.86 us
  other arithmetic: 8.79 us -> 2 us
  matrix products: 3.01 us -> 1.17 us
    all_to_all x2 -> x0, blocking collectives: 59.4 us -> none  [the longest x1 47.8 us: shards(): lax.all_to_all(jnp.broadcast_to(along_z, (N_PLANE,) + along_z.shape), PLA...]
    all_to_all x2, waiting for transfers between devices: 64.5 us -> 17.8 us  [the longest x1 8.95 us: shards(): lax.all_to_all(plane_sum.reshape(N_Z, BLOCK // N_Z, half), 'z', 0, 0)]
    ppermute x5 -> x22, waiting for transfers between devices: 8.37 us -> 46.9 us  [the longest x13 42.5 us: in_plane(): return lax.ppermute(value, ('xlo', 'y', 'xhi', 'core'), pairs)]
    ppermute x5 -> x22, starting transfers between devices: 11.3 us -> 35.6 us  [the longest x9 21.8 us: swap(): return lax.ppermute(value, 'core', SWAP)]
    pallas_call x0 -> x3, Pallas kernels: none -> 6.86 us  [the longest x2 5.04 us: join(): pl.pallas_call(functools.partial(join_kernel, tuple((item[1:] for item in...]
    select_n x3 -> x2, other arithmetic: 4.01 us -> 0.11 us  [in_core_order(): jnp.where(first_core, jnp.concatenate([own, peer], axis), jnp.concatenate...]
    reduce_sum x2 -> x1, other arithmetic: 3.33 us -> 0.03 us  [shards(): grad = jnp.sum(parts.astype(jnp.float32), 0)]
    all_to_all x2, starting transfers between devices: 13.2 us -> 10.3 us  [the longest x1 6.92 us: shards(): lax.all_to_all(plane_sum.reshape(N_Z, BLOCK // N_Z, half), 'z', 0, 0)]
  transfers between devices with their start and end apart: 7 -> 24, of which waited for: 5 -> 15; matrix products, arithmetic and copies ran while one was open for 1% -> 1% of each run, Pallas kernels for 0% -> 2%
where the time goes in v4:
time: 125 us; the launch traced here: 124 us
  waiting for transfers between devices  64.7 us (52%)
  starting transfers between devices  46 us (37%)
  Pallas kernels  6.86 us (5%)
  local copies, waits for them, and re-layouts  2.63 us (2%)
  other arithmetic  2 us (2%)
    ppermute x13, waiting for transfers between devices, in_plane(): return lax.ppermute(value, ('xlo', 'y', 'xhi', 'core'), pairs)  42.5 us
    ppermute x9, starting transfers between devices, swap(): return lax.ppermute(value, 'core', SWAP)  21.8 us
    ppermute x13, starting transfers between devices, in_plane(): return lax.ppermute(value, ('xlo', 'y', 'xhi', 'core'), pairs)  13.8 us
    all_to_all x1, waiting for transfers between devices, shards(): lax.all_to_all(plane_sum.reshape(N_Z, BLOCK // N_Z, half), 'z', 0, 0)  8.95 us
    all_to_all x1, waiting for transfers between devices, shards(): lax.all_to_all(jnp.broadcast_to(piece, (N_Z,) + piece.shape), 'z', 0, 0)  8.84 us
    all_to_all x1, starting transfers between devices, shards(): lax.all_to_all(plane_sum.reshape(N_Z, BLOCK // N_Z, half), 'z', 0, 0)  6.92 us
    pallas_call x2, Pallas kernels, join(): pl.pallas_call(functools.partial(join_kernel, tuple((item[1:] for item in...  5.04 us
    ppermute x9, waiting for transfers between devices, swap(): return lax.ppermute(value, 'core', SWAP)  4.37 us
  transfers between devices with their start and end apart: 24, of which 15 were waited for; matrix products, arithmetic and copies ran while one was open for 1% of the time, Pallas kernels for 2%

profile of v4, /device:TPU:1, one launch (start us, length us, event | category | flops | bytes accessed | tf_op | source)
XLA Modules:
  0.0 124.3 jit_solution(14227286072382138671)
XLA Ops:
  0.7 1.2 copy-done
  1.8 1.2 fusion
  3.1 3.3 %collective-permute-start.1 = (bf16[128,1792]{1,0:T(8,128)(2,1)S(1)}, bf16[128,1792]{1,0:T(8,128)(2,1)S(1)}, u32[]{:S(2)}, u32[]{:S(2)}) collective-permute-start(bf16[128,1792]{1,0:T(8,128)(2,1)S(1)} %get-tuple-element.69), channel_id=1, source_target_pairs={{0,1},{1,0},{2,3},{3,2},{4,5},{5,4},{6,7},{7,6},{8,9},{9,8},{10,11... | collective-permute-start | bytes 1376264 | tf_op jit(solution)/shard_map/ppermute | solution.py:46
  6.8 1.4 %collective-permute-done.hidden_peer = bf16[128,1024]{1,0:T(8,128)(2,1)S(1)} collective-permute-done((bf16[128,1024]{1,0:T(8,128)(2,1)S(1)}, bf16[128,1024]{1,0:T(8,128)(2,1)S(1)}, u32[]{:S(2)}, u32[]{:S(2)}) %collective-permute-start) | collective-permute-done | bytes 262176 | tf_op jit(solution)/shard_map/ppermute | solution.py:46
  8.2 1.8 %shard_map.111 = (bf16[256,1792]{1,0:T(8,128)(2,1)S(1)}, bf16[256,1792]{1,0:T(8,128)(2,1)S(1)}, bf16[256,1792]{1,0:T(8,128)(2,1)S(1)}, bf16[256,1792]{1,0:T(8,128)(2,1)S(1)}) custom-call(s32[3]{0:T(128)S(1)} %pad_add_fusion.here, bf16[128,1024]{1,0:T(8,128)(2,1)S(1)} %fusion.5.hidden, bf16[128,1024]{1,0:T(8,128)(2,1)S(1)} %collective-permute-done.hidden_peer, ...), custom_call_target="tpu_custom_call" | custom-call | flops 939524096 | bytes 5000000 | tf_op jit(solution)/shard_map/pallas_call | solution.py:72
  10.1 1.1 collective-permute-start.2
  11.5 2.4 %collective-permute-start.4 = (bf16[256,1792]{1,0:T(8,128)(2,1)S(1)}, bf16[256,1792]{1,0:T(8,128)(2,1)S(1)}, u32[]{:S(2)}, u32[]{:S(2)}) collective-permute-start(bf16[256,1792]{1,0:T(8,128)(2,1)S(1)} %get-tuple-element.35), channel_id=1, source_target_pairs={{0,96},{1,145},{32,0},{33,177},{64,32},{65,209},{96,64},{97,241},{... | collective-permute-start | bytes 2752520 | tf_op jit(solution)/shard_map/ppermute | solution.py:34
  13.9 1.5 %collective-permute-start.5 = (f32[3,4,1792]{2,1,0:T(4,128)S(1)}, f32[3,4,1792]{2,1,0:T(4,128)S(1)}, u32[]{:S(2)}, u32[]{:S(2)}) collective-permute-start(f32[3,4,1792]{2,1,0:T(4,128)S(1)} %get-tuple-element.77), channel_id=1, source_target_pairs={{0,1},{1,0},{2,3},{3,2},{4,5},{5,4},{6,7},{7,6},{8,9},{9,8},{10,11... | collective-permute-start | bytes 258056 | tf_op jit(solution)/shard_map/ppermute | solution.py:46
  16.3 7.9 %collective-permute-done.2 = bf16[256,1792]{1,0:T(8,128)(2,1)S(1)} collective-permute-done((bf16[256,1792]{1,0:T(8,128)(2,1)S(1)}, bf16[256,1792]{1,0:T(8,128)(2,1)S(1)}, u32[]{:S(2)}, u32[]{:S(2)}) %collective-permute-start.2) | collective-permute-done | bytes 917536 | tf_op jit(solution)/shard_map/ppermute | solution.py:34
  24.2 9.8 %collective-permute-done.3 = bf16[256,1792]{1,0:T(8,128)(2,1)S(1)} collective-permute-done((bf16[256,1792]{1,0:T(8,128)(2,1)S(1)}, bf16[256,1792]{1,0:T(8,128)(2,1)S(1)}, u32[]{:S(2)}, u32[]{:S(2)}) %collective-permute-start.3) | collective-permute-done | bytes 917536 | tf_op jit(solution)/shard_map/ppermute | solution.py:34
  34.5 1.4 %collective-permute-start.6 = (bf16[64,1792]{1,0:T(8,128)(2,1)S(1)}, bf16[64,1792]{1,0:T(8,128)(2,1)S(1)}, u32[]{:S(2)}, u32[]{:S(2)}) collective-permute-start(bf16[64,1792]{1,0:T(8,128)(2,1)S(1)} %get-tuple-element.42), channel_id=1, source_target_pairs={{0,16},{1,65},{32,48},{33,97},{64,80},{65,1},{96,112},{97,33},{128... | collective-permute-start | bytes 688136 | tf_op jit(solution)/shard_map/ppermute | solution.py:34
  36.3 2.3 %collective-permute-start.8 = (bf16[64,1792]{1,0:T(8,128)(2,1)S(1)}, bf16[64,1792]{1,0:T(8,128)(2,1)S(1)}, u32[]{:S(2)}, u32[]{:S(2)}) collective-permute-start(bf16[64,1792]{1,0:T(8,128)(2,1)S(1)} %get-tuple-element.44), channel_id=1, source_target_pairs={{0,144},{1,97},{32,176},{33,1},{64,208},{65,33},{96,240},{97,65},{... | collective-permute-start | bytes 688136 | tf_op jit(solution)/shard_map/ppermute | solution.py:34
  38.6 2.7 %collective-permute-done.6 = bf16[64,1792]{1,0:T(8,128)(2,1)S(1)} collective-permute-done((bf16[64,1792]{1,0:T(8,128)(2,1)S(1)}, bf16[64,1792]{1,0:T(8,128)(2,1)S(1)}, u32[]{:S(2)}, u32[]{:S(2)}) %collective-permute-start.6) | collective-permute-done | bytes 229408 | tf_op jit(solution)/shard_map/ppermute | solution.py:34
  41.2 2.5 %collective-permute-done.7 = bf16[64,1792]{1,0:T(8,128)(2,1)S(1)} collective-permute-done((bf16[64,1792]{1,0:T(8,128)(2,1)S(1)}, bf16[64,1792]{1,0:T(8,128)(2,1)S(1)}, u32[]{:S(2)}, u32[]{:S(2)}) %collective-permute-start.7) | collective-permute-done | bytes 229408 | tf_op jit(solution)/shard_map/ppermute | solution.py:34
  44.5 6.9 %all-to-all-start = ((bf16[8,8,1792]{2,1,0:T(8,128)(2,1)}), bf16[8,8,1792]{2,1,0:T(8,128)(2,1)S(1)}, u32[]{:S(2)}, u32[]{:S(2)}) async-start(bf16[8,8,1792]{2,1,0:T(8,128)(2,1)} %fusion.6), calls=%async_computation | async-start | bytes 458752 | tf_op jit(solution)/shard_map/all_to_all | solution.py:179
  51.5 9.0 %all-to-all-done = bf16[8,8,1792]{2,1,0:T(8,128)(2,1)S(1)} async-done(((bf16[8,8,1792]{2,1,0:T(8,128)(2,1)}), bf16[8,8,1792]{2,1,0:T(8,128)(2,1)S(1)}, u32[]{:S(2)}, u32[]{:S(2)}) %all-to-all-start) | async-done | bytes 229408 | tf_op jit(solution)/shard_map/all_to_all | solution.py:179
  61.2 3.4 %all-to-all-start.1 = ((bf16[8,8,1792]{2,1,0:T(8,128)(2,1)}), bf16[8,8,1792]{2,1,0:T(8,128)(2,1)S(1)}, u32[]{:S(2)}, u32[]{:S(2)}) async-start(bf16[8,8,1792]{2,1,0:T(8,128)(2,1)} %broadcast_in_dim.2), calls=%async_computation.1 | async-start | bytes 458752 | tf_op jit(solution)/shard_map/all_to_all | solution.py:196
  64.7 8.8 %all-to-all-done.1 = bf16[8,8,1792]{2,1,0:T(8,128)(2,1)S(1)} async-done(((bf16[8,8,1792]{2,1,0:T(8,128)(2,1)}), bf16[8,8,1792]{2,1,0:T(8,128)(2,1)S(1)}, u32[]{:S(2)}, u32[]{:S(2)}) %all-to-all-start.1) | async-done | bytes 229408 | tf_op jit(solution)/shard_map/all_to_all | solution.py:196
  73.6 2.4 %collective-permute-start.11 = (bf16[64,1792]{1,0:T(8,128)(2,1)S(1)}, bf16[64,1792]{1,0:T(8,128)(2,1)S(1)}, u32[]{:S(2)}, u32[]{:S(2)}) collective-permute-start(bf16[64,1792]{1,0:T(8,128)(2,1)S(1)} %bitcast.44), channel_id=1, source_target_pairs={{0,144},{1,97},{32,176},{33,1},{64,208},{65,33},{96,240},{97,65},{... | collective-permute-start | bytes 688136 | tf_op jit(solution)/shard_map/ppermute | solution.py:34
  76.6 5.9 %collective-permute-start.15 = (f32[3,4,1792]{2,1,0:T(4,128)S(1)}, f32[3,4,1792]{2,1,0:T(4,128)S(1)}, u32[]{:S(2)}, u32[]{:S(2)}) collective-permute-start(f32[3,4,1792]{2,1,0:T(4,128)S(1)} %get-tuple-element.75), channel_id=1, source_target_pairs={{0,1},{1,0},{2,3},{3,2},{4,5},{5,4},{6,7},{7,6},{8,9},{9,8},{10,11... | collective-permute-start | bytes 258056 | tf_op jit(solution)/shard_map/ppermute | solution.py:46
  82.6 2.3 %collective-permute-done.9 = bf16[64,1792]{1,0:T(8,128)(2,1)S(1)} collective-permute-done((bf16[64,1792]{1,0:T(8,128)(2,1)S(1)}, bf16[64,1792]{1,0:T(8,128)(2,1)S(1)}, u32[]{:S(2)}, u32[]{:S(2)}) %collective-permute-start.9) | collective-permute-done | bytes 229408 | tf_op jit(solution)/shard_map/ppermute | solution.py:34
  84.9 6.8 %collective-permute-start.14 = (bf16[256,1792]{1,0:T(8,128)(2,1)S(1)}, bf16[256,1792]{1,0:T(8,128)(2,1)S(1)}, u32[]{:S(2)}, u32[]{:S(2)}) collective-permute-start(bf16[256,1792]{1,0:T(8,128)(2,1)S(1)} %pad_maximum_fusion.refs_0_), channel_id=1, source_target_pairs={{0,1},{1,0},{2,3},{3,2},{4,5},{5,4},{6,7},{7,6},{8,9},{9,8},{10,11... | collective-permute-start | bytes 2752520 | tf_op jit(solution)/shard_map/ppermute | solution.py:46
  92.2 1.0 collective-permute-start.12
  93.9 10.4 %collective-permute-done.13.refs_2_ = bf16[256,1792]{1,0:T(8,128)(2,1)S(1)} collective-permute-done((bf16[256,1792]{1,0:T(8,128)(2,1)S(1)}, bf16[256,1792]{1,0:T(8,128)(2,1)S(1)}, u32[]{:S(2)}, u32[]{:S(2)}) %collective-permute-start.13) | collective-permute-done | bytes 917536 | tf_op jit(solution)/shard_map/ppermute | solution.py:34
  104.3 1.7 %collective-permute-done.12.refs_1_ = bf16[256,1792]{1,0:T(8,128)(2,1)S(1)} collective-permute-done((bf16[256,1792]{1,0:T(8,128)(2,1)S(1)}, bf16[256,1792]{1,0:T(8,128)(2,1)S(1)}, u32[]{:S(2)}, u32[]{:S(2)}) %collective-permute-start.12) | collective-permute-done | bytes 917536 | tf_op jit(solution)/shard_map/ppermute | solution.py:34
  106.0 3.1 %collective-permute-start.18 = (bf16[256,1792]{1,0:T(8,128)(2,1)S(1)}, bf16[256,1792]{1,0:T(8,128)(2,1)S(1)}, u32[]{:S(2)}, u32[]{:S(2)}) collective-permute-start(bf16[256,1792]{1,0:T(8,128)(2,1)S(1)} %collective-permute-done.12.refs_1_), channel_id=1, source_target_pairs={{0,1},{1,0},{2,3},{3,2},{4,5},{5,4},{6,7},{7,6},{8,9},{9,8},{10,11... | collective-permute-start | bytes 2752520 | tf_op jit(solution)/shard_map/ppermute | solution.py:46
  109.7 1.0 collective-permute-start.16
  110.7 2.5 %shard_map.112.refs_6_ = bf16[1024,3584]{1,0:T(8,128)(2,1)} custom-call(s32[3]{0:T(128)S(1)} %pad_add_fusion.here, bf16[256,1792]{1,0:T(8,128)(2,1)S(1)} %pad_maximum_fusion.refs_0_, bf16[256,1792]{1,0:T(8,128)(2,1)S(1)} %collective-permute-done.12.refs_1_, bf16[256,1792]{1,0:T(8,128)(2,1)S(1)} %collective-permute-done.13.refs_2_, ...), custom_call_target="tpu_custom_call" | custom-call | bytes 7340032 | tf_op jit(solution)/shard_map/pallas_call | solution.py:114
  113.2 3.6 %collective-permute-done.17.refs_1_ = bf16[128,1792]{1,0:T(8,128)(2,1)S(1)} collective-permute-done((bf16[128,1792]{1,0:T(8,128)(2,1)S(1)}, bf16[128,1792]{1,0:T(8,128)(2,1)S(1)}, u32[]{:S(2)}, u32[]{:S(2)}) %collective-permute-start.17) | collective-permute-done | bytes 458784 | tf_op jit(solution)/shard_map/ppermute | solution.py:34
  116.8 1.7 %collective-permute-done.16.refs_0_ = bf16[128,1792]{1,0:T(8,128)(2,1)S(1)} collective-permute-done((bf16[128,1792]{1,0:T(8,128)(2,1)S(1)}, bf16[128,1792]{1,0:T(8,128)(2,1)S(1)}, u32[]{:S(2)}, u32[]{:S(2)}) %collective-permute-start.16) | collective-permute-done | bytes 458784 | tf_op jit(solution)/shard_map/ppermute | solution.py:34
  119.6 1.3 %collective-permute-done.20.refs_4_ = bf16[128,1792]{1,0:T(8,128)(2,1)S(1)} collective-permute-done((bf16[128,1792]{1,0:T(8,128)(2,1)S(1)}, bf16[128,1792]{1,0:T(8,128)(2,1)S(1)}, u32[]{:S(2)}, u32[]{:S(2)}) %collective-permute-start.20) | collective-permute-done | bytes 458784 | tf_op jit(solution)/shard_map/ppermute | solution.py:46
  121.6 2.5 %shard_map.113 = bf16[1024,3584]{1,0:T(8,128)(2,1)} custom-call(s32[3]{0:T(128)S(1)} %pad_add_fusion.here, bf16[128,1792]{1,0:T(8,128)(2,1)S(1)} %collective-permute-done.16.refs_0_, bf16[128,1792]{1,0:T(8,128)(2,1)S(1)} %collective-permute-done.17.refs_1_, bf16[256,1792]{1,0:T(8,128)(2,1)S(1)} %collective-permute-done.18.refs_2_, ...), custom_call_target="tpu_custom_call", output_to_operand_aliasing={{}: (7, {})} | custom-call | bytes 7340032 | tf_op jit(solution)/shard_map/pallas_call | solution.py:114
  (51 shorter events, 8.6 us)
Async XLA Ops:
  0.6 1.2 copy-start
  1.8 4.6 %copy-start.1 = (bf16[128,1024]{1,0:T(8,128)(2,1)S(1)}, bf16[128,1024]{1,0:T(8,128)(2,1)}, u32[]{:S(2)}) copy-start(bf16[128,1024]{1,0:T(8,128)(2,1)} %param.9) | copy-start | bytes 786436
  1.8 4.6 %copy-start.2 = (bf16[128,1024]{1,0:T(8,128)(2,1)S(1)}, bf16[128,1024]{1,0:T(8,128)(2,1)}, u32[]{:S(2)}) copy-start(bf16[128,1024]{1,0:T(8,128)(2,1)} %param.8) | copy-start | bytes 786436
  3.1 5.2 %collective-permute-start.1 = (bf16[128,1792]{1,0:T(8,128)(2,1)S(1)}, bf16[128,1792]{1,0:T(8,128)(2,1)S(1)}, u32[]{:S(2)}, u32[]{:S(2)}) collective-permute-start(bf16[128,1792]{1,0:T(8,128)(2,1)S(1)} %get-tuple-element.69), channel_id=1, source_target_pairs={{0,1},{1,0},{2,3},{3,2},{4,5},{5,4},{6,7},{7,6},{8,9},{9,8},{10,11... | collective-permute-start | bytes 1376264 | tf_op jit(solution)/shard_map/ppermute | solution.py:46
  6.6 7.3 %copy-start.3 = (f32[4,3584]{1,0:T(4,128)S(1)}, f32[4,3584]{1,0:T(4,128)}, u32[]{:S(2)}) copy-start(f32[4,3584]{1,0:T(4,128)} %param.15) | copy-start | bytes 172036
  6.6 7.3 %copy-start.4 = (f32[4,3584]{1,0:T(4,128)S(1)}, f32[4,3584]{1,0:T(4,128)}, u32[]{:S(2)}) copy-start(f32[4,3584]{1,0:T(4,128)} %param.14) | copy-start | bytes 172036
  6.6 7.3 %copy-start.5 = (f32[4,3584]{1,0:T(4,128)S(1)}, f32[4,3584]{1,0:T(4,128)}, u32[]{:S(2)}) copy-start(f32[4,3584]{1,0:T(4,128)} %param.13) | copy-start | bytes 172036
  6.6 1.6 %collective-permute-start = (bf16[128,1024]{1,0:T(8,128)(2,1)S(1)}, bf16[128,1024]{1,0:T(8,128)(2,1)S(1)}, u32[]{:S(2)}, u32[]{:S(2)}) collective-permute-start(bf16[128,1024]{1,0:T(8,128)(2,1)S(1)} %fusion.5.hidden), channel_id=1, source_target_pairs={{0,1},{1,0},{2,3},{3,2},{4,5},{5,4},{6,7},{7,6},{8,9},{9,8},{10,11... | collective-permute-start | bytes 786440 | tf_op jit(solution)/shard_map/ppermute | solution.py:46
  10.1 14.2 %collective-permute-start.2 = (bf16[256,1792]{1,0:T(8,128)(2,1)S(1)}, bf16[256,1792]{1,0:T(8,128)(2,1)S(1)}, u32[]{:S(2)}, u32[]{:S(2)}) collective-permute-start(bf16[256,1792]{1,0:T(8,128)(2,1)S(1)} %get-tuple-element.33), channel_id=1, source_target_pairs={{0,64},{1,17},{32,96},{33,49},{64,0},{65,81},{96,32},{97,113},{128... | collective-permute-start | bytes 2752520 | tf_op jit(solution)/shard_map/ppermute | solution.py:34
  11.2 22.9 %collective-permute-start.3 = (bf16[256,1792]{1,0:T(8,128)(2,1)S(1)}, bf16[256,1792]{1,0:T(8,128)(2,1)S(1)}, u32[]{:S(2)}, u32[]{:S(2)}) collective-permute-start(bf16[256,1792]{1,0:T(8,128)(2,1)S(1)} %get-tuple-element.34), channel_id=1, source_target_pairs={{0,32},{1,129},{32,64},{33,161},{64,96},{65,193},{96,0},{97,225},{... | collective-permute-start | bytes 2752520 | tf_op jit(solution)/shard_map/ppermute | solution.py:34
  11.5 22.6 %collective-permute-start.4 = (bf16[256,1792]{1,0:T(8,128)(2,1)S(1)}, bf16[256,1792]{1,0:T(8,128)(2,1)S(1)}, u32[]{:S(2)}, u32[]{:S(2)}) collective-permute-start(bf16[256,1792]{1,0:T(8,128)(2,1)S(1)} %get-tuple-element.35), channel_id=1, source_target_pairs={{0,96},{1,145},{32,0},{33,177},{64,32},{65,209},{96,64},{97,241},{... | collective-permute-start | bytes 2752520 | tf_op jit(solution)/shard_map/ppermute | solution.py:34
  13.9 2.4 %collective-permute-start.5 = (f32[3,4,1792]{2,1,0:T(4,128)S(1)}, f32[3,4,1792]{2,1,0:T(4,128)S(1)}, u32[]{:S(2)}, u32[]{:S(2)}) collective-permute-start(f32[3,4,1792]{2,1,0:T(4,128)S(1)} %get-tuple-element.77), channel_id=1, source_target_pairs={{0,1},{1,0},{2,3},{3,2},{4,5},{5,4},{6,7},{7,6},{8,9},{9,8},{10,11... | collective-permute-start | bytes 258056 | tf_op jit(solution)/shard_map/ppermute | solution.py:46
  34.5 6.8 %collective-permute-start.6 = (bf16[64,1792]{1,0:T(8,128)(2,1)S(1)}, bf16[64,1792]{1,0:T(8,128)(2,1)S(1)}, u32[]{:S(2)}, u32[]{:S(2)}) collective-permute-start(bf16[64,1792]{1,0:T(8,128)(2,1)S(1)} %get-tuple-element.42), channel_id=1, source_target_pairs={{0,16},{1,65},{32,48},{33,97},{64,80},{65,1},{96,112},{97,33},{128... | collective-permute-start | bytes 688136 | tf_op jit(solution)/shard_map/ppermute | solution.py:34
  35.9 7.8 %collective-permute-start.7 = (bf16[64,1792]{1,0:T(8,128)(2,1)S(1)}, bf16[64,1792]{1,0:T(8,128)(2,1)S(1)}, u32[]{:S(2)}, u32[]{:S(2)}) collective-permute-start(bf16[64,1792]{1,0:T(8,128)(2,1)S(1)} %get-tuple-element.43), channel_id=1, source_target_pairs={{0,128},{1,33},{32,160},{33,65},{64,192},{65,97},{96,224},{97,1},{... | collective-permute-start | bytes 688136 | tf_op jit(solution)/shard_map/ppermute | solution.py:34
  36.3 7.4 %collective-permute-start.8 = (bf16[64,1792]{1,0:T(8,128)(2,1)S(1)}, bf16[64,1792]{1,0:T(8,128)(2,1)S(1)}, u32[]{:S(2)}, u32[]{:S(2)}) collective-permute-start(bf16[64,1792]{1,0:T(8,128)(2,1)S(1)} %get-tuple-element.44), channel_id=1, source_target_pairs={{0,144},{1,97},{32,176},{33,1},{64,208},{65,33},{96,240},{97,65},{... | collective-permute-start | bytes 688136 | tf_op jit(solution)/shard_map/ppermute | solution.py:34
  44.5 15.9 %all-to-all-start = ((bf16[8,8,1792]{2,1,0:T(8,128)(2,1)}), bf16[8,8,1792]{2,1,0:T(8,128)(2,1)S(1)}, u32[]{:S(2)}, u32[]{:S(2)}) async-start(bf16[8,8,1792]{2,1,0:T(8,128)(2,1)} %fusion.6), calls=%async_computation | async-start | bytes 458752 | tf_op jit(solution)/shard_map/all_to_all | solution.py:179
  61.2 12.3 %all-to-all-start.1 = ((bf16[8,8,1792]{2,1,0:T(8,128)(2,1)}), bf16[8,8,1792]{2,1,0:T(8,128)(2,1)S(1)}, u32[]{:S(2)}, u32[]{:S(2)}) async-start(bf16[8,8,1792]{2,1,0:T(8,128)(2,1)} %broadcast_in_dim.2), calls=%async_computation.1 | async-start | bytes 458752 | tf_op jit(solution)/shard_map/all_to_all | solution.py:196
  73.6 9.0 %collective-permute-start.11 = (bf16[64,1792]{1,0:T(8,128)(2,1)S(1)}, bf16[64,1792]{1,0:T(8,128)(2,1)S(1)}, u32[]{:S(2)}, u32[]{:S(2)}) collective-permute-start(bf16[64,1792]{1,0:T(8,128)(2,1)S(1)} %bitcast.44), channel_id=1, source_target_pairs={{0,144},{1,97},{32,176},{33,1},{64,208},{65,33},{96,240},{97,65},{... | collective-permute-start | bytes 688136 | tf_op jit(solution)/shard_map/ppermute | solution.py:34
  76.0 6.6 %collective-permute-start.10 = (bf16[64,1792]{1,0:T(8,128)(2,1)S(1)}, bf16[64,1792]{1,0:T(8,128)(2,1)S(1)}, u32[]{:S(2)}, u32[]{:S(2)}) collective-permute-start(bf16[64,1792]{1,0:T(8,128)(2,1)S(1)} %bitcast.45), channel_id=1, source_target_pairs={{0,16},{1,65},{32,48},{33,97},{64,80},{65,1},{96,112},{97,33},{128... | collective-permute-start | bytes 688136 | tf_op jit(solution)/shard_map/ppermute | solution.py:34
  76.4 8.4 %collective-permute-start.9 = (bf16[64,1792]{1,0:T(8,128)(2,1)S(1)}, bf16[64,1792]{1,0:T(8,128)(2,1)S(1)}, u32[]{:S(2)}, u32[]{:S(2)}) collective-permute-start(bf16[64,1792]{1,0:T(8,128)(2,1)S(1)} %bitcast.46), channel_id=1, source_target_pairs={{0,128},{1,33},{32,160},{33,65},{64,192},{65,97},{96,224},{97,1},{... | collective-permute-start | bytes 688136 | tf_op jit(solution)/shard_map/ppermute | solution.py:34
  76.6 16.6 %collective-permute-start.15 = (f32[3,4,1792]{2,1,0:T(4,128)S(1)}, f32[3,4,1792]{2,1,0:T(4,128)S(1)}, u32[]{:S(2)}, u32[]{:S(2)}) collective-permute-start(f32[3,4,1792]{2,1,0:T(4,128)S(1)} %get-tuple-element.75), channel_id=1, source_target_pairs={{0,1},{1,0},{2,3},{3,2},{4,5},{5,4},{6,7},{7,6},{8,9},{9,8},{10,11... | collective-permute-start | bytes 258056 | tf_op jit(solution)/shard_map/ppermute | solution.py:46
  84.9 9.0 %collective-permute-start.14 = (bf16[256,1792]{1,0:T(8,128)(2,1)S(1)}, bf16[256,1792]{1,0:T(8,128)(2,1)S(1)}, u32[]{:S(2)}, u32[]{:S(2)}) collective-permute-start(bf16[256,1792]{1,0:T(8,128)(2,1)S(1)} %pad_maximum_fusion.refs_0_), channel_id=1, source_target_pairs={{0,1},{1,0},{2,3},{3,2},{4,5},{5,4},{6,7},{7,6},{8,9},{9,8},{10,11... | collective-permute-start | bytes 2752520 | tf_op jit(solution)/shard_map/ppermute | solution.py:46
  91.7 12.5 %collective-permute-start.13 = (bf16[256,1792]{1,0:T(8,128)(2,1)S(1)}, bf16[256,1792]{1,0:T(8,128)(2,1)S(1)}, u32[]{:S(2)}, u32[]{:S(2)}) collective-permute-start(bf16[256,1792]{1,0:T(8,128)(2,1)S(1)} %pad_maximum_fusion.refs_0_), channel_id=1, source_target_pairs={{0,96},{1,145},{32,0},{33,177},{64,32},{65,209},{96,64},{97,241},{... | collective-permute-start | bytes 2752520 | tf_op jit(solution)/shard_map/ppermute | solution.py:34
  92.2 13.8 %collective-permute-start.12 = (bf16[256,1792]{1,0:T(8,128)(2,1)S(1)}, bf16[256,1792]{1,0:T(8,128)(2,1)S(1)}, u32[]{:S(2)}, u32[]{:S(2)}) collective-permute-start(bf16[256,1792]{1,0:T(8,128)(2,1)S(1)} %pad_maximum_fusion.refs_0_), channel_id=1, source_target_pairs={{0,32},{1,129},{32,64},{33,161},{64,96},{65,193},{96,0},{97,225},{... | collective-permute-start | bytes 2752520 | tf_op jit(solution)/shard_map/ppermute | solution.py:34
  106.0 12.6 %collective-permute-start.18 = (bf16[256,1792]{1,0:T(8,128)(2,1)S(1)}, bf16[256,1792]{1,0:T(8,128)(2,1)S(1)}, u32[]{:S(2)}, u32[]{:S(2)}) collective-permute-start(bf16[256,1792]{1,0:T(8,128)(2,1)S(1)} %collective-permute-done.12.refs_1_), channel_id=1, source_target_pairs={{0,1},{1,0},{2,3},{3,2},{4,5},{5,4},{6,7},{7,6},{8,9},{9,8},{10,11... | collective-permute-start | bytes 2752520 | tf_op jit(solution)/shard_map/ppermute | solution.py:46
  109.0 9.5 %collective-permute-start.19 = (bf16[256,1792]{1,0:T(8,128)(2,1)S(1)}, bf16[256,1792]{1,0:T(8,128)(2,1)S(1)}, u32[]{:S(2)}, u32[]{:S(2)}) collective-permute-start(bf16[256,1792]{1,0:T(8,128)(2,1)S(1)} %collective-permute-done.13.refs_2_), channel_id=1, source_target_pairs={{0,1},{1,0},{2,3},{3,2},{4,5},{5,4},{6,7},{7,6},{8,9},{9,8},{10,11... | collective-permute-start | bytes 2752520 | tf_op jit(solution)/shard_map/ppermute | solution.py:46
  109.1 7.7 %collective-permute-start.17 = (bf16[128,1792]{1,0:T(8,128)(2,1)S(1)}, bf16[128,1792]{1,0:T(8,128)(2,1)S(1)}, u32[]{:S(2)}, u32[]{:S(2)}) collective-permute-start(bf16[128,1792]{1,0:T(8,128)(2,1)S(1)} %slice.120), channel_id=1, source_target_pairs={{0,96},{1,145},{32,0},{33,177},{64,32},{65,209},{96,64},{97,241},{... | collective-permute-start | bytes 1376264 | tf_op jit(solution)/shard_map/ppermute | solution.py:34
  109.7 8.8 %collective-permute-start.16 = (bf16[128,1792]{1,0:T(8,128)(2,1)S(1)}, bf16[128,1792]{1,0:T(8,128)(2,1)S(1)}, u32[]{:S(2)}, u32[]{:S(2)}) collective-permute-start(bf16[128,1792]{1,0:T(8,128)(2,1)S(1)} %slice.119), channel_id=1, source_target_pairs={{0,32},{1,129},{32,64},{33,161},{64,96},{65,193},{96,0},{97,225},{... | collective-permute-start | bytes 1376264 | tf_op jit(solution)/shard_map/ppermute | solution.py:34
  118.5 2.4 %collective-permute-start.20 = (bf16[128,1792]{1,0:T(8,128)(2,1)S(1)}, bf16[128,1792]{1,0:T(8,128)(2,1)S(1)}, u32[]{:S(2)}, u32[]{:S(2)}) collective-permute-start(bf16[128,1792]{1,0:T(8,128)(2,1)S(1)} %collective-permute-done.16.refs_0_), channel_id=1, source_target_pairs={{0,1},{1,0},{2,3},{3,2},{4,5},{5,4},{6,7},{7,6},{8,9},{9,8},{10,11... | collective-permute-start | bytes 1376264 | tf_op jit(solution)/shard_map/ppermute | solution.py:46
  119.5 2.1 %collective-permute-start.21 = (bf16[128,1792]{1,0:T(8,128)(2,1)S(1)}, bf16[128,1792]{1,0:T(8,128)(2,1)S(1)}, u32[]{:S(2)}, u32[]{:S(2)}) collective-permute-start(bf16[128,1792]{1,0:T(8,128)(2,1)S(1)} %collective-permute-done.17.refs_1_), channel_id=1, source_target_pairs={{0,1},{1,0},{2,3},{3,2},{4,5},{5,4},{6,7},{7,6},{8,9},{9,8},{10,11... | collective-permute-start | bytes 1376264 | tf_op jit(solution)/shard_map/ppermute | solution.py:46

commit v5 on v4

--- a/solution.py
+++ b/solution.py
@@ -27,9 +27,9 @@
         for y in range(N):
             for core in range(2):
                 if (core == 0) == first_axis:
-                    there = index(x, (y + shift) % N, core)
+                    there = index(x, y ^ shift, core)
                 else:
-                    there = index((x + shift) % N, y, core)
+                    there = index(x ^ shift, y, core)
                 pairs.append((index(x, y, core), there))
     return lax.ppermute(value, ("xlo", "y", "xhi", "core"), pairs)
 
@@ -49,7 +49,7 @@
 def block_row(here, core, far_step, near_step):
     dx = near_step + core * (far_step - near_step)
     dy = far_step + core * (near_step - far_step)
-    x, y = (here[0] + dx) % N, (here[1] + dy) % N
+    x, y = here[0] ^ dx, here[1] ^ dy
     return pl.multiple_of(((x % 2) * 8 + y * 2 + x // 2) * BLOCK, BLOCK)
 
 
@@ -94,7 +94,7 @@
             copy = pltpu.make_async_copy(
                 piece.at[pl.ds(n * BLOCK, BLOCK), :],
                 out.at[
-                    pl.ds(block_row(here, core, N - shift, N - begin - n), BLOCK),
+                    pl.ds(block_row(here, core, shift, begin + n), BLOCK),
                     pl.ds(pl.multiple_of(core * width, 128), width),
                 ],
                 sems.at[len(copies)],
@@ -197,20 +197,15 @@
     column = together(column.reshape(BLOCK, half))[0]
     parts = together(*[near(column, s) for s in (1, 2, 3)])
     (plane,) = together(jnp.concatenate([column, *parts], 0))
+    two = far(plane, 2)
     one, three, peer, *state_out = together(
         far(plane, 1), far(plane, 3), swap(plane), *[state_out[k] for k in range(3)]
     )
-    middle = plane.shape[0] // 2
-    two_a, two_b, one_peer, three_peer, weight = together(
-        far(one[:middle], 1),
-        far(three[middle:], 3),
-        swap(one),
-        swap(three),
-        join(here, [(plane, 0, 0, 0), (one, 1, 0, 0), (three, 3, 0, 0), (peer, 0, 0, 1)]),
-    )
-    items = [(two_a, 2, 0, 0), (two_b, 2, 2, 0), (one_peer, 1, 0, 1), (three_peer, 3, 0, 1)]
-    items += [(swap(two_a), 2, 0, 1), (swap(two_b), 2, 2, 1)]
-    weight = join(here, items, weight)
+    items = [(plane, 0, 0, 0), (one, 1, 0, 0), (three, 3, 0, 0), (peer, 0, 0, 1)]
+    two, one_peer, three_peer, weight = together(two, swap(one), swap(three), join(here, items))
+    items = [(two, 2, 0, 0), (one_peer, 1, 0, 1), (three_peer, 3, 0, 1)]
+    two_peer, weight = together(swap(two), join(here, items, weight))
+    weight = join(here, [(two_peer, 2, 0, 1)], weight)
     return (weight, state_out[0], state_out[1], state_out[2])
 
 

time: 125 us -> 120 us (0.960)
  waiting for transfers between devices: 64.7 us -> 60 us
    ppermute x13 -> x12, waiting for transfers between devices: 42.5 us -> 39.9 us  [in_plane(): return lax.ppermute(value, ('xlo', 'y', 'xhi', 'core'), pairs)]
    ppermute x9 -> x8, waiting for transfers between devices: 4.37 us -> 2.37 us  [swap(): return lax.ppermute(value, 'core', SWAP)]
    ppermute x9 -> x8, starting transfers between devices: 21.8 us -> 20.5 us  [swap(): return lax.ppermute(value, 'core', SWAP)]
    pallas_call x2 -> x3, Pallas kernels: 5.04 us -> 6.2 us  [join(): pl.pallas_call(functools.partial(join_kernel, tuple((item[1:] for item in...]
    ppermute x13 -> x12, starting transfers between devices: 13.8 us -> 13.8 us  [in_plane(): return lax.ppermute(value, ('xlo', 'y', 'xhi', 'core'), pairs)]
  transfers between devices with their start and end apart: 24 -> 22, of which waited for: 15 -> 13; matrix products, arithmetic and copies ran while one was open for 1% -> 1% of each run, Pallas kernels for 2% -> 4%
where the time goes in v5:
time: 120 us
  waiting for transfers between devices  60 us (50%)
  starting transfers between devices  44.8 us (37%)
  Pallas kernels  8.02 us (7%)
  local copies, waits for them, and re-layouts  2.57 us (2%)
  other arithmetic  2 us (2%)
    ppermute x12, waiting for transfers between devices, in_plane(): return lax.ppermute(value, ('xlo', 'y', 'xhi', 'core'), pairs)  39.9 us
    ppermute x8, starting transfers between devices, swap(): return lax.ppermute(value, 'core', SWAP)  20.5 us
    ppermute x12, starting transfers between devices, in_plane(): return lax.ppermute(value, ('xlo', 'y', 'xhi', 'core'), pairs)  13.8 us
    all_to_all x1, waiting for transfers between devices, shards(): lax.all_to_all(plane_sum.reshape(N_Z, BLOCK // N_Z, half), 'z', 0, 0)  8.94 us
    all_to_all x1, waiting for transfers between devices, shards(): lax.all_to_all(jnp.broadcast_to(piece, (N_Z,) + piece.shape), 'z', 0, 0)  8.81 us
    all_to_all x1, starting transfers between devices, shards(): lax.all_to_all(plane_sum.reshape(N_Z, BLOCK // N_Z, half), 'z', 0, 0)  7.15 us
    pallas_call x3, Pallas kernels, join(): pl.pallas_call(functools.partial(join_kernel, tuple((item[1:] for item in...  6.2 us
    all_to_all x1, starting transfers between devices, shards(): lax.all_to_all(jnp.broadcast_to(piece, (N_Z,) + piece.shape), 'z', 0, 0)  3.4 us
  transfers between devices with their start and end apart: 22, of which 13 were waited for; matrix products, arithmetic and copies ran while one was open for 1% of the time, Pallas kernels for 4%

profile of v5, /device:TPU:1, one launch (start us, length us, event | category | flops | bytes accessed | tf_op | source)
XLA Modules:
  0.0 119.6 jit_solution(13802627050527891217)
XLA Ops:
  0.7 1.2 copy-done
  1.8 1.2 fusion
  3.1 3.3 %collective-permute-start.1 = (bf16[128,1792]{1,0:T(8,128)(2,1)S(1)}, bf16[128,1792]{1,0:T(8,128)(2,1)S(1)}, u32[]{:S(2)}, u32[]{:S(2)}) collective-permute-start(bf16[128,1792]{1,0:T(8,128)(2,1)S(1)} %get-tuple-element.71), channel_id=1, source_target_pairs={{0,1},{1,0},{2,3},{3,2},{4,5},{5,4},{6,7},{7,6},{8,9},{9,8},{10,11... | collective-permute-start | bytes 1376264 | tf_op jit(solution)/shard_map/ppermute | solution.py:46
  6.8 1.4 %collective-permute-done.hidden_peer = bf16[128,1024]{1,0:T(8,128)(2,1)S(1)} collective-permute-done((bf16[128,1024]{1,0:T(8,128)(2,1)S(1)}, bf16[128,1024]{1,0:T(8,128)(2,1)S(1)}, u32[]{:S(2)}, u32[]{:S(2)}) %collective-permute-start) | collective-permute-done | bytes 262176 | tf_op jit(solution)/shard_map/ppermute | solution.py:46
  8.2 1.8 %shard_map.111 = (bf16[256,1792]{1,0:T(8,128)(2,1)S(1)}, bf16[256,1792]{1,0:T(8,128)(2,1)S(1)}, bf16[256,1792]{1,0:T(8,128)(2,1)S(1)}, bf16[256,1792]{1,0:T(8,128)(2,1)S(1)}) custom-call(s32[3]{0:T(128)S(1)} %pad_add_fusion.here, bf16[128,1024]{1,0:T(8,128)(2,1)S(1)} %fusion.5.hidden, bf16[128,1024]{1,0:T(8,128)(2,1)S(1)} %collective-permute-done.hidden_peer, ...), custom_call_target="tpu_custom_call" | custom-call | flops 939524096 | bytes 5000000 | tf_op jit(solution)/shard_map/pallas_call | solution.py:72
  10.1 1.1 collective-permute-start.2
  11.5 1.9 %collective-permute-start.4 = (bf16[256,1792]{1,0:T(8,128)(2,1)S(1)}, bf16[256,1792]{1,0:T(8,128)(2,1)S(1)}, u32[]{:S(2)}, u32[]{:S(2)}) collective-permute-start(bf16[256,1792]{1,0:T(8,128)(2,1)S(1)} %get-tuple-element.36), channel_id=1, source_target_pairs={{0,96},{1,145},{32,64},{33,177},{64,32},{65,209},{96,0},{97,241},{... | collective-permute-start | bytes 2752520 | tf_op jit(solution)/shard_map/ppermute | solution.py:34
  13.5 1.3 %collective-permute-start.5 = (f32[3,4,1792]{2,1,0:T(4,128)S(1)}, f32[3,4,1792]{2,1,0:T(4,128)S(1)}, u32[]{:S(2)}, u32[]{:S(2)}) collective-permute-start(f32[3,4,1792]{2,1,0:T(4,128)S(1)} %get-tuple-element.79), channel_id=1, source_target_pairs={{0,1},{1,0},{2,3},{3,2},{4,5},{5,4},{6,7},{7,6},{8,9},{9,8},{10,11... | collective-permute-start | bytes 258056 | tf_op jit(solution)/shard_map/ppermute | solution.py:46
  15.7 8.5 %collective-permute-done.2 = bf16[256,1792]{1,0:T(8,128)(2,1)S(1)} collective-permute-done((bf16[256,1792]{1,0:T(8,128)(2,1)S(1)}, bf16[256,1792]{1,0:T(8,128)(2,1)S(1)}, u32[]{:S(2)}, u32[]{:S(2)}) %collective-permute-start.2) | collective-permute-done | bytes 917536 | tf_op jit(solution)/shard_map/ppermute | solution.py:34
  24.2 8.2 %collective-permute-done.3 = bf16[256,1792]{1,0:T(8,128)(2,1)S(1)} collective-permute-done((bf16[256,1792]{1,0:T(8,128)(2,1)S(1)}, bf16[256,1792]{1,0:T(8,128)(2,1)S(1)}, u32[]{:S(2)}, u32[]{:S(2)}) %collective-permute-start.3) | collective-permute-done | bytes 917536 | tf_op jit(solution)/shard_map/ppermute | solution.py:34
  32.4 1.6 %collective-permute-done.4 = bf16[256,1792]{1,0:T(8,128)(2,1)S(1)} collective-permute-done((bf16[256,1792]{1,0:T(8,128)(2,1)S(1)}, bf16[256,1792]{1,0:T(8,128)(2,1)S(1)}, u32[]{:S(2)}, u32[]{:S(2)}) %collective-permute-start.4) | collective-permute-done | bytes 917536 | tf_op jit(solution)/shard_map/ppermute | solution.py:34
  34.5 1.4 %collective-permute-start.6 = (bf16[64,1792]{1,0:T(8,128)(2,1)S(1)}, bf16[64,1792]{1,0:T(8,128)(2,1)S(1)}, u32[]{:S(2)}, u32[]{:S(2)}) collective-permute-start(bf16[64,1792]{1,0:T(8,128)(2,1)S(1)} %get-tuple-element.43), channel_id=1, source_target_pairs={{0,16},{1,65},{32,48},{33,97},{64,80},{65,1},{96,112},{97,33},{128... | collective-permute-start | bytes 688136 | tf_op jit(solution)/shard_map/ppermute | solution.py:34
  36.3 1.5 %collective-permute-start.8 = (bf16[64,1792]{1,0:T(8,128)(2,1)S(1)}, bf16[64,1792]{1,0:T(8,128)(2,1)S(1)}, u32[]{:S(2)}, u32[]{:S(2)}) collective-permute-start(bf16[64,1792]{1,0:T(8,128)(2,1)S(1)} %get-tuple-element.45), channel_id=1, source_target_pairs={{0,144},{1,97},{32,176},{33,65},{64,208},{65,33},{96,240},{97,1},{... | collective-permute-start | bytes 688136 | tf_op jit(solution)/shard_map/ppermute | solution.py:34
  37.8 3.4 %collective-permute-done.6 = bf16[64,1792]{1,0:T(8,128)(2,1)S(1)} collective-permute-done((bf16[64,1792]{1,0:T(8,128)(2,1)S(1)}, bf16[64,1792]{1,0:T(8,128)(2,1)S(1)}, u32[]{:S(2)}, u32[]{:S(2)}) %collective-permute-start.6) | collective-permute-done | bytes 229408 | tf_op jit(solution)/shard_map/ppermute | solution.py:34
  41.2 1.2 %collective-permute-done.7 = bf16[64,1792]{1,0:T(8,128)(2,1)S(1)} collective-permute-done((bf16[64,1792]{1,0:T(8,128)(2,1)S(1)}, bf16[64,1792]{1,0:T(8,128)(2,1)S(1)}, u32[]{:S(2)}, u32[]{:S(2)}) %collective-permute-start.7) | collective-permute-done | bytes 229408 | tf_op jit(solution)/shard_map/ppermute | solution.py:34
  42.4 1.3 %collective-permute-done.8 = bf16[64,1792]{1,0:T(8,128)(2,1)S(1)} collective-permute-done((bf16[64,1792]{1,0:T(8,128)(2,1)S(1)}, bf16[64,1792]{1,0:T(8,128)(2,1)S(1)}, u32[]{:S(2)}, u32[]{:S(2)}) %collective-permute-start.8) | collective-permute-done | bytes 229408 | tf_op jit(solution)/shard_map/ppermute | solution.py:34
  44.5 7.2 %all-to-all-start = ((bf16[8,8,1792]{2,1,0:T(8,128)(2,1)}), bf16[8,8,1792]{2,1,0:T(8,128)(2,1)S(1)}, u32[]{:S(2)}, u32[]{:S(2)}) async-start(bf16[8,8,1792]{2,1,0:T(8,128)(2,1)} %fusion.6), calls=%async_computation | async-start | bytes 458752 | tf_op jit(solution)/shard_map/all_to_all | solution.py:179
  51.7 8.9 %all-to-all-done = bf16[8,8,1792]{2,1,0:T(8,128)(2,1)S(1)} async-done(((bf16[8,8,1792]{2,1,0:T(8,128)(2,1)}), bf16[8,8,1792]{2,1,0:T(8,128)(2,1)S(1)}, u32[]{:S(2)}, u32[]{:S(2)}) %all-to-all-start) | async-done | bytes 229408 | tf_op jit(solution)/shard_map/all_to_all | solution.py:179
  61.5 3.4 %all-to-all-start.1 = ((bf16[8,8,1792]{2,1,0:T(8,128)(2,1)}), bf16[8,8,1792]{2,1,0:T(8,128)(2,1)S(1)}, u32[]{:S(2)}, u32[]{:S(2)}) async-start(bf16[8,8,1792]{2,1,0:T(8,128)(2,1)} %broadcast_in_dim.2), calls=%async_computation.1 | async-start | bytes 458752 | tf_op jit(solution)/shard_map/all_to_all | solution.py:196
  65.0 8.8 %all-to-all-done.1 = bf16[8,8,1792]{2,1,0:T(8,128)(2,1)S(1)} async-done(((bf16[8,8,1792]{2,1,0:T(8,128)(2,1)}), bf16[8,8,1792]{2,1,0:T(8,128)(2,1)S(1)}, u32[]{:S(2)}, u32[]{:S(2)}) %all-to-all-start.1) | async-done | bytes 229408 | tf_op jit(solution)/shard_map/all_to_all | solution.py:196
  73.8 2.3 %collective-permute-start.11 = (bf16[64,1792]{1,0:T(8,128)(2,1)S(1)}, bf16[64,1792]{1,0:T(8,128)(2,1)S(1)}, u32[]{:S(2)}, u32[]{:S(2)}) collective-permute-start(bf16[64,1792]{1,0:T(8,128)(2,1)S(1)} %bitcast.44), channel_id=1, source_target_pairs={{0,144},{1,97},{32,176},{33,65},{64,208},{65,33},{96,240},{97,1},{... | collective-permute-start | bytes 688136 | tf_op jit(solution)/shard_map/ppermute | solution.py:34
  77.1 6.1 %collective-permute-start.16 = (f32[3,4,1792]{2,1,0:T(4,128)S(1)}, f32[3,4,1792]{2,1,0:T(4,128)S(1)}, u32[]{:S(2)}, u32[]{:S(2)}) collective-permute-start(f32[3,4,1792]{2,1,0:T(4,128)S(1)} %get-tuple-element.77), channel_id=1, source_target_pairs={{0,1},{1,0},{2,3},{3,2},{4,5},{5,4},{6,7},{7,6},{8,9},{9,8},{10,11... | collective-permute-start | bytes 258056 | tf_op jit(solution)/shard_map/ppermute | solution.py:46
  83.2 6.4 %collective-permute-start.15 = (bf16[256,1792]{1,0:T(8,128)(2,1)S(1)}, bf16[256,1792]{1,0:T(8,128)(2,1)S(1)}, u32[]{:S(2)}, u32[]{:S(2)}) collective-permute-start(bf16[256,1792]{1,0:T(8,128)(2,1)S(1)} %pad_maximum_fusion.refs_0_), channel_id=1, source_target_pairs={{0,1},{1,0},{2,3},{3,2},{4,5},{5,4},{6,7},{7,6},{8,9},{9,8},{10,11... | collective-permute-start | bytes 2752520 | tf_op jit(solution)/shard_map/ppermute | solution.py:46
  89.7 1.6 %collective-permute-start.14 = (bf16[256,1792]{1,0:T(8,128)(2,1)S(1)}, bf16[256,1792]{1,0:T(8,128)(2,1)S(1)}, u32[]{:S(2)}, u32[]{:S(2)}) collective-permute-start(bf16[256,1792]{1,0:T(8,128)(2,1)S(1)} %pad_maximum_fusion.refs_0_), channel_id=1, source_target_pairs={{0,96},{1,145},{32,64},{33,177},{64,32},{65,209},{96,0},{97,241},{... | collective-permute-start | bytes 2752520 | tf_op jit(solution)/shard_map/ppermute | solution.py:34
  92.0 2.2 %collective-permute-start.12 = (bf16[256,1792]{1,0:T(8,128)(2,1)S(1)}, bf16[256,1792]{1,0:T(8,128)(2,1)S(1)}, u32[]{:S(2)}, u32[]{:S(2)}) collective-permute-start(bf16[256,1792]{1,0:T(8,128)(2,1)S(1)} %pad_maximum_fusion.refs_0_), channel_id=1, source_target_pairs={{0,64},{1,17},{32,96},{33,49},{64,0},{65,81},{96,32},{97,113},{128... | collective-permute-start | bytes 2752520 | tf_op jit(solution)/shard_map/ppermute | solution.py:34
  94.3 9.2 %collective-permute-done.14.refs_2_ = bf16[256,1792]{1,0:T(8,128)(2,1)S(1)} collective-permute-done((bf16[256,1792]{1,0:T(8,128)(2,1)S(1)}, bf16[256,1792]{1,0:T(8,128)(2,1)S(1)}, u32[]{:S(2)}, u32[]{:S(2)}) %collective-permute-start.14) | collective-permute-done | bytes 917536 | tf_op jit(solution)/shard_map/ppermute | solution.py:34
  103.8 2.0 %collective-permute-start.17 = (bf16[256,1792]{1,0:T(8,128)(2,1)S(1)}, bf16[256,1792]{1,0:T(8,128)(2,1)S(1)}, u32[]{:S(2)}, u32[]{:S(2)}) collective-permute-start(bf16[256,1792]{1,0:T(8,128)(2,1)S(1)} %collective-permute-done.13.refs_1_), channel_id=1, source_target_pairs={{0,1},{1,0},{2,3},{3,2},{4,5},{5,4},{6,7},{7,6},{8,9},{9,8},{10,11... | collective-permute-start | bytes 2752520 | tf_op jit(solution)/shard_map/ppermute | solution.py:46
  105.8 2.5 %shard_map.112.refs_3_ = bf16[1024,3584]{1,0:T(8,128)(2,1)} custom-call(s32[3]{0:T(128)S(1)} %pad_add_fusion.here, bf16[256,1792]{1,0:T(8,128)(2,1)S(1)} %pad_maximum_fusion.refs_0_, bf16[256,1792]{1,0:T(8,128)(2,1)S(1)} %collective-permute-done.13.refs_1_, bf16[256,1792]{1,0:T(8,128)(2,1)S(1)} %collective-permute-done.14.refs_2_, ...), custom_call_target="tpu_custom_call" | custom-call | bytes 7340032 | tf_op jit(solution)/shard_map/pallas_call | solution.py:114
  108.3 6.1 %collective-permute-done.12.refs_0_ = bf16[256,1792]{1,0:T(8,128)(2,1)S(1)} collective-permute-done((bf16[256,1792]{1,0:T(8,128)(2,1)S(1)}, bf16[256,1792]{1,0:T(8,128)(2,1)S(1)}, u32[]{:S(2)}, u32[]{:S(2)}) %collective-permute-start.12) | collective-permute-done | bytes 917536 | tf_op jit(solution)/shard_map/ppermute | solution.py:34
  114.5 1.2 %collective-permute-start.19 = (bf16[256,1792]{1,0:T(8,128)(2,1)S(1)}, bf16[256,1792]{1,0:T(8,128)(2,1)S(1)}, u32[]{:S(2)}, u32[]{:S(2)}) collective-permute-start(bf16[256,1792]{1,0:T(8,128)(2,1)S(1)} %collective-permute-done.12.refs_0_), channel_id=1, source_target_pairs={{0,1},{1,0},{2,3},{3,2},{4,5},{5,4},{6,7},{7,6},{8,9},{9,8},{10,11... | collective-permute-start | bytes 2752520 | tf_op jit(solution)/shard_map/ppermute | solution.py:46
  115.7 2.2 %shard_map.113.refs_1_ = bf16[1024,3584]{1,0:T(8,128)(2,1)} custom-call(s32[3]{0:T(128)S(1)} %pad_add_fusion.here, bf16[256,1792]{1,0:T(8,128)(2,1)S(1)} %collective-permute-done.12.refs_0_, bf16[256,1792]{1,0:T(8,128)(2,1)S(1)} %collective-permute-done.17.refs_1_, ...), custom_call_target="tpu_custom_call", output_to_operand_aliasing={{}: (4, {})} | custom-call | bytes 5505024 | tf_op jit(solution)/shard_map/pallas_call | solution.py:114
  117.9 1.5 %shard_map.114 = bf16[1024,3584]{1,0:T(8,128)(2,1)} custom-call(s32[3]{0:T(128)S(1)} %pad_add_fusion.here, bf16[256,1792]{1,0:T(8,128)(2,1)S(1)} %collective-permute-done.19.refs_0_, bf16[1024,3584]{1,0:T(8,128)(2,1)} %shard_map.113.refs_1_), custom_call_target="tpu_custom_call", output_to_operand_aliasing={{}: (2, {})} | custom-call | bytes 1835008 | tf_op jit(solution)/shard_map/pallas_call | solution.py:114
  (46 shorter events, 6.6 us)
Async XLA Ops:
  0.6 1.2 copy-start
  1.8 4.6 %copy-start.1 = (bf16[128,1024]{1,0:T(8,128)(2,1)S(1)}, bf16[128,1024]{1,0:T(8,128)(2,1)}, u32[]{:S(2)}) copy-start(bf16[128,1024]{1,0:T(8,128)(2,1)} %param.9) | copy-start | bytes 786436
  1.8 4.6 %copy-start.2 = (bf16[128,1024]{1,0:T(8,128)(2,1)S(1)}, bf16[128,1024]{1,0:T(8,128)(2,1)}, u32[]{:S(2)}) copy-start(bf16[128,1024]{1,0:T(8,128)(2,1)} %param.8) | copy-start | bytes 786436
  3.1 5.2 %collective-permute-start.1 = (bf16[128,1792]{1,0:T(8,128)(2,1)S(1)}, bf16[128,1792]{1,0:T(8,128)(2,1)S(1)}, u32[]{:S(2)}, u32[]{:S(2)}) collective-permute-start(bf16[128,1792]{1,0:T(8,128)(2,1)S(1)} %get-tuple-element.71), channel_id=1, source_target_pairs={{0,1},{1,0},{2,3},{3,2},{4,5},{5,4},{6,7},{7,6},{8,9},{9,8},{10,11... | collective-permute-start | bytes 1376264 | tf_op jit(solution)/shard_map/ppermute | solution.py:46
  6.6 6.8 %copy-start.3 = (f32[4,3584]{1,0:T(4,128)S(1)}, f32[4,3584]{1,0:T(4,128)}, u32[]{:S(2)}) copy-start(f32[4,3584]{1,0:T(4,128)} %param.15) | copy-start | bytes 172036
  6.6 6.8 %copy-start.4 = (f32[4,3584]{1,0:T(4,128)S(1)}, f32[4,3584]{1,0:T(4,128)}, u32[]{:S(2)}) copy-start(f32[4,3584]{1,0:T(4,128)} %param.14) | copy-start | bytes 172036
  6.6 6.8 %copy-start.5 = (f32[4,3584]{1,0:T(4,128)S(1)}, f32[4,3584]{1,0:T(4,128)}, u32[]{:S(2)}) copy-start(f32[4,3584]{1,0:T(4,128)} %param.13) | copy-start | bytes 172036
  6.6 1.6 %collective-permute-start = (bf16[128,1024]{1,0:T(8,128)(2,1)S(1)}, bf16[128,1024]{1,0:T(8,128)(2,1)S(1)}, u32[]{:S(2)}, u32[]{:S(2)}) collective-permute-start(bf16[128,1024]{1,0:T(8,128)(2,1)S(1)} %fusion.5.hidden), channel_id=1, source_target_pairs={{0,1},{1,0},{2,3},{3,2},{4,5},{5,4},{6,7},{7,6},{8,9},{9,8},{10,11... | collective-permute-start | bytes 786440 | tf_op jit(solution)/shard_map/ppermute | solution.py:46
  10.1 14.2 %collective-permute-start.2 = (bf16[256,1792]{1,0:T(8,128)(2,1)S(1)}, bf16[256,1792]{1,0:T(8,128)(2,1)S(1)}, u32[]{:S(2)}, u32[]{:S(2)}) collective-permute-start(bf16[256,1792]{1,0:T(8,128)(2,1)S(1)} %get-tuple-element.34), channel_id=1, source_target_pairs={{0,64},{1,17},{32,96},{33,49},{64,0},{65,81},{96,32},{97,113},{128... | collective-permute-start | bytes 2752520 | tf_op jit(solution)/shard_map/ppermute | solution.py:34
  11.2 21.3 %collective-permute-start.3 = (bf16[256,1792]{1,0:T(8,128)(2,1)S(1)}, bf16[256,1792]{1,0:T(8,128)(2,1)S(1)}, u32[]{:S(2)}, u32[]{:S(2)}) collective-permute-start(bf16[256,1792]{1,0:T(8,128)(2,1)S(1)} %get-tuple-element.35), channel_id=1, source_target_pairs={{0,32},{1,129},{32,0},{33,161},{64,96},{65,193},{96,64},{97,225},{... | collective-permute-start | bytes 2752520 | tf_op jit(solution)/shard_map/ppermute | solution.py:34
  11.5 22.6 %collective-permute-start.4 = (bf16[256,1792]{1,0:T(8,128)(2,1)S(1)}, bf16[256,1792]{1,0:T(8,128)(2,1)S(1)}, u32[]{:S(2)}, u32[]{:S(2)}) collective-permute-start(bf16[256,1792]{1,0:T(8,128)(2,1)S(1)} %get-tuple-element.36), channel_id=1, source_target_pairs={{0,96},{1,145},{32,64},{33,177},{64,32},{65,209},{96,0},{97,241},{... | collective-permute-start | bytes 2752520 | tf_op jit(solution)/shard_map/ppermute | solution.py:34
  13.5 2.2 %collective-permute-start.5 = (f32[3,4,1792]{2,1,0:T(4,128)S(1)}, f32[3,4,1792]{2,1,0:T(4,128)S(1)}, u32[]{:S(2)}, u32[]{:S(2)}) collective-permute-start(f32[3,4,1792]{2,1,0:T(4,128)S(1)} %get-tuple-element.79), channel_id=1, source_target_pairs={{0,1},{1,0},{2,3},{3,2},{4,5},{5,4},{6,7},{7,6},{8,9},{9,8},{10,11... | collective-permute-start | bytes 258056 | tf_op jit(solution)/shard_map/ppermute | solution.py:46
  34.5 6.8 %collective-permute-start.6 = (bf16[64,1792]{1,0:T(8,128)(2,1)S(1)}, bf16[64,1792]{1,0:T(8,128)(2,1)S(1)}, u32[]{:S(2)}, u32[]{:S(2)}) collective-permute-start(bf16[64,1792]{1,0:T(8,128)(2,1)S(1)} %get-tuple-element.43), channel_id=1, source_target_pairs={{0,16},{1,65},{32,48},{33,97},{64,80},{65,1},{96,112},{97,33},{128... | collective-permute-start | bytes 688136 | tf_op jit(solution)/shard_map/ppermute | solution.py:34
  35.9 6.6 %collective-permute-start.7 = (bf16[64,1792]{1,0:T(8,128)(2,1)S(1)}, bf16[64,1792]{1,0:T(8,128)(2,1)S(1)}, u32[]{:S(2)}, u32[]{:S(2)}) collective-permute-start(bf16[64,1792]{1,0:T(8,128)(2,1)S(1)} %get-tuple-element.44), channel_id=1, source_target_pairs={{0,128},{1,33},{32,160},{33,1},{64,192},{65,97},{96,224},{97,65},{... | collective-permute-start | bytes 688136 | tf_op jit(solution)/shard_map/ppermute | solution.py:34
  36.3 7.4 %collective-permute-start.8 = (bf16[64,1792]{1,0:T(8,128)(2,1)S(1)}, bf16[64,1792]{1,0:T(8,128)(2,1)S(1)}, u32[]{:S(2)}, u32[]{:S(2)}) collective-permute-start(bf16[64,1792]{1,0:T(8,128)(2,1)S(1)} %get-tuple-element.45), channel_id=1, source_target_pairs={{0,144},{1,97},{32,176},{33,65},{64,208},{65,33},{96,240},{97,1},{... | collective-permute-start | bytes 688136 | tf_op jit(solution)/shard_map/ppermute | solution.py:34
  44.5 16.2 %all-to-all-start = ((bf16[8,8,1792]{2,1,0:T(8,128)(2,1)}), bf16[8,8,1792]{2,1,0:T(8,128)(2,1)S(1)}, u32[]{:S(2)}, u32[]{:S(2)}) async-start(bf16[8,8,1792]{2,1,0:T(8,128)(2,1)} %fusion.6), calls=%async_computation | async-start | bytes 458752 | tf_op jit(solution)/shard_map/all_to_all | solution.py:179
  61.5 12.3 %all-to-all-start.1 = ((bf16[8,8,1792]{2,1,0:T(8,128)(2,1)}), bf16[8,8,1792]{2,1,0:T(8,128)(2,1)S(1)}, u32[]{:S(2)}, u32[]{:S(2)}) async-start(bf16[8,8,1792]{2,1,0:T(8,128)(2,1)} %broadcast_in_dim.2), calls=%async_computation.1 | async-start | bytes 458752 | tf_op jit(solution)/shard_map/all_to_all | solution.py:196
  73.8 9.4 %collective-permute-start.11 = (bf16[64,1792]{1,0:T(8,128)(2,1)S(1)}, bf16[64,1792]{1,0:T(8,128)(2,1)S(1)}, u32[]{:S(2)}, u32[]{:S(2)}) collective-permute-start(bf16[64,1792]{1,0:T(8,128)(2,1)S(1)} %bitcast.44), channel_id=1, source_target_pairs={{0,144},{1,97},{32,176},{33,65},{64,208},{65,33},{96,240},{97,1},{... | collective-permute-start | bytes 688136 | tf_op jit(solution)/shard_map/ppermute | solution.py:34
  76.0 7.1 %collective-permute-start.10 = (bf16[64,1792]{1,0:T(8,128)(2,1)S(1)}, bf16[64,1792]{1,0:T(8,128)(2,1)S(1)}, u32[]{:S(2)}, u32[]{:S(2)}) collective-permute-start(bf16[64,1792]{1,0:T(8,128)(2,1)S(1)} %bitcast.45), channel_id=1, source_target_pairs={{0,16},{1,65},{32,48},{33,97},{64,80},{65,1},{96,112},{97,33},{128... | collective-permute-start | bytes 688136 | tf_op jit(solution)/shard_map/ppermute | solution.py:34
  76.5 6.6 %collective-permute-start.9 = (bf16[64,1792]{1,0:T(8,128)(2,1)S(1)}, bf16[64,1792]{1,0:T(8,128)(2,1)S(1)}, u32[]{:S(2)}, u32[]{:S(2)}) collective-permute-start(bf16[64,1792]{1,0:T(8,128)(2,1)S(1)} %bitcast.46), channel_id=1, source_target_pairs={{0,128},{1,33},{32,160},{33,1},{64,192},{65,97},{96,224},{97,65},{... | collective-permute-start | bytes 688136 | tf_op jit(solution)/shard_map/ppermute | solution.py:34
  77.1 14.2 %collective-permute-start.16 = (f32[3,4,1792]{2,1,0:T(4,128)S(1)}, f32[3,4,1792]{2,1,0:T(4,128)S(1)}, u32[]{:S(2)}, u32[]{:S(2)}) collective-permute-start(f32[3,4,1792]{2,1,0:T(4,128)S(1)} %get-tuple-element.77), channel_id=1, source_target_pairs={{0,1},{1,0},{2,3},{3,2},{4,5},{5,4},{6,7},{7,6},{8,9},{9,8},{10,11... | collective-permute-start | bytes 258056 | tf_op jit(solution)/shard_map/ppermute | solution.py:46
  83.2 11.0 %collective-permute-start.15 = (bf16[256,1792]{1,0:T(8,128)(2,1)S(1)}, bf16[256,1792]{1,0:T(8,128)(2,1)S(1)}, u32[]{:S(2)}, u32[]{:S(2)}) collective-permute-start(bf16[256,1792]{1,0:T(8,128)(2,1)S(1)} %pad_maximum_fusion.refs_0_), channel_id=1, source_target_pairs={{0,1},{1,0},{2,3},{3,2},{4,5},{5,4},{6,7},{7,6},{8,9},{9,8},{10,11... | collective-permute-start | bytes 2752520 | tf_op jit(solution)/shard_map/ppermute | solution.py:46
  89.7 13.8 %collective-permute-start.14 = (bf16[256,1792]{1,0:T(8,128)(2,1)S(1)}, bf16[256,1792]{1,0:T(8,128)(2,1)S(1)}, u32[]{:S(2)}, u32[]{:S(2)}) collective-permute-start(bf16[256,1792]{1,0:T(8,128)(2,1)S(1)} %pad_maximum_fusion.refs_0_), channel_id=1, source_target_pairs={{0,96},{1,145},{32,64},{33,177},{64,32},{65,209},{96,0},{97,241},{... | collective-permute-start | bytes 2752520 | tf_op jit(solution)/shard_map/ppermute | solution.py:34
  91.3 12.5 %collective-permute-start.13 = (bf16[256,1792]{1,0:T(8,128)(2,1)S(1)}, bf16[256,1792]{1,0:T(8,128)(2,1)S(1)}, u32[]{:S(2)}, u32[]{:S(2)}) collective-permute-start(bf16[256,1792]{1,0:T(8,128)(2,1)S(1)} %pad_maximum_fusion.refs_0_), channel_id=1, source_target_pairs={{0,32},{1,129},{32,0},{33,161},{64,96},{65,193},{96,64},{97,225},{... | collective-permute-start | bytes 2752520 | tf_op jit(solution)/shard_map/ppermute | solution.py:34
  92.0 22.4 %collective-permute-start.12 = (bf16[256,1792]{1,0:T(8,128)(2,1)S(1)}, bf16[256,1792]{1,0:T(8,128)(2,1)S(1)}, u32[]{:S(2)}, u32[]{:S(2)}) collective-permute-start(bf16[256,1792]{1,0:T(8,128)(2,1)S(1)} %pad_maximum_fusion.refs_0_), channel_id=1, source_target_pairs={{0,64},{1,17},{32,96},{33,49},{64,0},{65,81},{96,32},{97,113},{128... | collective-permute-start | bytes 2752520 | tf_op jit(solution)/shard_map/ppermute | solution.py:34
  103.8 10.6 %collective-permute-start.17 = (bf16[256,1792]{1,0:T(8,128)(2,1)S(1)}, bf16[256,1792]{1,0:T(8,128)(2,1)S(1)}, u32[]{:S(2)}, u32[]{:S(2)}) collective-permute-start(bf16[256,1792]{1,0:T(8,128)(2,1)S(1)} %collective-permute-done.13.refs_1_), channel_id=1, source_target_pairs={{0,1},{1,0},{2,3},{3,2},{4,5},{5,4},{6,7},{7,6},{8,9},{9,8},{10,11... | collective-permute-start | bytes 2752520 | tf_op jit(solution)/shard_map/ppermute | solution.py:46
  105.8 8.7 %collective-permute-start.18 = (bf16[256,1792]{1,0:T(8,128)(2,1)S(1)}, bf16[256,1792]{1,0:T(8,128)(2,1)S(1)}, u32[]{:S(2)}, u32[]{:S(2)}) collective-permute-start(bf16[256,1792]{1,0:T(8,128)(2,1)S(1)} %collective-permute-done.14.refs_2_), channel_id=1, source_target_pairs={{0,1},{1,0},{2,3},{3,2},{4,5},{5,4},{6,7},{7,6},{8,9},{9,8},{10,11... | collective-permute-start | bytes 2752520 | tf_op jit(solution)/shard_map/ppermute | solution.py:46
  114.5 3.4 %collective-permute-start.19 = (bf16[256,1792]{1,0:T(8,128)(2,1)S(1)}, bf16[256,1792]{1,0:T(8,128)(2,1)S(1)}, u32[]{:S(2)}, u32[]{:S(2)}) collective-permute-start(bf16[256,1792]{1,0:T(8,128)(2,1)S(1)} %collective-permute-done.12.refs_0_), channel_id=1, source_target_pairs={{0,1},{1,0},{2,3},{3,2},{4,5},{5,4},{6,7},{7,6},{8,9},{9,8},{10,11... | collective-permute-start | bytes 2752520 | tf_op jit(solution)/shard_map/ppermute | solution.py:46

commit v6 on v5

--- a/solution.py
+++ b/solution.py
@@ -61,9 +61,9 @@
     columns = jnp.concatenate([scaled[...], scaled_peer[...]], 0)
     for f in range(N):
         rows = [turned[pl.ds(block_row(here, here[2], f, n), BLOCK), :] for n in range(N)]
-        outs[f][...] = jnp.dot(
-            jnp.concatenate(rows, 0), columns, preferred_element_type=jnp.float32
-        ).astype(jnp.bfloat16)
+        block = jnp.dot(jnp.concatenate(rows, 0), columns, preferred_element_type=jnp.float32)
+        outs[f][...] = block[: 2 * BLOCK].astype(jnp.bfloat16)
+        outs[N + f][...] = block[2 * BLOCK :].astype(jnp.bfloat16)
 
 
 def terms(here, hidden, hidden_peer, scaled, scaled_peer):
@@ -71,9 +71,9 @@
     whole = pl.BlockSpec(memory_space=pltpu.VMEM)
     return pl.pallas_call(
         terms_kernel,
-        out_shape=[jax.ShapeDtypeStruct((N * BLOCK, width), jnp.bfloat16)] * N,
+        out_shape=[jax.ShapeDtypeStruct((2 * BLOCK, width), jnp.bfloat16)] * (2 * N),
         in_specs=[pl.BlockSpec(memory_space=pltpu.SMEM)] + [whole] * 4,
-        out_specs=[whole] * N,
+        out_specs=[whole] * (2 * N),
         scratch_shapes=[pltpu.VMEM((hidden.shape[1], 2 * tokens), jnp.bfloat16)],
         compiler_params=pltpu.CompilerParams(vmem_limit_bytes=VMEM),
         cost_estimate=pl.CostEstimate(
@@ -169,10 +169,21 @@
     scaled_mine, scaled_theirs = mine_and_theirs(scaled)
 
     blocks = terms(here, hidden, swap(hidden), scaled_mine, swap(scaled_theirs))
-    *parts, state_peer = together(*[far(blocks[s], s) for s in (2, 1, 3)], swap(state_theirs))
-    parts = [blocks[0], *parts]
+    tops, bottoms = blocks[:N], blocks[N:]
+    from_one, from_three = far(bottoms[1], 1), far(tops[3], 3)
+    over_three, over_one = together(far(tops[2], 3), far(bottoms[2], 1))
+    to_one, to_three = together(
+        total([tops[1], over_three]).astype(jnp.bfloat16),
+        total([bottoms[3], over_one]).astype(jnp.bfloat16),
+    )
+    from_one, from_three, both_one, both_three, state_peer = together(
+        from_one, from_three, far(to_one, 1), far(to_three, 3), swap(state_theirs)
+    )
     state_chip = in_core_order(state_mine, state_peer, 1)
-    sums = [total([part[s * BLOCK : (s + 1) * BLOCK] for part in parts]) for s in range(N)]
+    halves = [[tops[0], both_one, from_three], [bottoms[0], from_one, both_three]]
+    sums = [
+        total([part[s % 2 * BLOCK : (s % 2 + 1) * BLOCK] for part in halves[s // 2]]) for s in range(N)
+    ]
     sums = together(sums[0], *[sums[s].astype(jnp.bfloat16) for s in (2, 1, 3)])
     parts = [sums[0], *together(*[near(value, s) for value, s in zip(sums[1:], (2, 1, 3))])]
     plane_sum = total(parts).astype(jnp.bfloat16)

time: 120 us -> 116 us (0.967)
  waiting for transfers between devices: 60 us -> 52.7 us
  starting transfers between devices: 44.8 us -> 48.4 us
    ppermute x12 -> x15, waiting for transfers between devices: 39.9 us -> 32.6 us  [in_plane(): return lax.ppermute(value, ('xlo', 'y', 'xhi', 'core'), pairs)]
    ppermute x12 -> x15, starting transfers between devices: 13.8 us -> 16.4 us  [in_plane(): return lax.ppermute(value, ('xlo', 'y', 'xhi', 'core'), pairs)]
  transfers between devices with their start and end apart: 22 -> 25, of which waited for: 13 -> 13; matrix products, arithmetic and copies ran while one was open for 1% -> 1% of each run, Pallas kernels for 4% -> 4%
where the time goes in v6:
time: 116 us
  waiting for transfers between devices  52.7 us (45%)
  starting transfers between devices  48.4 us (42%)
  Pallas kernels  8.03 us (7%)
  local copies, waits for them, and re-layouts  2.57 us (2%)
  other arithmetic  2.12 us (2%)
  matrix products  1.17 us (1%)
    ppermute x15, waiting for transfers between devices, in_plane(): return lax.ppermute(value, ('xlo', 'y', 'xhi', 'core'), pairs)  32.6 us
    ppermute x8, starting transfers between devices, swap(): return lax.ppermute(value, 'core', SWAP)  20.6 us
    ppermute x15, starting transfers between devices, in_plane(): return lax.ppermute(value, ('xlo', 'y', 'xhi', 'core'), pairs)  16.4 us
    all_to_all x1, waiting for transfers between devices, shards(): lax.all_to_all(plane_sum.reshape(N_Z, BLOCK // N_Z, half), 'z', 0, 0)  8.92 us
    all_to_all x1, waiting for transfers between devices, shards(): lax.all_to_all(jnp.broadcast_to(piece, (N_Z,) + piece.shape), 'z', 0, 0)  8.81 us
    all_to_all x1, starting transfers between devices, shards(): lax.all_to_all(plane_sum.reshape(N_Z, BLOCK // N_Z, half), 'z', 0, 0)  7.98 us
    pallas_call x3, Pallas kernels, join(): pl.pallas_call(functools.partial(join_kernel, tuple((item[1:] for item in...  6.2 us
    all_to_all x1, starting transfers between devices, shards(): lax.all_to_all(jnp.broadcast_to(piece, (N_Z,) + piece.shape), 'z', 0, 0)  3.4 us
  transfers between devices with their start and end apart: 25, of which 13 were waited for; matrix products, arithmetic and copies ran while one was open for 1% of the time, Pallas kernels for 4%

profile of v6, /device:TPU:1, one launch (start us, length us, event | category | flops | bytes accessed | tf_op | source)
XLA Modules:
  0.0 116.0 jit_solution(15121263451068466602)
XLA Ops:
  0.7 1.2 %copy-done = bf16[128,3584]{1,0:T(8,128)(2,1)S(1)} copy-done((bf16[128,3584]{1,0:T(8,128)(2,1)S(1)}, bf16[128,3584]{1,0:T(8,128)(2,1)}, u32[]{:S(2)}) %copy-start) | copy-done | bytes 917528
  1.8 1.2 %fusion = bf16[128,3584]{1,0:T(8,128)(2,1)S(1)} fusion(bf16[128,3584]{1,0:T(8,128)(2,1)S(1)} %copy-done, f32[128]{0:T(128)} %param.11, s32[128]{0:T(128)} %param.12), kind=kOutput, calls=%fused_computation.1 | convolution fusion | flops 118374400 | bytes 1836032 | tf_op jit(solution)/shard_map/dot_general | solution.py:167
  3.1 3.3 %collective-permute-start.1 = (bf16[128,1792]{1,0:T(8,128)(2,1)S(1)}, bf16[128,1792]{1,0:T(8,128)(2,1)S(1)}, u32[]{:S(2)}, u32[]{:S(2)}) collective-permute-start(bf16[128,1792]{1,0:T(8,128)(2,1)S(1)} %get-tuple-element.89), channel_id=1, source_target_pairs={{0,1},{1,0},{2,3},{3,2},{4,5},{5,4},{6,7},{7,6},{8,9},{9,8},{10,11... | collective-permute-start | bytes 1376264 | tf_op jit(solution)/shard_map/ppermute | solution.py:46
  6.8 1.4 %collective-permute-done.hidden_peer = bf16[128,1024]{1,0:T(8,128)(2,1)S(1)} collective-permute-done((bf16[128,1024]{1,0:T(8,128)(2,1)S(1)}, bf16[128,1024]{1,0:T(8,128)(2,1)S(1)}, u32[]{:S(2)}, u32[]{:S(2)}) %collective-permute-start) | collective-permute-done | bytes 262176 | tf_op jit(solution)/shard_map/ppermute | solution.py:46
  8.2 1.8 %shard_map.111 = (bf16[128,1792]{1,0:T(8,128)(2,1)S(1)}, bf16[128,1792]{1,0:T(8,128)(2,1)S(1)}, bf16[128,1792]{1,0:T(8,128)(2,1)S(1)}, bf16[128,1792]{1,0:T(8,12...) custom-call(s32[3]{0:T(128)S(1)} %pad_add_fusion.here, ...), custom_call_target="tpu_custom_call" | custom-call | flops 939524096 | bytes 5000000 | tf_op jit(solution)/shard_map/pallas_call | solution.py:72
  10.1 0.8 collective-permute-start.4
  11.0 1.5 %collective-permute-start.2 = (bf16[128,1792]{1,0:T(8,128)(2,1)S(1)}, bf16[128,1792]{1,0:T(8,128)(2,1)S(1)}, u32[]{:S(2)}, u32[]{:S(2)}) collective-permute-start(bf16[128,1792]{1,0:T(8,128)(2,1)S(1)} %get-tuple-element.43), channel_id=1, source_target_pairs={{0,32},{1,129},{32,0},{33,161},{64,96},{65,193},{96,64},{97,225},{... | collective-permute-start | bytes 1376264 | tf_op jit(solution)/shard_map/ppermute | solution.py:34
  12.5 1.9 %collective-permute-start.3 = (bf16[128,1792]{1,0:T(8,128)(2,1)S(1)}, bf16[128,1792]{1,0:T(8,128)(2,1)S(1)}, u32[]{:S(2)}, u32[]{:S(2)}) collective-permute-start(bf16[128,1792]{1,0:T(8,128)(2,1)S(1)} %get-tuple-element.44), channel_id=1, source_target_pairs={{0,96},{1,145},{32,64},{33,177},{64,32},{65,209},{96,0},{97,241},{... | collective-permute-start | bytes 1376264 | tf_op jit(solution)/shard_map/ppermute | solution.py:34
  14.4 4.5 %collective-permute-done.4 = bf16[128,1792]{1,0:T(8,128)(2,1)S(1)} collective-permute-done((bf16[128,1792]{1,0:T(8,128)(2,1)S(1)}, bf16[128,1792]{1,0:T(8,128)(2,1)S(1)}, u32[]{:S(2)}, u32[]{:S(2)}) %collective-permute-start.4) | collective-permute-done | bytes 458784 | tf_op jit(solution)/shard_map/ppermute | solution.py:34
  19.3 1.5 %collective-permute-start.7 = (bf16[128,1792]{1,0:T(8,128)(2,1)S(1)}, bf16[128,1792]{1,0:T(8,128)(2,1)S(1)}, u32[]{:S(2)}, u32[]{:S(2)}) collective-permute-start(bf16[128,1792]{1,0:T(8,128)(2,1)S(1)} %get-tuple-element.52), channel_id=1, source_target_pairs={{0,96},{1,145},{32,64},{33,177},{64,32},{65,209},{96,0},{97,241},{... | collective-permute-start | bytes 1376264 | tf_op jit(solution)/shard_map/ppermute | solution.py:34
  20.9 1.9 %collective-permute-start.8 = (f32[3,4,1792]{2,1,0:T(4,128)S(1)}, f32[3,4,1792]{2,1,0:T(4,128)S(1)}, u32[]{:S(2)}, u32[]{:S(2)}) collective-permute-start(f32[3,4,1792]{2,1,0:T(4,128)S(1)} %get-tuple-element.97), channel_id=1, source_target_pairs={{0,1},{1,0},{2,3},{3,2},{4,5},{5,4},{6,7},{7,6},{8,9},{9,8},{10,11... | collective-permute-start | bytes 258056 | tf_op jit(solution)/shard_map/ppermute | solution.py:46
  22.8 0.9 collective-permute-done.8
  23.9 4.5 %collective-permute-done.6 = bf16[128,1792]{1,0:T(8,128)(2,1)S(1)} collective-permute-done((bf16[128,1792]{1,0:T(8,128)(2,1)S(1)}, bf16[128,1792]{1,0:T(8,128)(2,1)S(1)}, u32[]{:S(2)}, u32[]{:S(2)}) %collective-permute-start.6) | collective-permute-done | bytes 458784 | tf_op jit(solution)/shard_map/ppermute | solution.py:34
  29.2 2.5 %collective-permute-start.9 = (bf16[64,1792]{1,0:T(8,128)(2,1)S(1)}, bf16[64,1792]{1,0:T(8,128)(2,1)S(1)}, u32[]{:S(2)}, u32[]{:S(2)}) collective-permute-start(bf16[64,1792]{1,0:T(8,128)(2,1)S(1)} %get-tuple-element.61), channel_id=1, source_target_pairs={{0,16},{1,65},{32,48},{33,97},{64,80},{65,1},{96,112},{97,33},{128... | collective-permute-start | bytes 688136 | tf_op jit(solution)/shard_map/ppermute | solution.py:34
  32.5 3.4 %collective-permute-done.9 = bf16[64,1792]{1,0:T(8,128)(2,1)S(1)} collective-permute-done((bf16[64,1792]{1,0:T(8,128)(2,1)S(1)}, bf16[64,1792]{1,0:T(8,128)(2,1)S(1)}, u32[]{:S(2)}, u32[]{:S(2)}) %collective-permute-start.9) | collective-permute-done | bytes 229408 | tf_op jit(solution)/shard_map/ppermute | solution.py:34
  35.9 2.4 %collective-permute-done.10 = bf16[64,1792]{1,0:T(8,128)(2,1)S(1)} collective-permute-done((bf16[64,1792]{1,0:T(8,128)(2,1)S(1)}, bf16[64,1792]{1,0:T(8,128)(2,1)S(1)}, u32[]{:S(2)}, u32[]{:S(2)}) %collective-permute-start.10) | collective-permute-done | bytes 229408 | tf_op jit(solution)/shard_map/ppermute | solution.py:34
  38.3 0.8 fusion.6
  39.1 8.0 %all-to-all-start = ((bf16[8,8,1792]{2,1,0:T(8,128)(2,1)}), bf16[8,8,1792]{2,1,0:T(8,128)(2,1)S(1)}, u32[]{:S(2)}, u32[]{:S(2)}) async-start(bf16[8,8,1792]{2,1,0:T(8,128)(2,1)} %fusion.6), calls=%async_computation | async-start | bytes 458752 | tf_op jit(solution)/shard_map/all_to_all | solution.py:190
  47.2 8.9 %all-to-all-done = bf16[8,8,1792]{2,1,0:T(8,128)(2,1)S(1)} async-done(((bf16[8,8,1792]{2,1,0:T(8,128)(2,1)}), bf16[8,8,1792]{2,1,0:T(8,128)(2,1)S(1)}, u32[]{:S(2)}, u32[]{:S(2)}) %all-to-all-start) | async-done | bytes 229408 | tf_op jit(solution)/shard_map/all_to_all | solution.py:190
  56.9 3.4 %all-to-all-start.1 = ((bf16[8,8,1792]{2,1,0:T(8,128)(2,1)}), bf16[8,8,1792]{2,1,0:T(8,128)(2,1)S(1)}, u32[]{:S(2)}, u32[]{:S(2)}) async-start(bf16[8,8,1792]{2,1,0:T(8,128)(2,1)} %broadcast_in_dim.2), calls=%async_computation.1 | async-start | bytes 458752 | tf_op jit(solution)/shard_map/all_to_all | solution.py:207
  60.4 8.8 %all-to-all-done.1 = bf16[8,8,1792]{2,1,0:T(8,128)(2,1)S(1)} async-done(((bf16[8,8,1792]{2,1,0:T(8,128)(2,1)}), bf16[8,8,1792]{2,1,0:T(8,128)(2,1)S(1)}, u32[]{:S(2)}, u32[]{:S(2)}) %all-to-all-start.1) | async-done | bytes 229408 | tf_op jit(solution)/shard_map/all_to_all | solution.py:207
  69.2 2.6 %collective-permute-start.14 = (bf16[64,1792]{1,0:T(8,128)(2,1)S(1)}, bf16[64,1792]{1,0:T(8,128)(2,1)S(1)}, u32[]{:S(2)}, u32[]{:S(2)}) collective-permute-start(bf16[64,1792]{1,0:T(8,128)(2,1)S(1)} %bitcast.44), channel_id=1, source_target_pairs={{0,144},{1,97},{32,176},{33,65},{64,208},{65,33},{96,240},{97,1},{... | collective-permute-start | bytes 688136 | tf_op jit(solution)/shard_map/ppermute | solution.py:34
  72.5 7.3 %collective-permute-start.19 = (f32[3,4,1792]{2,1,0:T(4,128)S(1)}, f32[3,4,1792]{2,1,0:T(4,128)S(1)}, u32[]{:S(2)}, u32[]{:S(2)}) collective-permute-start(f32[3,4,1792]{2,1,0:T(4,128)S(1)} %get-tuple-element.95), channel_id=1, source_target_pairs={{0,1},{1,0},{2,3},{3,2},{4,5},{5,4},{6,7},{7,6},{8,9},{9,8},{10,11... | collective-permute-start | bytes 258056 | tf_op jit(solution)/shard_map/ppermute | solution.py:46
  79.8 6.3 %collective-permute-start.18 = (bf16[256,1792]{1,0:T(8,128)(2,1)S(1)}, bf16[256,1792]{1,0:T(8,128)(2,1)S(1)}, u32[]{:S(2)}, u32[]{:S(2)}) collective-permute-start(bf16[256,1792]{1,0:T(8,128)(2,1)S(1)} %pad_maximum_fusion.refs_0_), channel_id=1, source_target_pairs={{0,1},{1,0},{2,3},{3,2},{4,5},{5,4},{6,7},{7,6},{8,9},{9,8},{10,11... | collective-permute-start | bytes 2752520 | tf_op jit(solution)/shard_map/ppermute | solution.py:46
  86.1 1.6 %collective-permute-start.17 = (bf16[256,1792]{1,0:T(8,128)(2,1)S(1)}, bf16[256,1792]{1,0:T(8,128)(2,1)S(1)}, u32[]{:S(2)}, u32[]{:S(2)}) collective-permute-start(bf16[256,1792]{1,0:T(8,128)(2,1)S(1)} %pad_maximum_fusion.refs_0_), channel_id=1, source_target_pairs={{0,96},{1,145},{32,64},{33,177},{64,32},{65,209},{96,0},{97,241},{... | collective-permute-start | bytes 2752520 | tf_op jit(solution)/shard_map/ppermute | solution.py:34
  88.4 2.2 %collective-permute-start.15 = (bf16[256,1792]{1,0:T(8,128)(2,1)S(1)}, bf16[256,1792]{1,0:T(8,128)(2,1)S(1)}, u32[]{:S(2)}, u32[]{:S(2)}) collective-permute-start(bf16[256,1792]{1,0:T(8,128)(2,1)S(1)} %pad_maximum_fusion.refs_0_), channel_id=1, source_target_pairs={{0,64},{1,17},{32,96},{33,49},{64,0},{65,81},{96,32},{97,113},{128... | collective-permute-start | bytes 2752520 | tf_op jit(solution)/shard_map/ppermute | solution.py:34
  90.7 9.2 %collective-permute-done.17.refs_2_ = bf16[256,1792]{1,0:T(8,128)(2,1)S(1)} collective-permute-done((bf16[256,1792]{1,0:T(8,128)(2,1)S(1)}, bf16[256,1792]{1,0:T(8,128)(2,1)S(1)}, u32[]{:S(2)}, u32[]{:S(2)}) %collective-permute-start.17) | collective-permute-done | bytes 917536 | tf_op jit(solution)/shard_map/ppermute | solution.py:34
  100.8 2.5 %shard_map.112.refs_3_ = bf16[1024,3584]{1,0:T(8,128)(2,1)} custom-call(s32[3]{0:T(128)S(1)} %pad_add_fusion.here, bf16[256,1792]{1,0:T(8,128)(2,1)S(1)} %pad_maximum_fusion.refs_0_, bf16[256,1792]{1,0:T(8,128)(2,1)S(1)} %collective-permute-done.16.refs_1_, bf16[256,1792]{1,0:T(8,128)(2,1)S(1)} %collective-permute-done.17.refs_2_, ...), custom_call_target="tpu_custom_call" | custom-call | bytes 7340032 | tf_op jit(solution)/shard_map/pallas_call | solution.py:114
  103.3 7.5 %collective-permute-done.15.refs_0_ = bf16[256,1792]{1,0:T(8,128)(2,1)S(1)} collective-permute-done((bf16[256,1792]{1,0:T(8,128)(2,1)S(1)}, bf16[256,1792]{1,0:T(8,128)(2,1)S(1)}, u32[]{:S(2)}, u32[]{:S(2)}) %collective-permute-start.15) | collective-permute-done | bytes 917536 | tf_op jit(solution)/shard_map/ppermute | solution.py:34
  110.9 1.2 %collective-permute-start.22 = (bf16[256,1792]{1,0:T(8,128)(2,1)S(1)}, bf16[256,1792]{1,0:T(8,128)(2,1)S(1)}, u32[]{:S(2)}, u32[]{:S(2)}) collective-permute-start(bf16[256,1792]{1,0:T(8,128)(2,1)S(1)} %collective-permute-done.15.refs_0_), channel_id=1, source_target_pairs={{0,1},{1,0},{2,3},{3,2},{4,5},{5,4},{6,7},{7,6},{8,9},{9,8},{10,11... | collective-permute-start | bytes 2752520 | tf_op jit(solution)/shard_map/ppermute | solution.py:46
  112.1 2.2 %shard_map.113.refs_1_ = bf16[1024,3584]{1,0:T(8,128)(2,1)} custom-call(s32[3]{0:T(128)S(1)} %pad_add_fusion.here, bf16[256,1792]{1,0:T(8,128)(2,1)S(1)} %collective-permute-done.15.refs_0_, bf16[256,1792]{1,0:T(8,128)(2,1)S(1)} %collective-permute-done.20.refs_1_, ...), custom_call_target="tpu_custom_call", output_to_operand_aliasing={{}: (4, {})} | custom-call | bytes 5505024 | tf_op jit(solution)/shard_map/pallas_call | solution.py:114
  114.3 1.5 %shard_map.114 = bf16[1024,3584]{1,0:T(8,128)(2,1)} custom-call(s32[3]{0:T(128)S(1)} %pad_add_fusion.here, bf16[256,1792]{1,0:T(8,128)(2,1)S(1)} %collective-permute-done.22.refs_0_, bf16[1024,3584]{1,0:T(8,128)(2,1)} %shard_map.113.refs_1_), custom_call_target="tpu_custom_call", output_to_operand_aliasing={{}: (2, {})} | custom-call | bytes 1835008 | tf_op jit(solution)/shard_map/pallas_call | solution.py:114
  (54 shorter events, 6.1 us)
Async XLA Ops:
  0.6 1.2 %copy-start = (bf16[128,3584]{1,0:T(8,128)(2,1)S(1)}, bf16[128,3584]{1,0:T(8,128)(2,1)}, u32[]{:S(2)}) copy-start(bf16[128,3584]{1,0:T(8,128)(2,1)} %param.10) | copy-start | bytes 2752516
  1.8 4.6 %copy-start.1 = (bf16[128,1024]{1,0:T(8,128)(2,1)S(1)}, bf16[128,1024]{1,0:T(8,128)(2,1)}, u32[]{:S(2)}) copy-start(bf16[128,1024]{1,0:T(8,128)(2,1)} %param.9) | copy-start | bytes 786436
  1.8 4.6 %copy-start.2 = (bf16[128,1024]{1,0:T(8,128)(2,1)S(1)}, bf16[128,1024]{1,0:T(8,128)(2,1)}, u32[]{:S(2)}) copy-start(bf16[128,1024]{1,0:T(8,128)(2,1)} %param.8) | copy-start | bytes 786436
  3.1 5.2 %collective-permute-start.1 = (bf16[128,1792]{1,0:T(8,128)(2,1)S(1)}, bf16[128,1792]{1,0:T(8,128)(2,1)S(1)}, u32[]{:S(2)}, u32[]{:S(2)}) collective-permute-start(bf16[128,1792]{1,0:T(8,128)(2,1)S(1)} %get-tuple-element.89), channel_id=1, source_target_pairs={{0,1},{1,0},{2,3},{3,2},{4,5},{5,4},{6,7},{7,6},{8,9},{9,8},{10,11... | collective-permute-start | bytes 1376264 | tf_op jit(solution)/shard_map/ppermute | solution.py:46
  6.6 4.3 %copy-start.3 = (f32[4,3584]{1,0:T(4,128)S(1)}, f32[4,3584]{1,0:T(4,128)}, u32[]{:S(2)}) copy-start(f32[4,3584]{1,0:T(4,128)} %param.15) | copy-start | bytes 172036
  6.6 4.3 %copy-start.4 = (f32[4,3584]{1,0:T(4,128)S(1)}, f32[4,3584]{1,0:T(4,128)}, u32[]{:S(2)}) copy-start(f32[4,3584]{1,0:T(4,128)} %param.14) | copy-start | bytes 172036
  6.6 4.3 %copy-start.5 = (f32[4,3584]{1,0:T(4,128)S(1)}, f32[4,3584]{1,0:T(4,128)}, u32[]{:S(2)}) copy-start(f32[4,3584]{1,0:T(4,128)} %param.13) | copy-start | bytes 172036
  6.6 1.6 %collective-permute-start = (bf16[128,1024]{1,0:T(8,128)(2,1)S(1)}, bf16[128,1024]{1,0:T(8,128)(2,1)S(1)}, u32[]{:S(2)}, u32[]{:S(2)}) collective-permute-start(bf16[128,1024]{1,0:T(8,128)(2,1)S(1)} %fusion.5.hidden), channel_id=1, source_target_pairs={{0,1},{1,0},{2,3},{3,2},{4,5},{5,4},{6,7},{7,6},{8,9},{9,8},{10,11... | collective-permute-start | bytes 786440 | tf_op jit(solution)/shard_map/ppermute | solution.py:46
  10.1 8.9 %collective-permute-start.4 = (bf16[128,1792]{1,0:T(8,128)(2,1)S(1)}, bf16[128,1792]{1,0:T(8,128)(2,1)S(1)}, u32[]{:S(2)}, u32[]{:S(2)}) collective-permute-start(bf16[128,1792]{1,0:T(8,128)(2,1)S(1)} %get-tuple-element.46), channel_id=1, source_target_pairs={{0,96},{1,145},{32,64},{33,177},{64,32},{65,209},{96,0},{97,241},{... | collective-permute-start | bytes 1376264 | tf_op jit(solution)/shard_map/ppermute | solution.py:34
  10.9 8.1 %collective-permute-start.5 = (bf16[128,1792]{1,0:T(8,128)(2,1)S(1)}, bf16[128,1792]{1,0:T(8,128)(2,1)S(1)}, u32[]{:S(2)}, u32[]{:S(2)}) collective-permute-start(bf16[128,1792]{1,0:T(8,128)(2,1)S(1)} %get-tuple-element.47), channel_id=1, source_target_pairs={{0,32},{1,129},{32,0},{33,161},{64,96},{65,193},{96,64},{97,225},{... | collective-permute-start | bytes 1376264 | tf_op jit(solution)/shard_map/ppermute | solution.py:34
  11.0 12.7 %collective-permute-start.2 = (bf16[128,1792]{1,0:T(8,128)(2,1)S(1)}, bf16[128,1792]{1,0:T(8,128)(2,1)S(1)}, u32[]{:S(2)}, u32[]{:S(2)}) collective-permute-start(bf16[128,1792]{1,0:T(8,128)(2,1)S(1)} %get-tuple-element.43), channel_id=1, source_target_pairs={{0,32},{1,129},{32,0},{33,161},{64,96},{65,193},{96,64},{97,225},{... | collective-permute-start | bytes 1376264 | tf_op jit(solution)/shard_map/ppermute | solution.py:34
  12.5 11.4 %collective-permute-start.3 = (bf16[128,1792]{1,0:T(8,128)(2,1)S(1)}, bf16[128,1792]{1,0:T(8,128)(2,1)S(1)}, u32[]{:S(2)}, u32[]{:S(2)}) collective-permute-start(bf16[128,1792]{1,0:T(8,128)(2,1)S(1)} %get-tuple-element.44), channel_id=1, source_target_pairs={{0,96},{1,145},{32,64},{33,177},{64,32},{65,209},{96,0},{97,241},{... | collective-permute-start | bytes 1376264 | tf_op jit(solution)/shard_map/ppermute | solution.py:34
  19.2 9.1 %collective-permute-start.6 = (bf16[128,1792]{1,0:T(8,128)(2,1)S(1)}, bf16[128,1792]{1,0:T(8,128)(2,1)S(1)}, u32[]{:S(2)}, u32[]{:S(2)}) collective-permute-start(bf16[128,1792]{1,0:T(8,128)(2,1)S(1)} %get-tuple-element.51), channel_id=1, source_target_pairs={{0,32},{1,129},{32,0},{33,161},{64,96},{65,193},{96,64},{97,225},{... | collective-permute-start | bytes 1376264 | tf_op jit(solution)/shard_map/ppermute | solution.py:34
  19.3 9.5 %collective-permute-start.7 = (bf16[128,1792]{1,0:T(8,128)(2,1)S(1)}, bf16[128,1792]{1,0:T(8,128)(2,1)S(1)}, u32[]{:S(2)}, u32[]{:S(2)}) collective-permute-start(bf16[128,1792]{1,0:T(8,128)(2,1)S(1)} %get-tuple-element.52), channel_id=1, source_target_pairs={{0,96},{1,145},{32,64},{33,177},{64,32},{65,209},{96,0},{97,241},{... | collective-permute-start | bytes 1376264 | tf_op jit(solution)/shard_map/ppermute | solution.py:34
  20.9 2.8 %collective-permute-start.8 = (f32[3,4,1792]{2,1,0:T(4,128)S(1)}, f32[3,4,1792]{2,1,0:T(4,128)S(1)}, u32[]{:S(2)}, u32[]{:S(2)}) collective-permute-start(f32[3,4,1792]{2,1,0:T(4,128)S(1)} %get-tuple-element.97), channel_id=1, source_target_pairs={{0,1},{1,0},{2,3},{3,2},{4,5},{5,4},{6,7},{7,6},{8,9},{9,8},{10,11... | collective-permute-start | bytes 258056 | tf_op jit(solution)/shard_map/ppermute | solution.py:46
  29.2 6.8 %collective-permute-start.9 = (bf16[64,1792]{1,0:T(8,128)(2,1)S(1)}, bf16[64,1792]{1,0:T(8,128)(2,1)S(1)}, u32[]{:S(2)}, u32[]{:S(2)}) collective-permute-start(bf16[64,1792]{1,0:T(8,128)(2,1)S(1)} %get-tuple-element.61), channel_id=1, source_target_pairs={{0,16},{1,65},{32,48},{33,97},{64,80},{65,1},{96,112},{97,33},{128... | collective-permute-start | bytes 688136 | tf_op jit(solution)/shard_map/ppermute | solution.py:34
  31.7 6.6 %collective-permute-start.10 = (bf16[64,1792]{1,0:T(8,128)(2,1)S(1)}, bf16[64,1792]{1,0:T(8,128)(2,1)S(1)}, u32[]{:S(2)}, u32[]{:S(2)}) collective-permute-start(bf16[64,1792]{1,0:T(8,128)(2,1)S(1)} %get-tuple-element.62), channel_id=1, source_target_pairs={{0,128},{1,33},{32,160},{33,1},{64,192},{65,97},{96,224},{97,65},{... | collective-permute-start | bytes 688136 | tf_op jit(solution)/shard_map/ppermute | solution.py:34
  32.1 6.2 %collective-permute-start.11 = (bf16[64,1792]{1,0:T(8,128)(2,1)S(1)}, bf16[64,1792]{1,0:T(8,128)(2,1)S(1)}, u32[]{:S(2)}, u32[]{:S(2)}) collective-permute-start(bf16[64,1792]{1,0:T(8,128)(2,1)S(1)} %get-tuple-element.63), channel_id=1, source_target_pairs={{0,144},{1,97},{32,176},{33,65},{64,208},{65,33},{96,240},{97,1},{... | collective-permute-start | bytes 688136 | tf_op jit(solution)/shard_map/ppermute | solution.py:34
  39.1 17.0 %all-to-all-start = ((bf16[8,8,1792]{2,1,0:T(8,128)(2,1)}), bf16[8,8,1792]{2,1,0:T(8,128)(2,1)S(1)}, u32[]{:S(2)}, u32[]{:S(2)}) async-start(bf16[8,8,1792]{2,1,0:T(8,128)(2,1)} %fusion.6), calls=%async_computation | async-start | bytes 458752 | tf_op jit(solution)/shard_map/all_to_all | solution.py:190
  56.9 12.3 %all-to-all-start.1 = ((bf16[8,8,1792]{2,1,0:T(8,128)(2,1)}), bf16[8,8,1792]{2,1,0:T(8,128)(2,1)S(1)}, u32[]{:S(2)}, u32[]{:S(2)}) async-start(bf16[8,8,1792]{2,1,0:T(8,128)(2,1)} %broadcast_in_dim.2), calls=%async_computation.1 | async-start | bytes 458752 | tf_op jit(solution)/shard_map/all_to_all | solution.py:207
  69.2 10.6 %collective-permute-start.14 = (bf16[64,1792]{1,0:T(8,128)(2,1)S(1)}, bf16[64,1792]{1,0:T(8,128)(2,1)S(1)}, u32[]{:S(2)}, u32[]{:S(2)}) collective-permute-start(bf16[64,1792]{1,0:T(8,128)(2,1)S(1)} %bitcast.44), channel_id=1, source_target_pairs={{0,144},{1,97},{32,176},{33,65},{64,208},{65,33},{96,240},{97,1},{... | collective-permute-start | bytes 688136 | tf_op jit(solution)/shard_map/ppermute | solution.py:34
  71.8 8.0 %collective-permute-start.13 = (bf16[64,1792]{1,0:T(8,128)(2,1)S(1)}, bf16[64,1792]{1,0:T(8,128)(2,1)S(1)}, u32[]{:S(2)}, u32[]{:S(2)}) collective-permute-start(bf16[64,1792]{1,0:T(8,128)(2,1)S(1)} %bitcast.45), channel_id=1, source_target_pairs={{0,16},{1,65},{32,48},{33,97},{64,80},{65,1},{96,112},{97,33},{128... | collective-permute-start | bytes 688136 | tf_op jit(solution)/shard_map/ppermute | solution.py:34
  72.2 7.5 %collective-permute-start.12 = (bf16[64,1792]{1,0:T(8,128)(2,1)S(1)}, bf16[64,1792]{1,0:T(8,128)(2,1)S(1)}, u32[]{:S(2)}, u32[]{:S(2)}) collective-permute-start(bf16[64,1792]{1,0:T(8,128)(2,1)S(1)} %bitcast.46), channel_id=1, source_target_pairs={{0,128},{1,33},{32,160},{33,1},{64,192},{65,97},{96,224},{97,65},{... | collective-permute-start | bytes 688136 | tf_op jit(solution)/shard_map/ppermute | solution.py:34
  72.5 15.2 %collective-permute-start.19 = (f32[3,4,1792]{2,1,0:T(4,128)S(1)}, f32[3,4,1792]{2,1,0:T(4,128)S(1)}, u32[]{:S(2)}, u32[]{:S(2)}) collective-permute-start(f32[3,4,1792]{2,1,0:T(4,128)S(1)} %get-tuple-element.95), channel_id=1, source_target_pairs={{0,1},{1,0},{2,3},{3,2},{4,5},{5,4},{6,7},{7,6},{8,9},{9,8},{10,11... | collective-permute-start | bytes 258056 | tf_op jit(solution)/shard_map/ppermute | solution.py:46
  79.8 10.8 %collective-permute-start.18 = (bf16[256,1792]{1,0:T(8,128)(2,1)S(1)}, bf16[256,1792]{1,0:T(8,128)(2,1)S(1)}, u32[]{:S(2)}, u32[]{:S(2)}) collective-permute-start(bf16[256,1792]{1,0:T(8,128)(2,1)S(1)} %pad_maximum_fusion.refs_0_), channel_id=1, source_target_pairs={{0,1},{1,0},{2,3},{3,2},{4,5},{5,4},{6,7},{7,6},{8,9},{9,8},{10,11... | collective-permute-start | bytes 2752520 | tf_op jit(solution)/shard_map/ppermute | solution.py:46
  86.1 13.8 %collective-permute-start.17 = (bf16[256,1792]{1,0:T(8,128)(2,1)S(1)}, bf16[256,1792]{1,0:T(8,128)(2,1)S(1)}, u32[]{:S(2)}, u32[]{:S(2)}) collective-permute-start(bf16[256,1792]{1,0:T(8,128)(2,1)S(1)} %pad_maximum_fusion.refs_0_), channel_id=1, source_target_pairs={{0,96},{1,145},{32,64},{33,177},{64,32},{65,209},{96,0},{97,241},{... | collective-permute-start | bytes 2752520 | tf_op jit(solution)/shard_map/ppermute | solution.py:34
  87.7 12.5 %collective-permute-start.16 = (bf16[256,1792]{1,0:T(8,128)(2,1)S(1)}, bf16[256,1792]{1,0:T(8,128)(2,1)S(1)}, u32[]{:S(2)}, u32[]{:S(2)}) collective-permute-start(bf16[256,1792]{1,0:T(8,128)(2,1)S(1)} %pad_maximum_fusion.refs_0_), channel_id=1, source_target_pairs={{0,32},{1,129},{32,0},{33,161},{64,96},{65,193},{96,64},{97,225},{... | collective-permute-start | bytes 2752520 | tf_op jit(solution)/shard_map/ppermute | solution.py:34
  88.4 22.4 %collective-permute-start.15 = (bf16[256,1792]{1,0:T(8,128)(2,1)S(1)}, bf16[256,1792]{1,0:T(8,128)(2,1)S(1)}, u32[]{:S(2)}, u32[]{:S(2)}) collective-permute-start(bf16[256,1792]{1,0:T(8,128)(2,1)S(1)} %pad_maximum_fusion.refs_0_), channel_id=1, source_target_pairs={{0,64},{1,17},{32,96},{33,49},{64,0},{65,81},{96,32},{97,113},{128... | collective-permute-start | bytes 2752520 | tf_op jit(solution)/shard_map/ppermute | solution.py:34
  100.3 10.6 %collective-permute-start.20 = (bf16[256,1792]{1,0:T(8,128)(2,1)S(1)}, bf16[256,1792]{1,0:T(8,128)(2,1)S(1)}, u32[]{:S(2)}, u32[]{:S(2)}) collective-permute-start(bf16[256,1792]{1,0:T(8,128)(2,1)S(1)} %collective-permute-done.16.refs_1_), channel_id=1, source_target_pairs={{0,1},{1,0},{2,3},{3,2},{4,5},{5,4},{6,7},{7,6},{8,9},{9,8},{10,11... | collective-permute-start | bytes 2752520 | tf_op jit(solution)/shard_map/ppermute | solution.py:46
  100.8 10.1 %collective-permute-start.21 = (bf16[256,1792]{1,0:T(8,128)(2,1)S(1)}, bf16[256,1792]{1,0:T(8,128)(2,1)S(1)}, u32[]{:S(2)}, u32[]{:S(2)}) collective-permute-start(bf16[256,1792]{1,0:T(8,128)(2,1)S(1)} %collective-permute-done.17.refs_2_), channel_id=1, source_target_pairs={{0,1},{1,0},{2,3},{3,2},{4,5},{5,4},{6,7},{7,6},{8,9},{9,8},{10,11... | collective-permute-start | bytes 2752520 | tf_op jit(solution)/shard_map/ppermute | solution.py:46
  110.9 3.4 %collective-permute-start.22 = (bf16[256,1792]{1,0:T(8,128)(2,1)S(1)}, bf16[256,1792]{1,0:T(8,128)(2,1)S(1)}, u32[]{:S(2)}, u32[]{:S(2)}) collective-permute-start(bf16[256,1792]{1,0:T(8,128)(2,1)S(1)} %collective-permute-done.15.refs_0_), channel_id=1, source_target_pairs={{0,1},{1,0},{2,3},{3,2},{4,5},{5,4},{6,7},{7,6},{8,9},{9,8},{10,11... | collective-permute-start | bytes 2752520 | tf_op jit(solution)/shard_map/ppermute | solution.py:46

commit v7 on v6

--- a/solution.py
+++ b/solution.py
@@ -207,16 +207,27 @@
     column = lax.all_to_all(jnp.broadcast_to(piece, (N_Z,) + piece.shape), "z", 0, 0)
     column = together(column.reshape(BLOCK, half))[0]
     parts = together(*[near(column, s) for s in (1, 2, 3)])
-    (plane,) = together(jnp.concatenate([column, *parts], 0))
-    two = far(plane, 2)
-    one, three, peer, *state_out = together(
-        far(plane, 1), far(plane, 3), swap(plane), *[state_out[k] for k in range(3)]
-    )
-    items = [(plane, 0, 0, 0), (one, 1, 0, 0), (three, 3, 0, 0), (peer, 0, 0, 1)]
-    two, one_peer, three_peer, weight = together(two, swap(one), swap(three), join(here, items))
-    items = [(two, 2, 0, 0), (one_peer, 1, 0, 1), (three_peer, 3, 0, 1)]
-    two_peer, weight = together(swap(two), join(here, items, weight))
-    weight = join(here, [(two_peer, 2, 0, 1)], weight)
+    top, bottom = together(jnp.concatenate([column, parts[0]], 0), jnp.concatenate(parts[1:], 0))
+    one_b, three_a = far(bottom, 1), far(top, 3)
+    one_a, three_b, top_peer, *state_out = together(
+        far(top, 1), far(bottom, 3), swap(top), *[state_out[k] for k in range(3)]
+    )
+    items = [(top, 0, 0, 0), (bottom, 0, 2, 0), (one_a, 1, 0, 0), (three_b, 3, 2, 0)]
+    items += [(top_peer, 0, 0, 1)]
+    one_b, three_a, two_a, two_b, bottom_peer, one_a, three_b, weight = together(
+        one_b, three_a, far(one_a, 3), far(three_b, 1), swap(bottom), one_a, three_b, join(here, items)
+    )
+    items = [(one_b, 1, 2, 0), (three_a, 3, 0, 0), (two_a, 2, 0, 0), (two_b, 2, 2, 0)]
+    items += [(bottom_peer, 0, 2, 1)]
+    one_a, three_b, one_b, three_a, two_a, two_b, weight = together(
+        *[swap(piece) for piece in (one_a, three_b, one_b, three_a)],
+        two_a,
+        two_b,
+        join(here, items, weight),
+    )
+    items = [(one_a, 1, 0, 1), (three_b, 3, 2, 1), (one_b, 1, 2, 1), (three_a, 3, 0, 1)]
+    two_a, two_b, weight = together(swap(two_a), swap(two_b), join(here, items, weight))
+    weight = join(here, [(two_a, 2, 0, 1), (two_b, 2, 2, 1)], weight)
     return (weight, state_out[0], state_out[1], state_out[2])
 
 

time: 116 us -> 117 us (level)
  waiting for transfers between devices: 52.7 us -> 47.9 us
  starting transfers between devices: 48.4 us -> 51.9 us
    all_to_all x1, waiting for transfers between devices: 8.81 us -> 4.57 us  [shards(): lax.all_to_all(jnp.broadcast_to(piece, (N_Z,) + piece.shape), 'z', 0, 0)]
    ppermute x8 -> x12, starting transfers between devices: 20.6 us -> 23 us  [swap(): return lax.ppermute(value, 'core', SWAP)]
    ppermute x15 -> x18, waiting for transfers between devices: 32.6 us -> 31.1 us  [in_plane(): return lax.ppermute(value, ('xlo', 'y', 'xhi', 'core'), pairs)]
    pallas_call x3 -> x4, Pallas kernels: 6.2 us -> 7.36 us  [join(): pl.pallas_call(functools.partial(join_kernel, tuple((item[1:] for item in...]
    ppermute x8 -> x12, waiting for transfers between devices: 2.37 us -> 3.35 us  [swap(): return lax.ppermute(value, 'core', SWAP)]
    ppermute x15 -> x18, starting transfers between devices: 16.4 us -> 17 us  [in_plane(): return lax.ppermute(value, ('xlo', 'y', 'xhi', 'core'), pairs)]
  transfers between devices with their start and end apart: 25 -> 32, of which waited for: 13 -> 20; matrix products, arithmetic and copies ran while one was open for 1% -> 2% of each run, Pallas kernels for 4% -> 5%
where the time goes in v7:
time: 117 us
  starting transfers between devices  51.9 us (44%)
  waiting for transfers between devices  47.9 us (41%)
  Pallas kernels  9.19 us (8%)
  other arithmetic  3.15 us (3%)
  local copies, waits for them, and re-layouts  2.52 us (2%)
    ppermute x18, waiting for transfers between devices, in_plane(): return lax.ppermute(value, ('xlo', 'y', 'xhi', 'core'), pairs)  31.1 us
    ppermute x12, starting transfers between devices, swap(): return lax.ppermute(value, 'core', SWAP)  23 us
    ppermute x18, starting transfers between devices, in_plane(): return lax.ppermute(value, ('xlo', 'y', 'xhi', 'core'), pairs)  17 us
    all_to_all x1, waiting for transfers between devices, shards(): lax.all_to_all(plane_sum.reshape(N_Z, BLOCK // N_Z, half), 'z', 0, 0)  8.94 us
    all_to_all x1, starting transfers between devices, shards(): lax.all_to_all(plane_sum.reshape(N_Z, BLOCK // N_Z, half), 'z', 0, 0)  8.49 us
    pallas_call x4, Pallas kernels, join(): pl.pallas_call(functools.partial(join_kernel, tuple((item[1:] for item in...  7.36 us
    all_to_all x1, waiting for transfers between devices, shards(): lax.all_to_all(jnp.broadcast_to(piece, (N_Z,) + piece.shape), 'z', 0, 0)  4.57 us
    all_to_all x1, starting transfers between devices, shards(): lax.all_to_all(jnp.broadcast_to(piece, (N_Z,) + piece.shape), 'z', 0, 0)  3.4 us
  transfers between devices with their start and end apart: 32, of which 20 were waited for; matrix products, arithmetic and copies ran while one was open for 2% of the time, Pallas kernels for 5%

profile of v7, /device:TPU:1, one launch (start us, length us, event | category | flops | bytes accessed | tf_op | source)
XLA Modules:
  0.0 116.9 jit_solution(15141267611547671115)
XLA Ops:
  0.7 1.1 copy-done
  3.0 3.3 %collective-permute-start.1 = (bf16[128,1792]{1,0:T(8,128)(2,1)S(1)}, bf16[128,1792]{1,0:T(8,128)(2,1)S(1)}, u32[]{:S(2)}, u32[]{:S(2)}) collective-permute-start(bf16[128,1792]{1,0:T(8,128)(2,1)S(1)} %get-tuple-element.117), channel_id=1, source_target_pairs={{0,1},{1,0},{2,3},{3,2},{4,5},{5,4},{6,7},{7,6},{8,9},{9,8},{10,11... | collective-permute-start | bytes 1376264 | tf_op jit(solution)/shard_map/ppermute | solution.py:46
  6.3 1.2 %fusion.5.hidden = bf16[128,1024]{1,0:T(8,128)(2,1)S(1)} fusion(bf16[128,1024]{1,0:T(8,128)(2,1)} %param.9, bf16[128,1024]{1,0:T(8,128)(2,1)} %param.8), kind=kLoop, calls=%fused_computation.10 | loop fusion | flops 1048576 | bytes 786432 | tf_op jit(solution)/shard_map/convert_element_type | solution.py:163
  7.7 1.4 %collective-permute-done.hidden_peer = bf16[128,1024]{1,0:T(8,128)(2,1)S(1)} collective-permute-done((bf16[128,1024]{1,0:T(8,128)(2,1)S(1)}, bf16[128,1024]{1,0:T(8,128)(2,1)S(1)}, u32[]{:S(2)}, u32[]{:S(2)}) %collective-permute-start) | collective-permute-done | bytes 262176 | tf_op jit(solution)/shard_map/ppermute | solution.py:46
  9.2 1.8 %shard_map.111 = (bf16[128,1792]{1,0:T(8,128)(2,1)S(1)}, bf16[128,1792]{1,0:T(8,128)(2,1)S(1)}, bf16[128,1792]{1,0:T(8,128)(2,1)S(1)}, bf16[128,1792]{1,0:T(8,12...) custom-call(s32[3]{0:T(128)S(1)} %pad_add_fusion.here, ...), custom_call_target="tpu_custom_call" | custom-call | flops 939524096 | bytes 5000000 | tf_op jit(solution)/shard_map/pallas_call | solution.py:72
  11.9 1.5 %collective-permute-start.2 = (bf16[128,1792]{1,0:T(8,128)(2,1)S(1)}, bf16[128,1792]{1,0:T(8,128)(2,1)S(1)}, u32[]{:S(2)}, u32[]{:S(2)}) collective-permute-start(bf16[128,1792]{1,0:T(8,128)(2,1)S(1)} %get-tuple-element.57), channel_id=1, source_target_pairs={{0,32},{1,129},{32,0},{33,161},{64,96},{65,193},{96,64},{97,225},{... | collective-permute-start | bytes 1376264 | tf_op jit(solution)/shard_map/ppermute | solution.py:34
  13.4 1.9 %collective-permute-start.3 = (bf16[128,1792]{1,0:T(8,128)(2,1)S(1)}, bf16[128,1792]{1,0:T(8,128)(2,1)S(1)}, u32[]{:S(2)}, u32[]{:S(2)}) collective-permute-start(bf16[128,1792]{1,0:T(8,128)(2,1)S(1)} %get-tuple-element.58), channel_id=1, source_target_pairs={{0,96},{1,145},{32,64},{33,177},{64,32},{65,209},{96,0},{97,241},{... | collective-permute-start | bytes 1376264 | tf_op jit(solution)/shard_map/ppermute | solution.py:34
  15.4 4.5 %collective-permute-done.4 = bf16[128,1792]{1,0:T(8,128)(2,1)S(1)} collective-permute-done((bf16[128,1792]{1,0:T(8,128)(2,1)S(1)}, bf16[128,1792]{1,0:T(8,128)(2,1)S(1)}, u32[]{:S(2)}, u32[]{:S(2)}) %collective-permute-start.4) | collective-permute-done | bytes 458784 | tf_op jit(solution)/shard_map/ppermute | solution.py:34
  20.2 1.5 %collective-permute-start.7 = (bf16[128,1792]{1,0:T(8,128)(2,1)S(1)}, bf16[128,1792]{1,0:T(8,128)(2,1)S(1)}, u32[]{:S(2)}, u32[]{:S(2)}) collective-permute-start(bf16[128,1792]{1,0:T(8,128)(2,1)S(1)} %get-tuple-element.66), channel_id=1, source_target_pairs={{0,96},{1,145},{32,64},{33,177},{64,32},{65,209},{96,0},{97,241},{... | collective-permute-start | bytes 1376264 | tf_op jit(solution)/shard_map/ppermute | solution.py:34
  21.8 1.6 %collective-permute-start.8 = (f32[3,4,1792]{2,1,0:T(4,128)S(1)}, f32[3,4,1792]{2,1,0:T(4,128)S(1)}, u32[]{:S(2)}, u32[]{:S(2)}) collective-permute-start(f32[3,4,1792]{2,1,0:T(4,128)S(1)} %get-tuple-element.125), channel_id=1, source_target_pairs={{0,1},{1,0},{2,3},{3,2},{4,5},{5,4},{6,7},{7,6},{8,9},{9,8},{10,11... | collective-permute-start | bytes 258056 | tf_op jit(solution)/shard_map/ppermute | solution.py:46
  24.8 4.4 %collective-permute-done.6 = bf16[128,1792]{1,0:T(8,128)(2,1)S(1)} collective-permute-done((bf16[128,1792]{1,0:T(8,128)(2,1)S(1)}, bf16[128,1792]{1,0:T(8,128)(2,1)S(1)}, u32[]{:S(2)}, u32[]{:S(2)}) %collective-permute-start.6) | collective-permute-done | bytes 458784 | tf_op jit(solution)/shard_map/ppermute | solution.py:34
  31.0 1.9 %collective-permute-start.11 = (bf16[64,1792]{1,0:T(8,128)(2,1)S(1)}, bf16[64,1792]{1,0:T(8,128)(2,1)S(1)}, u32[]{:S(2)}, u32[]{:S(2)}) collective-permute-start(bf16[64,1792]{1,0:T(8,128)(2,1)S(1)} %get-tuple-element.77), channel_id=1, source_target_pairs={{0,144},{1,97},{32,176},{33,65},{64,208},{65,33},{96,240},{97,1},{... | collective-permute-start | bytes 688136 | tf_op jit(solution)/shard_map/ppermute | solution.py:34
  33.6 1.7 %collective-permute-done.10 = bf16[64,1792]{1,0:T(8,128)(2,1)S(1)} collective-permute-done((bf16[64,1792]{1,0:T(8,128)(2,1)S(1)}, bf16[64,1792]{1,0:T(8,128)(2,1)S(1)}, u32[]{:S(2)}, u32[]{:S(2)}) %collective-permute-start.10) | collective-permute-done | bytes 229408 | tf_op jit(solution)/shard_map/ppermute | solution.py:34
  35.4 3.0 %collective-permute-done.11 = bf16[64,1792]{1,0:T(8,128)(2,1)S(1)} collective-permute-done((bf16[64,1792]{1,0:T(8,128)(2,1)S(1)}, bf16[64,1792]{1,0:T(8,128)(2,1)S(1)}, u32[]{:S(2)}, u32[]{:S(2)}) %collective-permute-start.11) | collective-permute-done | bytes 229408 | tf_op jit(solution)/shard_map/ppermute | solution.py:34
  38.4 1.2 %collective-permute-done.9 = bf16[64,1792]{1,0:T(8,128)(2,1)S(1)} collective-permute-done((bf16[64,1792]{1,0:T(8,128)(2,1)S(1)}, bf16[64,1792]{1,0:T(8,128)(2,1)S(1)}, u32[]{:S(2)}, u32[]{:S(2)}) %collective-permute-start.9) | collective-permute-done | bytes 229408 | tf_op jit(solution)/shard_map/ppermute | solution.py:34
  40.4 8.5 %all-to-all-start = ((bf16[8,8,1792]{2,1,0:T(8,128)(2,1)}), bf16[8,8,1792]{2,1,0:T(8,128)(2,1)S(1)}, u32[]{:S(2)}, u32[]{:S(2)}) async-start(bf16[8,8,1792]{2,1,0:T(8,128)(2,1)} %fusion.6), calls=%async_computation | async-start | bytes 458752 | tf_op jit(solution)/shard_map/all_to_all | solution.py:190
  48.9 8.9 %all-to-all-done = bf16[8,8,1792]{2,1,0:T(8,128)(2,1)S(1)} async-done(((bf16[8,8,1792]{2,1,0:T(8,128)(2,1)}), bf16[8,8,1792]{2,1,0:T(8,128)(2,1)S(1)}, u32[]{:S(2)}, u32[]{:S(2)}) %all-to-all-start) | async-done | bytes 229408 | tf_op jit(solution)/shard_map/all_to_all | solution.py:190
  58.7 3.4 %all-to-all-start.1 = ((bf16[8,8,1792]{2,1,0:T(8,128)(2,1)}), bf16[8,8,1792]{2,1,0:T(8,128)(2,1)S(1)}, u32[]{:S(2)}, u32[]{:S(2)}) async-start(bf16[8,8,1792]{2,1,0:T(8,128)(2,1)} %broadcast_in_dim.2), calls=%async_computation.1 | async-start | bytes 458752 | tf_op jit(solution)/shard_map/all_to_all | solution.py:207
  62.2 4.4 %collective-permute-start.20 = (f32[3,4,1792]{2,1,0:T(4,128)S(1)}, f32[3,4,1792]{2,1,0:T(4,128)S(1)}, u32[]{:S(2)}, u32[]{:S(2)}) collective-permute-start(f32[3,4,1792]{2,1,0:T(4,128)S(1)} %get-tuple-element.123), channel_id=1, source_target_pairs={{0,1},{1,0},{2,3},{3,2},{4,5},{5,4},{6,7},{7,6},{8,9},{9,8},{10,11... | collective-permute-start | bytes 258056 | tf_op jit(solution)/shard_map/ppermute | solution.py:46
  66.6 4.6 %all-to-all-done.1 = bf16[8,8,1792]{2,1,0:T(8,128)(2,1)S(1)} async-done(((bf16[8,8,1792]{2,1,0:T(8,128)(2,1)}), bf16[8,8,1792]{2,1,0:T(8,128)(2,1)S(1)}, u32[]{:S(2)}, u32[]{:S(2)}) %all-to-all-start.1) | async-done | bytes 229408 | tf_op jit(solution)/shard_map/all_to_all | solution.py:207
  71.1 2.8 %collective-permute-start.13 = (bf16[64,1792]{1,0:T(8,128)(2,1)S(1)}, bf16[64,1792]{1,0:T(8,128)(2,1)S(1)}, u32[]{:S(2)}, u32[]{:S(2)}) collective-permute-start(bf16[64,1792]{1,0:T(8,128)(2,1)S(1)} %bitcast.45), channel_id=1, source_target_pairs={{0,16},{1,65},{32,48},{33,97},{64,80},{65,1},{96,112},{97,33},{128... | collective-permute-start | bytes 688136 | tf_op jit(solution)/shard_map/ppermute | solution.py:34
  76.1 3.9 %collective-permute-done.13 = bf16[64,1792]{1,0:T(8,128)(2,1)S(1)} collective-permute-done((bf16[64,1792]{1,0:T(8,128)(2,1)S(1)}, bf16[64,1792]{1,0:T(8,128)(2,1)S(1)}, u32[]{:S(2)}, u32[]{:S(2)}) %collective-permute-start.13) | collective-permute-done | bytes 229408 | tf_op jit(solution)/shard_map/ppermute | solution.py:34
  80.0 2.4 %collective-permute-done.14 = bf16[64,1792]{1,0:T(8,128)(2,1)S(1)} collective-permute-done((bf16[64,1792]{1,0:T(8,128)(2,1)S(1)}, bf16[64,1792]{1,0:T(8,128)(2,1)S(1)}, u32[]{:S(2)}, u32[]{:S(2)}) %collective-permute-start.14) | collective-permute-done | bytes 229408 | tf_op jit(solution)/shard_map/ppermute | solution.py:34
  82.5 7.3 %collective-permute-start.19 = (bf16[128,1792]{1,0:T(8,128)(2,1)S(1)}, bf16[128,1792]{1,0:T(8,128)(2,1)S(1)}, u32[]{:S(2)}, u32[]{:S(2)}) collective-permute-start(bf16[128,1792]{1,0:T(8,128)(2,1)S(1)} %pad_maximum_fusion.refs_0_), channel_id=1, source_target_pairs={{0,1},{1,0},{2,3},{3,2},{4,5},{5,4},{6,7},{7,6},{8,9},{9,8},{10,11... | collective-permute-start | bytes 1376264 | tf_op jit(solution)/shard_map/ppermute | solution.py:46
  91.3 1.8 %collective-permute-start.16 = (bf16[128,1792]{1,0:T(8,128)(2,1)S(1)}, bf16[128,1792]{1,0:T(8,128)(2,1)S(1)}, u32[]{:S(2)}, u32[]{:S(2)}) collective-permute-start(bf16[128,1792]{1,0:T(8,128)(2,1)S(1)} %pad_maximum_fusion.refs_0_), channel_id=1, source_target_pairs={{0,96},{1,145},{32,64},{33,177},{64,32},{65,209},{96,0},{97,241},{... | collective-permute-start | bytes 1376264 | tf_op jit(solution)/shard_map/ppermute | solution.py:34
  93.1 4.5 %collective-permute-start.23 = (bf16[128,1792]{1,0:T(8,128)(2,1)S(1)}, bf16[128,1792]{1,0:T(8,128)(2,1)S(1)}, u32[]{:S(2)}, u32[]{:S(2)}) collective-permute-start(bf16[128,1792]{1,0:T(8,128)(2,1)S(1)} %pad_maximum_fusion.1.refs_1_), channel_id=1, source_target_pairs={{0,1},{1,0},{2,3},{3,2},{4,5},{5,4},{6,7},{7,6},{8,9},{9,8},{10,11... | collective-permute-start | bytes 1376264 | tf_op jit(solution)/shard_map/ppermute | solution.py:46
  99.5 2.0 %shard_map.112.refs_5_ = bf16[1024,3584]{1,0:T(8,128)(2,1)} custom-call(s32[3]{0:T(128)S(1)} %pad_add_fusion.here, bf16[128,1792]{1,0:T(8,128)(2,1)S(1)} %pad_maximum_fusion.refs_0_, bf16[128,1792]{1,0:T(8,128)(2,1)S(1)} %pad_maximum_fusion.1.refs_1_, bf16[128,1792]{1,0:T(8,128)(2,1)S(1)} %collective-permute-done.17.refs_2_, ...), custom_call_target="tpu_custom_call" | custom-call | bytes 4587520 | tf_op jit(solution)/shard_map/pallas_call | solution.py:114
  101.5 2.0 %collective-permute-done.16.refs_1_ = bf16[128,1792]{1,0:T(8,128)(2,1)S(1)} collective-permute-done((bf16[128,1792]{1,0:T(8,128)(2,1)S(1)}, bf16[128,1792]{1,0:T(8,128)(2,1)S(1)}, u32[]{:S(2)}, u32[]{:S(2)}) %collective-permute-start.16) | collective-permute-done | bytes 458784 | tf_op jit(solution)/shard_map/ppermute | solution.py:34
  103.5 4.9 %collective-permute-done.21.refs_2_ = bf16[128,1792]{1,0:T(8,128)(2,1)S(1)} collective-permute-done((bf16[128,1792]{1,0:T(8,128)(2,1)S(1)}, bf16[128,1792]{1,0:T(8,128)(2,1)S(1)}, u32[]{:S(2)}, u32[]{:S(2)}) %collective-permute-start.21) | collective-permute-done | bytes 458784 | tf_op jit(solution)/shard_map/ppermute | solution.py:34
  109.8 2.0 %shard_map.113.refs_4_ = bf16[1024,3584]{1,0:T(8,128)(2,1)} custom-call(s32[3]{0:T(128)S(1)} %pad_add_fusion.here, bf16[128,1792]{1,0:T(8,128)(2,1)S(1)} %collective-permute-done.15.refs_0_, bf16[128,1792]{1,0:T(8,128)(2,1)S(1)} %collective-permute-done.16.refs_1_, ...), custom_call_target="tpu_custom_call", output_to_operand_aliasing={{}: (6, {})} | custom-call | bytes 4587520 | tf_op jit(solution)/shard_map/pallas_call | solution.py:114
  113.2 1.8 %shard_map.114.refs_2_ = bf16[1024,3584]{1,0:T(8,128)(2,1)} custom-call(s32[3]{0:T(128)S(1)} %pad_add_fusion.here, bf16[128,1792]{1,0:T(8,128)(2,1)S(1)} %collective-permute-done.24.refs_0_, bf16[128,1792]{1,0:T(8,128)(2,1)S(1)} %collective-permute-done.25.refs_1_, ...), custom_call_target="tpu_custom_call", output_to_operand_aliasing={{}: (5, {})} | custom-call | bytes 3670016 | tf_op jit(solution)/shard_map/pallas_call | solution.py:114
  115.2 1.5 %shard_map.115 = bf16[1024,3584]{1,0:T(8,128)(2,1)} custom-call(s32[3]{0:T(128)S(1)} %pad_add_fusion.here, bf16[128,1792]{1,0:T(8,128)(2,1)S(1)} %collective-permute-done.28.refs_0_, bf16[128,1792]{1,0:T(8,128)(2,1)S(1)} %collective-permute-done.29.refs_1_, bf16[1024,3584]{1,0:T(8,128)(2,1)} %shard_map.114.refs_2_), custom_call_target="tpu_custom_call", output_to_operand_aliasing={{}: (3, {})} | custom-call | bytes 1835008 | tf_op jit(solution)/shard_map/pallas_call | solution.py:114
  (66 shorter events, 16.7 us)
Async XLA Ops:
  3.0 6.2 %collective-permute-start.1 = (bf16[128,1792]{1,0:T(8,128)(2,1)S(1)}, bf16[128,1792]{1,0:T(8,128)(2,1)S(1)}, u32[]{:S(2)}, u32[]{:S(2)}) collective-permute-start(bf16[128,1792]{1,0:T(8,128)(2,1)S(1)} %get-tuple-element.117), channel_id=1, source_target_pairs={{0,1},{1,0},{2,3},{3,2},{4,5},{5,4},{6,7},{7,6},{8,9},{9,8},{10,11... | collective-permute-start | bytes 1376264 | tf_op jit(solution)/shard_map/ppermute | solution.py:46
  7.5 1.6 %collective-permute-start = (bf16[128,1024]{1,0:T(8,128)(2,1)S(1)}, bf16[128,1024]{1,0:T(8,128)(2,1)S(1)}, u32[]{:S(2)}, u32[]{:S(2)}) collective-permute-start(bf16[128,1024]{1,0:T(8,128)(2,1)S(1)} %fusion.5.hidden), channel_id=1, source_target_pairs={{0,1},{1,0},{2,3},{3,2},{4,5},{5,4},{6,7},{7,6},{8,9},{9,8},{10,11... | collective-permute-start | bytes 786440 | tf_op jit(solution)/shard_map/ppermute | solution.py:46
  11.0 8.9 %collective-permute-start.4 = (bf16[128,1792]{1,0:T(8,128)(2,1)S(1)}, bf16[128,1792]{1,0:T(8,128)(2,1)S(1)}, u32[]{:S(2)}, u32[]{:S(2)}) collective-permute-start(bf16[128,1792]{1,0:T(8,128)(2,1)S(1)} %get-tuple-element.60), channel_id=1, source_target_pairs={{0,96},{1,145},{32,64},{33,177},{64,32},{65,209},{96,0},{97,241},{... | collective-permute-start | bytes 1376264 | tf_op jit(solution)/shard_map/ppermute | solution.py:34
  11.8 8.1 %collective-permute-start.5 = (bf16[128,1792]{1,0:T(8,128)(2,1)S(1)}, bf16[128,1792]{1,0:T(8,128)(2,1)S(1)}, u32[]{:S(2)}, u32[]{:S(2)}) collective-permute-start(bf16[128,1792]{1,0:T(8,128)(2,1)S(1)} %get-tuple-element.61), channel_id=1, source_target_pairs={{0,32},{1,129},{32,0},{33,161},{64,96},{65,193},{96,64},{97,225},{... | collective-permute-start | bytes 1376264 | tf_op jit(solution)/shard_map/ppermute | solution.py:34
  11.9 12.5 %collective-permute-start.2 = (bf16[128,1792]{1,0:T(8,128)(2,1)S(1)}, bf16[128,1792]{1,0:T(8,128)(2,1)S(1)}, u32[]{:S(2)}, u32[]{:S(2)}) collective-permute-start(bf16[128,1792]{1,0:T(8,128)(2,1)S(1)} %get-tuple-element.57), channel_id=1, source_target_pairs={{0,32},{1,129},{32,0},{33,161},{64,96},{65,193},{96,64},{97,225},{... | collective-permute-start | bytes 1376264 | tf_op jit(solution)/shard_map/ppermute | solution.py:34
  13.4 11.4 %collective-permute-start.3 = (bf16[128,1792]{1,0:T(8,128)(2,1)S(1)}, bf16[128,1792]{1,0:T(8,128)(2,1)S(1)}, u32[]{:S(2)}, u32[]{:S(2)}) collective-permute-start(bf16[128,1792]{1,0:T(8,128)(2,1)S(1)} %get-tuple-element.58), channel_id=1, source_target_pairs={{0,96},{1,145},{32,64},{33,177},{64,32},{65,209},{96,0},{97,241},{... | collective-permute-start | bytes 1376264 | tf_op jit(solution)/shard_map/ppermute | solution.py:34
  20.1 9.1 %collective-permute-start.6 = (bf16[128,1792]{1,0:T(8,128)(2,1)S(1)}, bf16[128,1792]{1,0:T(8,128)(2,1)S(1)}, u32[]{:S(2)}, u32[]{:S(2)}) collective-permute-start(bf16[128,1792]{1,0:T(8,128)(2,1)S(1)} %get-tuple-element.65), channel_id=1, source_target_pairs={{0,32},{1,129},{32,0},{33,161},{64,96},{65,193},{96,64},{97,225},{... | collective-permute-start | bytes 1376264 | tf_op jit(solution)/shard_map/ppermute | solution.py:34
  20.2 9.5 %collective-permute-start.7 = (bf16[128,1792]{1,0:T(8,128)(2,1)S(1)}, bf16[128,1792]{1,0:T(8,128)(2,1)S(1)}, u32[]{:S(2)}, u32[]{:S(2)}) collective-permute-start(bf16[128,1792]{1,0:T(8,128)(2,1)S(1)} %get-tuple-element.66), channel_id=1, source_target_pairs={{0,96},{1,145},{32,64},{33,177},{64,32},{65,209},{96,0},{97,241},{... | collective-permute-start | bytes 1376264 | tf_op jit(solution)/shard_map/ppermute | solution.py:34
  21.8 2.6 %collective-permute-start.8 = (f32[3,4,1792]{2,1,0:T(4,128)S(1)}, f32[3,4,1792]{2,1,0:T(4,128)S(1)}, u32[]{:S(2)}, u32[]{:S(2)}) collective-permute-start(f32[3,4,1792]{2,1,0:T(4,128)S(1)} %get-tuple-element.125), channel_id=1, source_target_pairs={{0,1},{1,0},{2,3},{3,2},{4,5},{5,4},{6,7},{7,6},{8,9},{9,8},{10,11... | collective-permute-start | bytes 258056 | tf_op jit(solution)/shard_map/ppermute | solution.py:46
  30.1 5.3 %collective-permute-start.10 = (bf16[64,1792]{1,0:T(8,128)(2,1)S(1)}, bf16[64,1792]{1,0:T(8,128)(2,1)S(1)}, u32[]{:S(2)}, u32[]{:S(2)}) collective-permute-start(bf16[64,1792]{1,0:T(8,128)(2,1)S(1)} %get-tuple-element.76), channel_id=1, source_target_pairs={{0,128},{1,33},{32,160},{33,1},{64,192},{65,97},{96,224},{97,65},{... | collective-permute-start | bytes 688136 | tf_op jit(solution)/shard_map/ppermute | solution.py:34
  31.0 7.3 %collective-permute-start.11 = (bf16[64,1792]{1,0:T(8,128)(2,1)S(1)}, bf16[64,1792]{1,0:T(8,128)(2,1)S(1)}, u32[]{:S(2)}, u32[]{:S(2)}) collective-permute-start(bf16[64,1792]{1,0:T(8,128)(2,1)S(1)} %get-tuple-element.77), channel_id=1, source_target_pairs={{0,144},{1,97},{32,176},{33,65},{64,208},{65,33},{96,240},{97,1},{... | collective-permute-start | bytes 688136 | tf_op jit(solution)/shard_map/ppermute | solution.py:34
  32.9 6.6 %collective-permute-start.9 = (bf16[64,1792]{1,0:T(8,128)(2,1)S(1)}, bf16[64,1792]{1,0:T(8,128)(2,1)S(1)}, u32[]{:S(2)}, u32[]{:S(2)}) collective-permute-start(bf16[64,1792]{1,0:T(8,128)(2,1)S(1)} %get-tuple-element.75), channel_id=1, source_target_pairs={{0,16},{1,65},{32,48},{33,97},{64,80},{65,1},{96,112},{97,33},{128... | collective-permute-start | bytes 688136 | tf_op jit(solution)/shard_map/ppermute | solution.py:34
  40.4 17.5 %all-to-all-start = ((bf16[8,8,1792]{2,1,0:T(8,128)(2,1)}), bf16[8,8,1792]{2,1,0:T(8,128)(2,1)S(1)}, u32[]{:S(2)}, u32[]{:S(2)}) async-start(bf16[8,8,1792]{2,1,0:T(8,128)(2,1)} %fusion.6), calls=%async_computation | async-start | bytes 458752 | tf_op jit(solution)/shard_map/all_to_all | solution.py:190
  58.7 12.4 %all-to-all-start.1 = ((bf16[8,8,1792]{2,1,0:T(8,128)(2,1)}), bf16[8,8,1792]{2,1,0:T(8,128)(2,1)S(1)}, u32[]{:S(2)}, u32[]{:S(2)}) async-start(bf16[8,8,1792]{2,1,0:T(8,128)(2,1)} %broadcast_in_dim.2), calls=%async_computation.1 | async-start | bytes 458752 | tf_op jit(solution)/shard_map/all_to_all | solution.py:207
  62.2 12.8 %collective-permute-start.20 = (f32[3,4,1792]{2,1,0:T(4,128)S(1)}, f32[3,4,1792]{2,1,0:T(4,128)S(1)}, u32[]{:S(2)}, u32[]{:S(2)}) collective-permute-start(f32[3,4,1792]{2,1,0:T(4,128)S(1)} %get-tuple-element.123), channel_id=1, source_target_pairs={{0,1},{1,0},{2,3},{3,2},{4,5},{5,4},{6,7},{7,6},{8,9},{9,8},{10,11... | collective-permute-start | bytes 258056 | tf_op jit(solution)/shard_map/ppermute | solution.py:46
  71.1 4.9 %collective-permute-start.12 = (bf16[64,1792]{1,0:T(8,128)(2,1)S(1)}, bf16[64,1792]{1,0:T(8,128)(2,1)S(1)}, u32[]{:S(2)}, u32[]{:S(2)}) collective-permute-start(bf16[64,1792]{1,0:T(8,128)(2,1)S(1)} %bitcast.44), channel_id=1, source_target_pairs={{0,128},{1,33},{32,160},{33,1},{64,192},{65,97},{96,224},{97,65},{... | collective-permute-start | bytes 688136 | tf_op jit(solution)/shard_map/ppermute | solution.py:34
  71.1 8.8 %collective-permute-start.13 = (bf16[64,1792]{1,0:T(8,128)(2,1)S(1)}, bf16[64,1792]{1,0:T(8,128)(2,1)S(1)}, u32[]{:S(2)}, u32[]{:S(2)}) collective-permute-start(bf16[64,1792]{1,0:T(8,128)(2,1)S(1)} %bitcast.45), channel_id=1, source_target_pairs={{0,16},{1,65},{32,48},{33,97},{64,80},{65,1},{96,112},{97,33},{128... | collective-permute-start | bytes 688136 | tf_op jit(solution)/shard_map/ppermute | solution.py:34
  74.0 8.3 %collective-permute-start.14 = (bf16[64,1792]{1,0:T(8,128)(2,1)S(1)}, bf16[64,1792]{1,0:T(8,128)(2,1)S(1)}, u32[]{:S(2)}, u32[]{:S(2)}) collective-permute-start(bf16[64,1792]{1,0:T(8,128)(2,1)S(1)} %bitcast.46), channel_id=1, source_target_pairs={{0,144},{1,97},{32,176},{33,65},{64,208},{65,33},{96,240},{97,1},{... | collective-permute-start | bytes 688136 | tf_op jit(solution)/shard_map/ppermute | solution.py:34
  82.4 10.7 %collective-permute-start.17 = (bf16[128,1792]{1,0:T(8,128)(2,1)S(1)}, bf16[128,1792]{1,0:T(8,128)(2,1)S(1)}, u32[]{:S(2)}, u32[]{:S(2)}) collective-permute-start(bf16[128,1792]{1,0:T(8,128)(2,1)S(1)} %pad_maximum_fusion.refs_0_), channel_id=1, source_target_pairs={{0,32},{1,129},{32,0},{33,161},{64,96},{65,193},{96,64},{97,225},{... | collective-permute-start | bytes 1376264 | tf_op jit(solution)/shard_map/ppermute | solution.py:34
  82.5 16.1 %collective-permute-start.19 = (bf16[128,1792]{1,0:T(8,128)(2,1)S(1)}, bf16[128,1792]{1,0:T(8,128)(2,1)S(1)}, u32[]{:S(2)}, u32[]{:S(2)}) collective-permute-start(bf16[128,1792]{1,0:T(8,128)(2,1)S(1)} %pad_maximum_fusion.refs_0_), channel_id=1, source_target_pairs={{0,1},{1,0},{2,3},{3,2},{4,5},{5,4},{6,7},{7,6},{8,9},{9,8},{10,11... | collective-permute-start | bytes 1376264 | tf_op jit(solution)/shard_map/ppermute | solution.py:46
  89.8 8.8 %collective-permute-start.18 = (bf16[128,1792]{1,0:T(8,128)(2,1)S(1)}, bf16[128,1792]{1,0:T(8,128)(2,1)S(1)}, u32[]{:S(2)}, u32[]{:S(2)}) collective-permute-start(bf16[128,1792]{1,0:T(8,128)(2,1)S(1)} %pad_maximum_fusion.1.refs_1_), channel_id=1, source_target_pairs={{0,96},{1,145},{32,64},{33,177},{64,32},{65,209},{96,0},{97,241},{... | collective-permute-start | bytes 1376264 | tf_op jit(solution)/shard_map/ppermute | solution.py:34
  91.3 10.2 %collective-permute-start.15 = (bf16[128,1792]{1,0:T(8,128)(2,1)S(1)}, bf16[128,1792]{1,0:T(8,128)(2,1)S(1)}, u32[]{:S(2)}, u32[]{:S(2)}) collective-permute-start(bf16[128,1792]{1,0:T(8,128)(2,1)S(1)} %pad_maximum_fusion.1.refs_1_), channel_id=1, source_target_pairs={{0,32},{1,129},{32,0},{33,161},{64,96},{65,193},{96,64},{97,225},{... | collective-permute-start | bytes 1376264 | tf_op jit(solution)/shard_map/ppermute | solution.py:34
  91.3 12.2 %collective-permute-start.16 = (bf16[128,1792]{1,0:T(8,128)(2,1)S(1)}, bf16[128,1792]{1,0:T(8,128)(2,1)S(1)}, u32[]{:S(2)}, u32[]{:S(2)}) collective-permute-start(bf16[128,1792]{1,0:T(8,128)(2,1)S(1)} %pad_maximum_fusion.refs_0_), channel_id=1, source_target_pairs={{0,96},{1,145},{32,64},{33,177},{64,32},{65,209},{96,0},{97,241},{... | collective-permute-start | bytes 1376264 | tf_op jit(solution)/shard_map/ppermute | solution.py:34
  93.1 10.4 %collective-permute-start.23 = (bf16[128,1792]{1,0:T(8,128)(2,1)S(1)}, bf16[128,1792]{1,0:T(8,128)(2,1)S(1)}, u32[]{:S(2)}, u32[]{:S(2)}) collective-permute-start(bf16[128,1792]{1,0:T(8,128)(2,1)S(1)} %pad_maximum_fusion.1.refs_1_), channel_id=1, source_target_pairs={{0,1},{1,0},{2,3},{3,2},{4,5},{5,4},{6,7},{7,6},{8,9},{9,8},{10,11... | collective-permute-start | bytes 1376264 | tf_op jit(solution)/shard_map/ppermute | solution.py:46
  98.6 9.8 %collective-permute-start.21 = (bf16[128,1792]{1,0:T(8,128)(2,1)S(1)}, bf16[128,1792]{1,0:T(8,128)(2,1)S(1)}, u32[]{:S(2)}, u32[]{:S(2)}) collective-permute-start(bf16[128,1792]{1,0:T(8,128)(2,1)S(1)} %collective-permute-done.17.refs_2_), channel_id=1, source_target_pairs={{0,96},{1,145},{32,64},{33,177},{64,32},{65,209},{96,0},{97,241},{... | collective-permute-start | bytes 1376264 | tf_op jit(solution)/shard_map/ppermute | solution.py:34
  99.5 9.0 %collective-permute-start.22 = (bf16[128,1792]{1,0:T(8,128)(2,1)S(1)}, bf16[128,1792]{1,0:T(8,128)(2,1)S(1)}, u32[]{:S(2)}, u32[]{:S(2)}) collective-permute-start(bf16[128,1792]{1,0:T(8,128)(2,1)S(1)} %collective-permute-done.18.refs_3_), channel_id=1, source_target_pairs={{0,32},{1,129},{32,0},{33,161},{64,96},{65,193},{96,64},{97,225},{... | collective-permute-start | bytes 1376264 | tf_op jit(solution)/shard_map/ppermute | solution.py:34
  108.4 3.4 %collective-permute-start.24 = (bf16[128,1792]{1,0:T(8,128)(2,1)S(1)}, bf16[128,1792]{1,0:T(8,128)(2,1)S(1)}, u32[]{:S(2)}, u32[]{:S(2)}) collective-permute-start(bf16[128,1792]{1,0:T(8,128)(2,1)S(1)} %collective-permute-done.17.refs_2_), channel_id=1, source_target_pairs={{0,1},{1,0},{2,3},{3,2},{4,5},{5,4},{6,7},{7,6},{8,9},{9,8},{10,11... | collective-permute-start | bytes 1376264 | tf_op jit(solution)/shard_map/ppermute | solution.py:46
  109.3 2.5 %collective-permute-start.25 = (bf16[128,1792]{1,0:T(8,128)(2,1)S(1)}, bf16[128,1792]{1,0:T(8,128)(2,1)S(1)}, u32[]{:S(2)}, u32[]{:S(2)}) collective-permute-start(bf16[128,1792]{1,0:T(8,128)(2,1)S(1)} %collective-permute-done.18.refs_3_), channel_id=1, source_target_pairs={{0,1},{1,0},{2,3},{3,2},{4,5},{5,4},{6,7},{7,6},{8,9},{9,8},{10,11... | collective-permute-start | bytes 1376264 | tf_op jit(solution)/shard_map/ppermute | solution.py:46
  109.3 2.8 %collective-permute-start.26 = (bf16[128,1792]{1,0:T(8,128)(2,1)S(1)}, bf16[128,1792]{1,0:T(8,128)(2,1)S(1)}, u32[]{:S(2)}, u32[]{:S(2)}) collective-permute-start(bf16[128,1792]{1,0:T(8,128)(2,1)S(1)} %collective-permute-done.15.refs_0_), channel_id=1, source_target_pairs={{0,1},{1,0},{2,3},{3,2},{4,5},{5,4},{6,7},{7,6},{8,9},{9,8},{10,11... | collective-permute-start | bytes 1376264 | tf_op jit(solution)/shard_map/ppermute | solution.py:46
  109.8 2.9 %collective-permute-start.27 = (bf16[128,1792]{1,0:T(8,128)(2,1)S(1)}, bf16[128,1792]{1,0:T(8,128)(2,1)S(1)}, u32[]{:S(2)}, u32[]{:S(2)}) collective-permute-start(bf16[128,1792]{1,0:T(8,128)(2,1)S(1)} %collective-permute-done.16.refs_1_), channel_id=1, source_target_pairs={{0,1},{1,0},{2,3},{3,2},{4,5},{5,4},{6,7},{7,6},{8,9},{9,8},{10,11... | collective-permute-start | bytes 1376264 | tf_op jit(solution)/shard_map/ppermute | solution.py:46
  112.7 2.4 %collective-permute-start.28 = (bf16[128,1792]{1,0:T(8,128)(2,1)S(1)}, bf16[128,1792]{1,0:T(8,128)(2,1)S(1)}, u32[]{:S(2)}, u32[]{:S(2)}) collective-permute-start(bf16[128,1792]{1,0:T(8,128)(2,1)S(1)} %collective-permute-done.21.refs_2_), channel_id=1, source_target_pairs={{0,1},{1,0},{2,3},{3,2},{4,5},{5,4},{6,7},{7,6},{8,9},{9,8},{10,11... | collective-permute-start | bytes 1376264 | tf_op jit(solution)/shard_map/ppermute | solution.py:46
  113.1 2.1 %collective-permute-start.29 = (bf16[128,1792]{1,0:T(8,128)(2,1)S(1)}, bf16[128,1792]{1,0:T(8,128)(2,1)S(1)}, u32[]{:S(2)}, u32[]{:S(2)}) collective-permute-start(bf16[128,1792]{1,0:T(8,128)(2,1)S(1)} %collective-permute-done.22.refs_3_), channel_id=1, source_target_pairs={{0,1},{1,0},{2,3},{3,2},{4,5},{5,4},{6,7},{7,6},{8,9},{9,8},{10,11... | collective-permute-start | bytes 1376264 | tf_op jit(solution)/shard_map/ppermute | solution.py:46
  (4 other events, 34.7 us)
